TPU v7x, 256 devices: a whole 4x4x8 slice. The times are simulated.
256 devices in a mesh: dp: 8 (over x_lo, y), ctx: 32 (over x_hi, z, core).
Axes of the slice: x: 4 (x_hi: 2, x_lo: 2; x = x_hi * 2 + x_lo), y: 4, z: 8, core: 2. Of those that a mesh axis runs over, the one named last changes fastest.
Arguments:
- q_raw: bfloat16 [8, 4096, 2048], P('dp', 'ctx'), may hold values from -220 to 220
- k_raw: bfloat16 [8, 4096, 2048], P('dp', 'ctx'), may hold values from -220 to 220
- values: bfloat16 [8, 4096, 2048], P('dp', 'ctx'), may hold values from -6 to 6
- d_out: bfloat16 [8, 4096, 2048], P('dp', 'ctx'), may hold values from -14 to 14
- q_gain: float32 [2048], replicated, may hold values from 0.5 to 6
- k_gain: float32 [2048], replicated, may hold values from 0.5 to 6
Outputs:
- grad_q_raw: bfloat16 [8, 4096, 2048], P('dp', 'ctx')
- grad_k_raw: bfloat16 [8, 4096, 2048], P('dp', 'ctx')
- grad_values: bfloat16 [8, 4096, 2048], P('dp', 'ctx')
- grad_q_gain: float32 [2048], replicated
- grad_k_gain: float32 [2048], replicated
All inputs are finite; a program needn't handle non-finite values.
Results may differ from a plain program's by a relative error of at most 0.013.
The roundings to bfloat16 on the way count: a program that leaves them out, or rounds other values in their place, can miss the bound.
Values may be sent and summed in bfloat16 or wider, within the bound.
No kernel may reach another device: no remote copies, remote signals or barrier semaphores. Data moves between devices by JAX's collectives and lax.ppermute only.
A program may use at most 64 MiB of HBM per device.

v0:
```python
import jax
import jax.numpy as jnp
from jax import lax
from jax.sharding import PartitionSpec as P

HEADS = 16
HD = 128
TILE = 64
S_DEV = 128
SEG1 = 1024
R1 = 4
R2 = 8


EPS = 1e-06


def for_sending(array):
    return jax.tree.map(lambda a: a.astype(jnp.bfloat16) if a.dtype == jnp.float32 else a, array)


def shifted(block, axis, distance):
    devices = range(lax.axis_size(axis))
    route = [(i - distance, i) for i in devices if i - distance in devices]
    return lax.ppermute(block, axis, route)


def product(pattern, first_arg, second_arg):
    return jnp.einsum(pattern, first_arg, second_arg, preferred_element_type=jnp.float32)


def normalize(raw_rows, gain_row):
    shaped = raw_rows.astype(jnp.float32).reshape(raw_rows.shape[:-1] + (HEADS, HD))
    inverse = lax.rsqrt(jnp.mean(shaped * shaped, axis=-1, keepdims=True) + EPS)
    normed = shaped * inverse
    scaled = (normed * gain_row.reshape(HEADS, HD)).astype(jnp.bfloat16)
    return (normed, inverse, scaled)


def norm_grad(upstream, normed, inverse, gain_row):
    weighted = upstream * gain_row.reshape(HEADS, HD)
    inner_dot = jnp.mean(weighted * normed, axis=-1, keepdims=True)
    result = inverse * (weighted - normed * inner_dot)
    return result.reshape(result.shape[:-2] + (HEADS * HD,)).astype(jnp.bfloat16)


def local_pick(source, dilation, first_res):
    batch_size = source.shape[0]
    trailing = source.shape[3:]
    shared = HEADS // dilation
    shaped = source.reshape((batch_size, 2, TILE, shared, dilation) + trailing)
    window_rows = lax.dynamic_slice_in_dim(shaped, first_res, 2, 4)
    diagonal = jnp.diagonal(window_rows, axis1=1, axis2=4)
    diagonal = jnp.moveaxis(diagonal, -1, 1)
    return jnp.moveaxis(diagonal, 3, 2)


def local_spread(compact, dilation, first_res, fill_value):
    batch_size = compact.shape[0]
    trailing = compact.shape[4:]
    shaped = jnp.moveaxis(compact, 2, 3)[:, :, :, :, None]
    residues = jnp.arange(dilation, dtype=jnp.int32)
    wanted = first_res + jnp.arange(2, dtype=jnp.int32)
    chosen = (residues[None, :] == wanted[:, None]).reshape(
        (1, 2, 1, 1, dilation) + (1,) * len(trailing)
    )
    placed = jnp.where(chosen, shaped, jnp.asarray(fill_value, compact.dtype))
    return placed.reshape((batch_size, 2 * TILE, HEADS) + trailing)


def reach_rows(payload, stride, slot_count):
    current = payload
    pieces = [payload]
    for offset in range(1, slot_count):
        current = shifted(for_sending(current), "ctx", stride).astype(current.dtype)
        pieces.append(current)
    by_hop = jnp.stack(pieces)
    return jnp.flip(by_hop, axis=0)


def return_terms(outgoing, stride):
    received = jnp.zeros(outgoing.shape[1:], jnp.float32)
    for offset in range(outgoing.shape[0]):
        arrived = shifted(outgoing[offset], "ctx", -stride * (offset + 1))
        received = received + arrived.astype(jnp.float32)
    return received


def merge_slots(buffer):
    moved = jnp.moveaxis(buffer, 0, 3)
    return moved.reshape(moved.shape[:3] + (moved.shape[3] * moved.shape[4], moved.shape[5]))


def split_slots(merged, slot_count):
    shaped = merged.reshape(merged.shape[:3] + (slot_count, TILE, merged.shape[4]))
    return jnp.moveaxis(shaped, 3, 0)


def per_device(q_raw, k_raw, values, d_out, q_gain, k_gain):
    batch_size, slab_rows, feature_width = q_raw.shape
    position = lax.axis_index("ctx")
    ctx_count = lax.axis_size("ctx")
    score_scale = HD ** (-0.5)
    normed_q, inverse_q, queries = normalize(q_raw, q_gain)
    normed_k, inverse_k, key_rows = normalize(k_raw, k_gain)
    value_rows = values.reshape(batch_size, slab_rows, HEADS, HD)
    grad_out = d_out.reshape(batch_size, slab_rows, HEADS, HD)
    row_index = jnp.arange(slab_rows, dtype=jnp.int32)
    causal = row_index[None, :] <= row_index[:, None]
    local_scores = jnp.where(
        causal, product("bihd,bjhd->bhij", queries, key_rows) * score_scale, -jnp.inf
    )
    tile_index = jnp.arange(TILE, dtype=jnp.int32)
    tile_lower = tile_index[None, None, :] <= tile_index[:, None, None]
    segment_slabs = SEG1 // S_DEV
    settings = (
        (R1, R1 // 2, segment_slabs // (R1 // 2), position % segment_slabs // (R1 // 2)),
        (R2, R2 // 2, ctx_count // (R2 // 2), position // (R2 // 2)),
    )
    levels = []
    for dilation, stride, slot_count, class_rank in settings:
        first_res = 2 * position % dilation
        q_pick = local_pick(queries, dilation, first_res)
        g_pick = local_pick(grad_out, dilation, first_res)
        payload = jnp.stack(
            [local_pick(key_rows, dilation, first_res), local_pick(value_rows, dilation, first_res)]
        )
        buffer_rows = reach_rows(payload, stride, slot_count)
        key_buffer = merge_slots(buffer_rows[:, 0])
        value_buffer = merge_slots(buffer_rows[:, 1])
        slot_ids = jnp.arange(slot_count, dtype=jnp.int32)
        live_slot = slot_count - 1 - slot_ids <= class_rank
        earlier = slot_ids < slot_count - 1
        allowed = live_slot[None, :, None] & (earlier[None, :, None] | tile_lower)
        allowed = allowed.reshape(TILE, slot_count * TILE)
        scores = jnp.where(
            allowed, product("buqid,buqkd->buqik", q_pick, key_buffer) * score_scale, -jnp.inf
        )
        levels.append(
            (
                dilation,
                first_res,
                stride,
                slot_count,
                q_pick,
                g_pick,
                key_buffer,
                value_buffer,
                scores,
            )
        )
    row_max = jnp.swapaxes(jnp.max(local_scores, axis=3), 1, 2)
    for (
        dilation,
        first_res,
        stride,
        slot_count,
        q_pick,
        g_pick,
        key_buffer,
        value_buffer,
        scores,
    ) in levels:
        row_max = jnp.maximum(
            row_max, local_spread(jnp.max(scores, axis=4), dilation, first_res, -jnp.inf)
        )
    row_total = jnp.swapaxes(
        jnp.sum(jnp.exp(local_scores - jnp.swapaxes(row_max, 1, 2)[..., None]), axis=3), 1, 2
    )
    for (
        dilation,
        first_res,
        stride,
        slot_count,
        q_pick,
        g_pick,
        key_buffer,
        value_buffer,
        scores,
    ) in levels:
        level_max = local_pick(row_max, dilation, first_res)
        level_sum = jnp.sum(jnp.exp(scores - level_max[..., None]), axis=4)
        row_total = row_total + local_spread(level_sum, dilation, first_res, 0.0)
    log_total = row_max + jnp.log(row_total)
    local_prob = jnp.exp(local_scores - jnp.swapaxes(log_total, 1, 2)[..., None])
    local_weight = local_prob.astype(jnp.bfloat16)
    attn_out = product("bhij,bjhd->bihd", local_weight, value_rows)
    level_probs = []
    for (
        dilation,
        first_res,
        stride,
        slot_count,
        q_pick,
        g_pick,
        key_buffer,
        value_buffer,
        scores,
    ) in levels:
        level_prob = jnp.exp(scores - local_pick(log_total, dilation, first_res)[..., None])
        level_weight = level_prob.astype(jnp.bfloat16)
        attn_out = attn_out + local_spread(
            product("buqik,buqkd->buqid", level_weight, value_buffer), dilation, first_res, 0.0
        )
        level_probs.append((level_prob, level_weight))
    row_dot = jnp.sum(grad_out.astype(jnp.float32) * attn_out, axis=3)
    local_dscore = (
        local_prob
        * (
            product("bihd,bjhd->bhij", grad_out, value_rows)
            - jnp.swapaxes(row_dot, 1, 2)[..., None]
        )
    ).astype(jnp.bfloat16)
    query_sum = product("bhij,bjhd->bihd", local_dscore, key_rows)
    key_grad = score_scale * product("bhij,bihd->bjhd", local_dscore, queries)
    value_grad = product("bhij,bihd->bjhd", local_weight, grad_out)
    for level_tuple, prob_pair in zip(levels, level_probs):
        (
            dilation,
            first_res,
            stride,
            slot_count,
            q_pick,
            g_pick,
            key_buffer,
            value_buffer,
            scores,
        ) = level_tuple
        level_prob, level_weight = prob_pair
        level_dot = local_pick(row_dot, dilation, first_res)
        level_dscore = (
            level_prob
            * (product("buqid,buqkd->buqik", g_pick, value_buffer) - level_dot[..., None])
        ).astype(jnp.bfloat16)
        query_sum = query_sum + local_spread(
            product("buqik,buqkd->buqid", level_dscore, key_buffer), dilation, first_res, 0.0
        )
        key_terms = split_slots(
            score_scale * product("buqik,buqid->buqkd", level_dscore, q_pick), slot_count
        )
        value_terms = split_slots(product("buqik,buqid->buqkd", level_weight, g_pick), slot_count)
        key_grad = key_grad + local_spread(key_terms[-1], dilation, first_res, 0.0)
        value_grad = value_grad + local_spread(value_terms[-1], dilation, first_res, 0.0)
        outgoing = jnp.flip(jnp.stack([key_terms[:-1], value_terms[:-1]], axis=1), axis=0).astype(
            jnp.bfloat16
        )
        incoming = return_terms(outgoing, stride)
        key_grad = key_grad + local_spread(incoming[0], dilation, first_res, 0.0)
        value_grad = value_grad + local_spread(incoming[1], dilation, first_res, 0.0)
    query_grad = score_scale * query_sum
    query_terms = jnp.sum(query_grad * normed_q, axis=(0, 1))
    key_terms_sum = jnp.sum(key_grad * normed_k, axis=(0, 1))
    query_gain_grad, key_gain_grad = lax.psum((query_terms, key_terms_sum), ("dp", "ctx"))
    return (
        norm_grad(query_grad, normed_q, inverse_q, q_gain),
        norm_grad(key_grad, normed_k, inverse_k, k_gain),
        value_grad.astype(jnp.bfloat16).reshape(batch_size, slab_rows, feature_width),
        query_gain_grad.reshape(HEADS * HD),
        key_gain_grad.reshape(HEADS * HD),
    )


def solution(mesh):
    return jax.shard_map(
        per_device,
        mesh=mesh,
        in_specs=(
            P("dp", "ctx", None),
            P("dp", "ctx", None),
            P("dp", "ctx", None),
            P("dp", "ctx", None),
            P(),
            P(),
        ),
        out_specs=(P("dp", "ctx", None), P("dp", "ctx", None), P("dp", "ctx", None), P(), P()),
        check_vma=False,
    )
```

profile of v0, /device:TPU:1, one launch (start us, length us, event | category | flops | bytes accessed | tf_op | source)
XLA Modules:
  0.0 350.3 jit_solution(8415920861310006207)
XLA Ops:
  2.1 1.9 copy.184
  4.2 1.9 copy.187
  8.2 1.9 constant_dynamic-slice_fusion.9
  11.5 1.7 constant_dynamic-slice_fusion.1
  15.9 6.4 %collective-permute-start.3 = (bf16[2,1,2,2,64,128]{5,4,3,2,1,0:T(8,128)(2,1)}, bf16[2,1,2,2,64,128]{5,4,3,2,1,0:T(8,128)(2,1)}, u32[]{:S(2)}, u32[]{:S(2)}) collective-permute-start(bf16[2,1,2,2,64,128]{5,4,3,2,1,0:T(8,128)(2,1)} %pad_maximum_fusion.4), channel_id=1, source_target_pairs={{0,4},{1,5},{2,6},{3,7},{4,8},{5,9},{6,10},{7,11},{8,12},{9,13},{1... | collective-permute-start | bytes 393224 | tf_op jit(solution)/shard_map/ppermute | solution.py:25
  29.0 2.1 constant_dynamic-slice_fusion.5
  34.0 4.4 %collective-permute-start = (bf16[2,1,2,4,64,128]{5,4,3,2,1,0:T(8,128)(2,1)}, bf16[2,1,2,4,64,128]{5,4,3,2,1,0:T(8,128)(2,1)}, u32[]{:S(2)}, u32[]{:S(2)}) collective-permute-start(bf16[2,1,2,4,64,128]{5,4,3,2,1,0:T(8,128)(2,1)} %get-tuple-element.45), channel_id=1, source_target_pairs={{0,2},{1,3},{2,4},{3,5},{4,6},{5,7},{6,8},{7,9},{8,10},{9,11},{10,... | collective-permute-start | bytes 786440 | tf_op jit(solution)/shard_map/ppermute | solution.py:25
  44.7 2.6 fusion.65
  50.7 2.2 copy.287
  59.8 4.0 %collective-permute-start.4 = (bf16[2,1,2,2,64,128]{5,4,3,2,1,0:T(8,128)(2,1)}, bf16[2,1,2,2,64,128]{5,4,3,2,1,0:T(8,128)(2,1)S(1)}, u32[]{:S(2)}, u32[]{:S(2)}) collective-permute-start(bf16[2,1,2,2,64,128]{5,4,3,2,1,0:T(8,128)(2,1)} %collective-permute-done.3), channel_id=1, source_target_pairs={{0,4},{1,5},{2,6},{3,7},{4,8},{5,9},{6,10},{7,11},{8,12},{9,13},{1... | collective-permute-start | bytes 393224 | tf_op jit(solution)/shard_map/ppermute | solution.py:25
  63.8 1.6 bitcast_dynamic-update-slice_fusion.6
  66.1 4.7 %collective-permute-start.5 = (bf16[2,1,2,2,64,128]{5,4,3,2,1,0:T(8,128)(2,1)S(1)}, bf16[2,1,2,2,64,128]{5,4,3,2,1,0:T(8,128)(2,1)S(1)}, u32[]{:S(2)}, u32[]{:S(2)}) collective-permute-start(bf16[2,1,2,2,64,128]{5,4,3,2,1,0:T(8,128)(2,1)S(1)} %collective-permute-done.4), channel_id=1, source_target_pairs={{0,4},{1,5},{2,6},{3,7},{4,8},{5,9},{6,10},{7,11},{8,12},{9,13},{1... | collective-permute-start | bytes 393224 | tf_op jit(solution)/shard_map/ppermute | solution.py:25
  70.7 6.5 %collective-permute-start.1 = (bf16[2,1,2,4,64,128]{5,4,3,2,1,0:T(8,128)(2,1)}, bf16[2,1,2,4,64,128]{5,4,3,2,1,0:T(8,128)(2,1)S(1)}, u32[]{:S(2)}, u32[]{:S(2)}) collective-permute-start(bf16[2,1,2,4,64,128]{5,4,3,2,1,0:T(8,128)(2,1)} %collective-permute-done), channel_id=1, source_target_pairs={{0,2},{1,3},{2,4},{3,5},{4,6},{5,7},{6,8},{7,9},{8,10},{9,11},{10,... | collective-permute-start | bytes 786440 | tf_op jit(solution)/shard_map/ppermute | solution.py:25
  77.9 1.9 collective-permute-start.6
  80.4 4.2 %collective-permute-done.6 = bf16[2,1,2,2,64,128]{5,4,3,2,1,0:T(8,128)(2,1)S(1)} collective-permute-done((bf16[2,1,2,2,64,128]{5,4,3,2,1,0:T(8,128)(2,1)S(1)}, bf16[2,1,2,2,64,128]{5,4,3,2,1,0:T(8,128)(2,1)S(1)}, u32[]{:S(2)}, u32[]{:S(2)}) %collective-permute-start.6) | collective-permute-done | bytes 131104 | tf_op jit(solution)/shard_map/ppermute | solution.py:25
  84.6 6.2 %collective-permute-start.7 = (bf16[2,1,2,2,64,128]{5,4,3,2,1,0:T(8,128)(2,1)S(1)}, bf16[2,1,2,2,64,128]{5,4,3,2,1,0:T(8,128)(2,1)}, u32[]{:S(2)}, u32[]{:S(2)}) collective-permute-start(bf16[2,1,2,2,64,128]{5,4,3,2,1,0:T(8,128)(2,1)S(1)} %collective-permute-done.6), channel_id=1, source_target_pairs={{0,4},{1,5},{2,6},{3,7},{4,8},{5,9},{6,10},{7,11},{8,12},{9,13},{1... | collective-permute-start | bytes 393224 | tf_op jit(solution)/shard_map/ppermute | solution.py:25
  90.8 7.6 %collective-permute-start.2 = (bf16[2,1,2,4,64,128]{5,4,3,2,1,0:T(8,128)(2,1)S(1)}, bf16[2,1,2,4,64,128]{5,4,3,2,1,0:T(8,128)(2,1)S(1)}, u32[]{:S(2)}, u32[]{:S(2)}) collective-permute-start(bf16[2,1,2,4,64,128]{5,4,3,2,1,0:T(8,128)(2,1)S(1)} %collective-permute-done.1), channel_id=1, source_target_pairs={{0,2},{1,3},{2,4},{3,5},{4,6},{5,7},{6,8},{7,9},{8,10},{9,11},{10,... | collective-permute-start | bytes 786440 | tf_op jit(solution)/shard_map/ppermute | solution.py:25
  99.1 5.6 %collective-permute-start.8 = (bf16[2,1,2,2,64,128]{5,4,3,2,1,0:T(8,128)(2,1)}, bf16[2,1,2,2,64,128]{5,4,3,2,1,0:T(8,128)(2,1)}, u32[]{:S(2)}, u32[]{:S(2)}) collective-permute-start(bf16[2,1,2,2,64,128]{5,4,3,2,1,0:T(8,128)(2,1)} %collective-permute-done.7), channel_id=1, source_target_pairs={{0,4},{1,5},{2,6},{3,7},{4,8},{5,9},{6,10},{7,11},{8,12},{9,13},{1... | collective-permute-start | bytes 393224 | tf_op jit(solution)/shard_map/ppermute | solution.py:25
  104.6 1.6 bitcast_dynamic-update-slice_fusion.2
  111.1 7.1 %collective-permute-start.9 = (bf16[2,1,2,2,64,128]{5,4,3,2,1,0:T(8,128)(2,1)}, bf16[2,1,2,2,64,128]{5,4,3,2,1,0:T(8,128)(2,1)S(1)}, u32[]{:S(2)}, u32[]{:S(2)}) collective-permute-start(bf16[2,1,2,2,64,128]{5,4,3,2,1,0:T(8,128)(2,1)} %collective-permute-done.8), channel_id=1, source_target_pairs={{0,4},{1,5},{2,6},{3,7},{4,8},{5,9},{6,10},{7,11},{8,12},{9,13},{1... | collective-permute-start | bytes 393224 | tf_op jit(solution)/shard_map/ppermute | solution.py:25
  153.4 2.6 fusion.47
  160.4 2.6 fusion.42
  169.0 3.5 %multiply_reduce_fusion.1 = (f32[16,128]{1,0:T(8,128)}, f32[128,16]{0,1:T(8,128)S(1)}, f32[1,128,16,128]{3,1,2,0:T(8,128)S(1)}) fusion(f32[1,128,16,128]{3,1,2,0:T(8,128)S(1)} %copy-done.4, f32[128,16]{0,1:T(8,128)S(1)} %copy-done.40, f32[16,128]{1,0:T(8,128)S(1)} %copy-done.62, f32[1,128,16,128]{3,1,2,0:T(8,128)S(1)} %bitcast.589, ...), kind=kOutput, calls=%fused_computation.61 | convolution fusion | flops 70774784 | bytes 5820416 | tf_op jit(solution)/shard_map/bhij,bjhd->bihd/dot_general | solution.py:29
  174.6 2.0 pad_maximum_fusion
  191.8 1.7 collective-permute-done.18
  194.9 5.3 %collective-permute-done.17 = bf16[2,1,2,2,64,128]{5,4,3,2,0,1:T(8,128)(2,1)} collective-permute-done((bf16[2,1,2,2,64,128]{5,4,3,2,0,1:T(8,128)(2,1)}, bf16[2,1,2,2,64,128]{5,4,3,2,0,1:T(8,128)(2,1)}, u32[]{:S(2)}, u32[]{:S(2)}) %collective-permute-start.17) | collective-permute-done | bytes 131104 | tf_op jit(solution)/shard_map/ppermute | solution.py:25
  201.5 7.3 %collective-permute-done.16 = bf16[2,1,2,2,64,128]{5,4,3,2,0,1:T(8,128)(2,1)} collective-permute-done((bf16[2,1,2,2,64,128]{5,4,3,2,0,1:T(8,128)(2,1)}, bf16[2,1,2,2,64,128]{5,4,3,2,0,1:T(8,128)(2,1)}, u32[]{:S(2)}, u32[]{:S(2)}) %collective-permute-start.16) | collective-permute-done | bytes 131104 | tf_op jit(solution)/shard_map/ppermute | solution.py:25
  213.6 7.3 %collective-permute-done.12 = bf16[2,1,2,4,64,128]{5,4,3,2,0,1:T(8,128)(2,1)S(1)} collective-permute-done((bf16[2,1,2,4,64,128]{5,4,3,2,0,1:T(8,128)(2,1)S(1)}, bf16[2,1,2,4,64,128]{5,4,3,2,0,1:T(8,128)(2,1)S(1)}, u32[]{:S(2)}, u32[]{:S(2)}) %collective-permute-start.12) | collective-permute-done | bytes 262176 | tf_op jit(solution)/shard_map/ppermute | solution.py:25
  220.9 4.5 %collective-permute-done.11 = bf16[2,1,2,4,64,128]{5,4,3,2,0,1:T(8,128)(2,1)S(1)} collective-permute-done((bf16[2,1,2,4,64,128]{5,4,3,2,0,1:T(8,128)(2,1)S(1)}, bf16[2,1,2,4,64,128]{5,4,3,2,0,1:T(8,128)(2,1)S(1)}, u32[]{:S(2)}, u32[]{:S(2)}) %collective-permute-start.11) | collective-permute-done | bytes 262176 | tf_op jit(solution)/shard_map/ppermute | solution.py:25
  225.4 3.5 %collective-permute-done.10 = bf16[2,1,2,4,64,128]{5,4,3,2,0,1:T(8,128)(2,1)S(1)} collective-permute-done((bf16[2,1,2,4,64,128]{5,4,3,2,0,1:T(8,128)(2,1)S(1)}, bf16[2,1,2,4,64,128]{5,4,3,2,0,1:T(8,128)(2,1)S(1)}, u32[]{:S(2)}, u32[]{:S(2)}) %collective-permute-start.10) | collective-permute-done | bytes 262176 | tf_op jit(solution)/shard_map/ppermute | solution.py:25
  232.2 3.6 %multiply_reduce_fusion = (f32[16,128]{1,0:T(8,128)}, f32[128,16]{0,1:T(8,128)S(1)}, f32[1,128,16,128]{3,1,2,0:T(8,128)S(1)}) fusion(f32[1,128,16,128]{3,1,2,0:T(8,128)S(1)} %copy-done.3, f32[128,16]{0,1:T(8,128)S(1)} %copy-done.43, f32[16,128]{1,0:T(8,128)S(1)} %bitcast.634, f32[1,128,16,128]{3,1,2,0:T(8,128)S(1)} %bitcast.587, ...), kind=kOutput, calls=%fused_computation.60 | convolution fusion | flops 71823360 | bytes 7917568 | tf_op jit(solution)/shard_map/bhij,bihd->bjhd/dot_general | solution.py:29
  241.4 108.9 %all-reduce = (f32[2048]{0:T(1024)}, f32[2048]{0:T(1024)}) all-reduce(f32[2048]{0:T(1024)S(1)} %bitcast.641, f32[2048]{0:T(1024)S(1)} %bitcast.642), channel_id=1, replica_groups=mesh['dp'=8,'ctx'=32] {'dp','ctx'}, use_global_device_ids=true, to_apply=%region_12.13 | all-reduce | flops 4096 | bytes 32768 | tf_op jit(solution)/shard_map/psum | solution.py:253
  (394 shorter events, 119.4 us)
Async XLA Ops:
  0.7 142.2 %copy-start.37 = (s32[2]{0:T(128)}, s32[2]{0:T(128)S(1)}, u32[]{:S(2)}) copy-start(s32[2]{0:T(128)S(1)} %or_bitcast_fusion) | copy-start | bytes 28
  6.3 38.4 %copy-start.39 = (f32[128,16]{0,1:T(8,128)}, f32[128,16]{0,1:T(8,128)S(1)}, u32[]{:S(2)}) copy-start(f32[128,16]{0,1:T(8,128)S(1)} %add_rsqrt_fusion.1) | copy-start | bytes 24580
  15.9 43.9 %collective-permute-start.3 = (bf16[2,1,2,2,64,128]{5,4,3,2,1,0:T(8,128)(2,1)}, bf16[2,1,2,2,64,128]{5,4,3,2,1,0:T(8,128)(2,1)}, u32[]{:S(2)}, u32[]{:S(2)}) collective-permute-start(bf16[2,1,2,2,64,128]{5,4,3,2,1,0:T(8,128)(2,1)} %pad_maximum_fusion.4), channel_id=1, source_target_pairs={{0,4},{1,5},{2,6},{3,7},{4,8},{5,9},{6,10},{7,11},{8,12},{9,13},{1... | collective-permute-start | bytes 393224 | tf_op jit(solution)/shard_map/ppermute | solution.py:25
  33.1 9.3 %copy-start.82 = (f32[2,2,128]{2,1,0:T(2,128)S(1)}, f32[2,2,128]{2,1,0:T(2,128)}, u32[]{:S(2)}) copy-start(f32[2,2,128]{2,1,0:T(2,128)} %get-tuple-element.61) | copy-start | bytes 6148
  34.0 10.7 %copy-start.42 = (f32[128,16]{0,1:T(8,128)S(1)}, f32[128,16]{0,1:T(8,128)}, u32[]{:S(2)}) copy-start(f32[128,16]{0,1:T(8,128)} %copy-done.41) | copy-start | bytes 24580
  34.0 10.7 %copy-start.51 = (f32[2048]{0:T(1024)S(1)}, f32[2048]{0:T(1024)}, u32[]{:S(2)}) copy-start(f32[2048]{0:T(1024)} %param.11) | copy-start | bytes 24580
  34.0 10.7 %copy-start.60 = (f32[2048]{0:T(1024)S(1)}, f32[2048]{0:T(1024)}, u32[]{:S(2)}) copy-start(f32[2048]{0:T(1024)} %param.10) | copy-start | bytes 24580
  34.0 36.7 %collective-permute-start = (bf16[2,1,2,4,64,128]{5,4,3,2,1,0:T(8,128)(2,1)}, bf16[2,1,2,4,64,128]{5,4,3,2,1,0:T(8,128)(2,1)}, u32[]{:S(2)}, u32[]{:S(2)}) collective-permute-start(bf16[2,1,2,4,64,128]{5,4,3,2,1,0:T(8,128)(2,1)} %get-tuple-element.45), channel_id=1, source_target_pairs={{0,2},{1,3},{2,4},{3,5},{4,6},{5,7},{6,8},{7,9},{8,10},{9,11},{10,... | collective-permute-start | bytes 786440 | tf_op jit(solution)/shard_map/ppermute | solution.py:25
  47.4 10.0 %copy-start.83 = (pred[2,4]{0,1:T(4,128)(4,1)}, pred[2,4]{0,1:T(4,128)(4,1)S(1)}, u32[]{:S(2)}) copy-start(pred[2,4]{0,1:T(4,128)(4,1)S(1)} %iota_compare_fusion.3) | copy-start | bytes 28
  59.8 46.4 %copy-start.28 = (bf16[1,2,1,2,4,64,128]{6,5,4,3,1,2,0:T(8,128)(2,1)S(1)}, bf16[1,2,1,2,4,64,128]{6,5,4,3,1,2,0:T(8,128)(2,1)}, u32[]{:S(2)}) copy-start(bf16[1,2,1,2,4,64,128]{6,5,4,3,1,2,0:T(8,128)(2,1)} %get-tuple-element.44) | copy-start | bytes 786436
  59.8 6.3 %collective-permute-start.4 = (bf16[2,1,2,2,64,128]{5,4,3,2,1,0:T(8,128)(2,1)}, bf16[2,1,2,2,64,128]{5,4,3,2,1,0:T(8,128)(2,1)S(1)}, u32[]{:S(2)}, u32[]{:S(2)}) collective-permute-start(bf16[2,1,2,2,64,128]{5,4,3,2,1,0:T(8,128)(2,1)} %collective-permute-done.3), channel_id=1, source_target_pairs={{0,4},{1,5},{2,6},{3,7},{4,8},{5,9},{6,10},{7,11},{8,12},{9,13},{1... | collective-permute-start | bytes 393224 | tf_op jit(solution)/shard_map/ppermute | solution.py:25
  66.1 11.8 %collective-permute-start.5 = (bf16[2,1,2,2,64,128]{5,4,3,2,1,0:T(8,128)(2,1)S(1)}, bf16[2,1,2,2,64,128]{5,4,3,2,1,0:T(8,128)(2,1)S(1)}, u32[]{:S(2)}, u32[]{:S(2)}) collective-permute-start(bf16[2,1,2,2,64,128]{5,4,3,2,1,0:T(8,128)(2,1)S(1)} %collective-permute-done.4), channel_id=1, source_target_pairs={{0,4},{1,5},{2,6},{3,7},{4,8},{5,9},{6,10},{7,11},{8,12},{9,13},{1... | collective-permute-start | bytes 393224 | tf_op jit(solution)/shard_map/ppermute | solution.py:25
  70.7 20.1 %collective-permute-start.1 = (bf16[2,1,2,4,64,128]{5,4,3,2,1,0:T(8,128)(2,1)}, bf16[2,1,2,4,64,128]{5,4,3,2,1,0:T(8,128)(2,1)S(1)}, u32[]{:S(2)}, u32[]{:S(2)}) collective-permute-start(bf16[2,1,2,4,64,128]{5,4,3,2,1,0:T(8,128)(2,1)} %collective-permute-done), channel_id=1, source_target_pairs={{0,2},{1,3},{2,4},{3,5},{4,6},{5,7},{6,8},{7,9},{8,10},{9,11},{10,... | collective-permute-start | bytes 786440 | tf_op jit(solution)/shard_map/ppermute | solution.py:25
  77.9 6.7 %collective-permute-start.6 = (bf16[2,1,2,2,64,128]{5,4,3,2,1,0:T(8,128)(2,1)S(1)}, bf16[2,1,2,2,64,128]{5,4,3,2,1,0:T(8,128)(2,1)S(1)}, u32[]{:S(2)}, u32[]{:S(2)}) collective-permute-start(bf16[2,1,2,2,64,128]{5,4,3,2,1,0:T(8,128)(2,1)S(1)} %collective-permute-done.5), channel_id=1, source_target_pairs={{0,4},{1,5},{2,6},{3,7},{4,8},{5,9},{6,10},{7,11},{8,12},{9,13},{1... | collective-permute-start | bytes 393224 | tf_op jit(solution)/shard_map/ppermute | solution.py:25
  84.6 14.5 %collective-permute-start.7 = (bf16[2,1,2,2,64,128]{5,4,3,2,1,0:T(8,128)(2,1)S(1)}, bf16[2,1,2,2,64,128]{5,4,3,2,1,0:T(8,128)(2,1)}, u32[]{:S(2)}, u32[]{:S(2)}) collective-permute-start(bf16[2,1,2,2,64,128]{5,4,3,2,1,0:T(8,128)(2,1)S(1)} %collective-permute-done.6), channel_id=1, source_target_pairs={{0,4},{1,5},{2,6},{3,7},{4,8},{5,9},{6,10},{7,11},{8,12},{9,13},{1... | collective-permute-start | bytes 393224 | tf_op jit(solution)/shard_map/ppermute | solution.py:25
  90.8 15.4 %collective-permute-start.2 = (bf16[2,1,2,4,64,128]{5,4,3,2,1,0:T(8,128)(2,1)S(1)}, bf16[2,1,2,4,64,128]{5,4,3,2,1,0:T(8,128)(2,1)S(1)}, u32[]{:S(2)}, u32[]{:S(2)}) collective-permute-start(bf16[2,1,2,4,64,128]{5,4,3,2,1,0:T(8,128)(2,1)S(1)} %collective-permute-done.1), channel_id=1, source_target_pairs={{0,2},{1,3},{2,4},{3,5},{4,6},{5,7},{6,8},{7,9},{8,10},{9,11},{10,... | collective-permute-start | bytes 786440 | tf_op jit(solution)/shard_map/ppermute | solution.py:25
  99.1 12.0 %collective-permute-start.8 = (bf16[2,1,2,2,64,128]{5,4,3,2,1,0:T(8,128)(2,1)}, bf16[2,1,2,2,64,128]{5,4,3,2,1,0:T(8,128)(2,1)}, u32[]{:S(2)}, u32[]{:S(2)}) collective-permute-start(bf16[2,1,2,2,64,128]{5,4,3,2,1,0:T(8,128)(2,1)} %collective-permute-done.7), channel_id=1, source_target_pairs={{0,4},{1,5},{2,6},{3,7},{4,8},{5,9},{6,10},{7,11},{8,12},{9,13},{1... | collective-permute-start | bytes 393224 | tf_op jit(solution)/shard_map/ppermute | solution.py:25
  110.2 8.0 %copy-start.23 = (bf16[8,2,1,2,2,64,128]{6,5,4,3,1,2,0:T(8,128)(2,1)S(1)}, bf16[8,2,1,2,2,64,128]{6,5,4,3,1,2,0:T(8,128)(2,1)}, u32[]{:S(2)}) copy-start(bf16[8,2,1,2,2,64,128]{6,5,4,3,1,2,0:T(8,128)(2,1)} %bitcast_dynamic-update-slice_fusion.2) | copy-start | bytes 3145732
  111.1 9.1 %collective-permute-start.9 = (bf16[2,1,2,2,64,128]{5,4,3,2,1,0:T(8,128)(2,1)}, bf16[2,1,2,2,64,128]{5,4,3,2,1,0:T(8,128)(2,1)S(1)}, u32[]{:S(2)}, u32[]{:S(2)}) collective-permute-start(bf16[2,1,2,2,64,128]{5,4,3,2,1,0:T(8,128)(2,1)} %collective-permute-done.8), channel_id=1, source_target_pairs={{0,4},{1,5},{2,6},{3,7},{4,8},{5,9},{6,10},{7,11},{8,12},{9,13},{1... | collective-permute-start | bytes 393224 | tf_op jit(solution)/shard_map/ppermute | solution.py:25
  123.1 14.7 %copy-start = (f32[16,128,128]{1,2,0:T(8,128)S(1)}, f32[16,128,128]{1,2,0:T(8,128)}, u32[]{:S(2)}) copy-start(f32[16,128,128]{1,2,0:T(8,128)} %get-tuple-element.51) | copy-start | bytes 3145732
  177.9 7.4 %copy-start.35 = (f32[2,64,2,128]{3,1,2,0:T(8,128)S(1)}, f32[2,64,2,128]{3,1,2,0:T(8,128)}, u32[]{:S(2)}) copy-start(f32[2,64,2,128]{3,1,2,0:T(8,128)} %slice_bitcast_fusion.21) | copy-start | bytes 393220
  178.8 11.7 %collective-permute-start.19 = (bf16[2,1,2,2,64,128]{5,4,3,2,0,1:T(8,128)(2,1)}, bf16[2,1,2,2,64,128]{5,4,3,2,0,1:T(8,128)(2,1)}, u32[]{:S(2)}, u32[]{:S(2)}) collective-permute-start(bf16[2,1,2,2,64,128]{5,4,3,2,0,1:T(8,128)(2,1)} %get-tuple-element.35), channel_id=1, source_target_pairs={{28,0},{29,1},{30,2},{31,3},{60,32},{61,33},{62,34},{63,35},{92,64... | collective-permute-start | bytes 393224 | tf_op jit(solution)/shard_map/ppermute | solution.py:25
  180.1 13.4 %collective-permute-start.18 = (bf16[2,1,2,2,64,128]{5,4,3,2,0,1:T(8,128)(2,1)}, bf16[2,1,2,2,64,128]{5,4,3,2,0,1:T(8,128)(2,1)}, u32[]{:S(2)}, u32[]{:S(2)}) collective-permute-start(bf16[2,1,2,2,64,128]{5,4,3,2,0,1:T(8,128)(2,1)} %get-tuple-element.36), channel_id=1, source_target_pairs={{24,0},{25,1},{26,2},{27,3},{28,4},{29,5},{30,6},{31,7},{56,32},{5... | collective-permute-start | bytes 393224 | tf_op jit(solution)/shard_map/ppermute | solution.py:25
  181.4 18.8 %collective-permute-start.17 = (bf16[2,1,2,2,64,128]{5,4,3,2,0,1:T(8,128)(2,1)}, bf16[2,1,2,2,64,128]{5,4,3,2,0,1:T(8,128)(2,1)}, u32[]{:S(2)}, u32[]{:S(2)}) collective-permute-start(bf16[2,1,2,2,64,128]{5,4,3,2,0,1:T(8,128)(2,1)} %get-tuple-element.31), channel_id=1, source_target_pairs={{20,0},{21,1},{22,2},{23,3},{24,4},{25,5},{26,6},{27,7},{28,8},{29... | collective-permute-start | bytes 393224 | tf_op jit(solution)/shard_map/ppermute | solution.py:25
  182.7 26.0 %collective-permute-start.16 = (bf16[2,1,2,2,64,128]{5,4,3,2,0,1:T(8,128)(2,1)}, bf16[2,1,2,2,64,128]{5,4,3,2,0,1:T(8,128)(2,1)}, u32[]{:S(2)}, u32[]{:S(2)}) collective-permute-start(bf16[2,1,2,2,64,128]{5,4,3,2,0,1:T(8,128)(2,1)} %get-tuple-element.32), channel_id=1, source_target_pairs={{16,0},{17,1},{18,2},{19,3},{20,4},{21,5},{22,6},{23,7},{24,8},{25... | collective-permute-start | bytes 393224 | tf_op jit(solution)/shard_map/ppermute | solution.py:25
  184.0 26.3 %collective-permute-start.15 = (bf16[2,1,2,2,64,128]{5,4,3,2,0,1:T(8,128)(2,1)}, bf16[2,1,2,2,64,128]{5,4,3,2,0,1:T(8,128)(2,1)}, u32[]{:S(2)}, u32[]{:S(2)}) collective-permute-start(bf16[2,1,2,2,64,128]{5,4,3,2,0,1:T(8,128)(2,1)} %get-tuple-element.33), channel_id=1, source_target_pairs={{12,0},{13,1},{14,2},{15,3},{16,4},{17,5},{18,6},{19,7},{20,8},{21... | collective-permute-start | bytes 393224 | tf_op jit(solution)/shard_map/ppermute | solution.py:25
  189.4 4.1 %copy-start.56 = (bf16[2,1,2,2,64,128]{5,4,3,2,0,1:T(8,128)(2,1)S(1)}, bf16[2,1,2,2,64,128]{5,4,3,2,0,1:T(8,128)(2,1)}, u32[]{:S(2)}) copy-start(bf16[2,1,2,2,64,128]{5,4,3,2,0,1:T(8,128)(2,1)} %get-tuple-element.30) | copy-start | bytes 393220
  190.5 21.0 %collective-permute-start.14 = (bf16[2,1,2,2,64,128]{5,4,3,2,0,1:T(8,128)(2,1)S(1)}, bf16[2,1,2,2,64,128]{5,4,3,2,0,1:T(8,128)(2,1)S(1)}, u32[]{:S(2)}, u32[]{:S(2)}) collective-permute-start(bf16[2,1,2,2,64,128]{5,4,3,2,0,1:T(8,128)(2,1)S(1)} %copy-done.57), channel_id=1, source_target_pairs={{8,0},{9,1},{10,2},{11,3},{12,4},{13,5},{14,6},{15,7},{16,8},{17,9... | collective-permute-start | bytes 393224 | tf_op jit(solution)/shard_map/ppermute | solution.py:25
  193.5 18.0 %collective-permute-start.13 = (bf16[2,1,2,2,64,128]{5,4,3,2,0,1:T(8,128)(2,1)S(1)}, bf16[2,1,2,2,64,128]{5,4,3,2,0,1:T(8,128)(2,1)S(1)}, u32[]{:S(2)}, u32[]{:S(2)}) collective-permute-start(bf16[2,1,2,2,64,128]{5,4,3,2,0,1:T(8,128)(2,1)S(1)} %copy-done.56), channel_id=1, source_target_pairs={{4,0},{5,1},{6,2},{7,3},{8,4},{9,5},{10,6},{11,7},{12,8},{13,9},{1... | collective-permute-start | bytes 393224 | tf_op jit(solution)/shard_map/ppermute | solution.py:25
  200.2 20.7 %collective-permute-start.12 = (bf16[2,1,2,4,64,128]{5,4,3,2,0,1:T(8,128)(2,1)S(1)}, bf16[2,1,2,4,64,128]{5,4,3,2,0,1:T(8,128)(2,1)S(1)}, u32[]{:S(2)}, u32[]{:S(2)}) collective-permute-start(bf16[2,1,2,4,64,128]{5,4,3,2,0,1:T(8,128)(2,1)S(1)} %get-tuple-element.38), channel_id=1, source_target_pairs={{6,0},{7,1},{8,2},{9,3},{10,4},{11,5},{12,6},{13,7},{14,8},{15,9},... | collective-permute-start | bytes 786440 | tf_op jit(solution)/shard_map/ppermute | solution.py:25
  208.7 16.7 %collective-permute-start.11 = (bf16[2,1,2,4,64,128]{5,4,3,2,0,1:T(8,128)(2,1)S(1)}, bf16[2,1,2,4,64,128]{5,4,3,2,0,1:T(8,128)(2,1)S(1)}, u32[]{:S(2)}, u32[]{:S(2)}) collective-permute-start(bf16[2,1,2,4,64,128]{5,4,3,2,0,1:T(8,128)(2,1)S(1)} %get-tuple-element.39), channel_id=1, source_target_pairs={{4,0},{5,1},{6,2},{7,3},{8,4},{9,5},{10,6},{11,7},{12,8},{13,9},{1... | collective-permute-start | bytes 786440 | tf_op jit(solution)/shard_map/ppermute | solution.py:25
  210.3 18.6 %collective-permute-start.10 = (bf16[2,1,2,4,64,128]{5,4,3,2,0,1:T(8,128)(2,1)S(1)}, bf16[2,1,2,4,64,128]{5,4,3,2,0,1:T(8,128)(2,1)S(1)}, u32[]{:S(2)}, u32[]{:S(2)}) collective-permute-start(bf16[2,1,2,4,64,128]{5,4,3,2,0,1:T(8,128)(2,1)S(1)} %get-tuple-element.37), channel_id=1, source_target_pairs={{2,0},{3,1},{4,2},{5,3},{6,4},{7,5},{8,6},{9,7},{10,8},{11,9},{12,... | collective-permute-start | bytes 786440 | tf_op jit(solution)/shard_map/ppermute | solution.py:25
  (74 other events, 112.3 us)
where the time goes:
time: 353 us; the launch traced here: 350 us
  blocking collectives  109 us (31%)
  local copies, waits for them, and re-layouts  88.4 us (25%)
  starting transfers between devices  67.1 us (19%)
  waiting for transfers between devices  35.8 us (10%)
  matrix products  25.4 us (7%)
  other arithmetic  22.6 us (6%)
    psum x1, blocking collectives, per_device(): lax.psum((query_terms, key_terms_sum), ('dp', 'ctx'))  109 us
    ppermute x20, starting transfers between devices, shifted(): return lax.ppermute(block, axis, route)  67.1 us
    ppermute x20, waiting for transfers between devices, shifted(): return lax.ppermute(block, axis, route)  35.8 us
    dot_general x18, matrix products, product(): jnp.einsum(pattern, first_arg, second_arg, preferred_element_type=jnp.flo...  25.4 us
    unnamed x195, local copies, waits for them, and re-layouts  21.9 us
    dynamic_slice x14, local copies, waits for them, and re-layouts, local_pick(): window_rows = lax.dynamic_slice_in_dim(shaped, first_res, 2, 4)  12.3 us
    broadcast_in_dim x38, local copies, waits for them, and re-layouts, local_spread(): placed = jnp.where(chosen, shaped, jnp.asarray(fill_value, compact.dtype))  8.82 us
    gather x14, local copies, waits for them, and re-layouts, local_pick(): diagonal = jnp.diagonal(window_rows, axis1=1, axis2=4)  8.24 us
  transfers between devices with their start and end apart: 20, of which 10 were waited for; matrix products, arithmetic and copies ran while one was open for 14% of the time, Pallas kernels for 0%

commit v1 on v0

v1 whole, which is shorter than its diff:
```python
import jax
import jax.numpy as jnp
from jax import lax
from jax.experimental import pallas as pl
from jax.experimental.pallas import tpu as pltpu
from jax.sharding import PartitionSpec as P

HEADS = 16
HD = 128
TILE = 64
ROWS = 128
EPS = 1e-06
SCALE = HD ** (-0.5)
BF = jnp.bfloat16
F32 = jnp.float32
NEG = -jnp.inf


def vmem_spec():
    return pl.BlockSpec(memory_space=pltpu.VMEM)


def smem_spec():
    return pl.BlockSpec(memory_space=pltpu.SMEM)


def any_spec():
    return pl.BlockSpec(memory_space=pl.ANY)


def place(c):
    core = c & 1
    zl = (c >> 1) & 3
    zh = (c >> 3) & 1
    xh = (c >> 4) & 1
    return core, zl, zh, xh


def owned_heads(c, k):
    core, zl, zh, xh = place(c)
    rank = (zl ^ (2 * zh)) ^ k
    par = rank & 1
    base = 2 * core + 8 * (rank >> 1)
    return base + 4 * par, base + 1 + 4 * (1 - par)


def normalize(raw, gain):
    x = raw.astype(F32)
    inverse = lax.rsqrt(jnp.mean(x * x, axis=-1, keepdims=True) + EPS)
    normed = x * inverse
    return normed, inverse, (normed * gain).astype(BF)


def norm_grad(upstream, normed, inverse, gain):
    weighted = upstream * gain
    inner = jnp.mean(weighted * normed, axis=-1, keepdims=True)
    return (inverse * (weighted - normed * inner)).astype(BF)


def dot_nt(a, b):
    return lax.dot_general(a, b, (((1,), (1,)), ((), ())), preferred_element_type=F32)


def dot_nn(a, b):
    return lax.dot_general(a, b, (((1,), (0,)), ((), ())), preferred_element_type=F32)


def dot_tn(a, b):
    return lax.dot_general(a, b, (((0,), (0,)), ((), ())), preferred_element_type=F32)


def pack_kernel(c_ref, q, k, v, g, m0, m1, m2, m3, sems):
    c = c_ref[0]
    copies = []
    for step, out in enumerate((m0, m1, m2, m3)):
        h0, h1 = owned_heads(c, step)
        tiles = (
            (q, 0, h0), (g, 0, h0), (k, 0, h0), (v, 0, h0),
            (q, 1, h1), (g, 1, h1), (k, 1, h1), (v, 1, h1),
            (k, 0, h1), (v, 0, h1),
        )
        for t, (src, e, h) in enumerate(tiles):
            copy = pltpu.make_async_copy(
                src.at[pl.ds(e * TILE, TILE), pl.ds(pl.multiple_of(h * HD, HD), HD)],
                out.at[pl.ds(t * TILE, TILE), :],
                sems.at[step, t],
            )
            copy.start()
            copies.append(copy)
    for copy in copies:
        copy.wait()


def forward_pack_kernel(r0, r1, r2, r3, out, sems):
    copies = []
    for k, (src, at) in enumerate(((r0, 2), (r2, 2), (r1, 6), (r3, 6))):
        copy = pltpu.make_async_copy(
            src.at[pl.ds(at * TILE, 2 * TILE), :], out.at[pl.ds(2 * k * TILE, 2 * TILE), :], sems.at[k]
        )
        copy.start()
        copies.append(copy)
    for copy in copies:
        copy.wait()


def home_kernel(
    c_ref, q, k, v, g, q_gain, k_gain, gq_out, gk_out, gv_out, part_k, part_v, gains, dk_all, dv_all
):
    c = c_ref[0]
    core = c & 1
    row = lax.broadcasted_iota(jnp.int32, (ROWS, ROWS), 0)
    col = lax.broadcasted_iota(jnp.int32, (ROWS, ROWS), 1)
    causal = col <= row
    tile_of_row = lax.broadcasted_iota(jnp.int32, (ROWS, 1), 0) // TILE
    for h in range(HEADS):
        cols = slice(h * HD, (h + 1) * HD)
        kind = h % 4
        owned = (tile_of_row == (kind & 1)) & (core == (kind >> 1))
        keep = jnp.where(owned, 0.0, 1.0)
        qg = q_gain[h : h + 1, :]
        kg = k_gain[h : h + 1, :]
        qn, q_inv, qb = normalize(q[:, cols], qg)
        kn, k_inv, kb = normalize(k[:, cols], kg)
        vb = v[:, cols]
        gb = g[:, cols]
        s = jnp.where(causal, dot_nt(qb, kb) * SCALE, NEG)
        top = jnp.max(s, axis=1, keepdims=True)
        total = jnp.sum(jnp.exp(s - top), axis=1, keepdims=True)
        p = jnp.exp(s - (top + jnp.log(total))) * keep
        w = p.astype(BF)
        dp = dot_nt(gb, vb)
        row_dot = jnp.sum(w.astype(F32) * dp, axis=1, keepdims=True)
        ds = (p * (dp - row_dot)).astype(BF)
        dq = dot_nn(ds, kb) * SCALE
        dk = dot_tn(ds, qb) * SCALE
        dv = dot_tn(w, gb)
        gq_out[:, cols] = norm_grad(dq, qn, q_inv, qg)
        gk_out[:, cols] = norm_grad(dk, kn, k_inv, kg)
        gv_out[:, cols] = dv.astype(BF)
        dk_all[h] = dk
        dv_all[h] = dv
        gains[h : h + 1, :] = jnp.sum(dq * qn, axis=0, keepdims=True)
        gains[HEADS + h : HEADS + h + 1, :] = jnp.sum(dk * kn, axis=0, keepdims=True)
    for step in range(4):
        h0, h1 = owned_heads(c, step)
        for i, (h, e) in enumerate(((h0, 0), (h1, 1), (h1, 0))):
            rows = slice(e * TILE, (e + 1) * TILE)
            part_k[3 * step + i] = dk_all[h, rows, :]
            part_v[3 * step + i] = dv_all[h, rows, :]


def owner_kernel(
    c_ref, r0, r1, r2, r3, b1, b2, b3, q_gain, k_gain, home_gains,
    x0, x1, x2, x3, t1, t2, t3, far_k, far_v, gains,
):
    c = c_ref[0]
    core, zl, zh, xh = place(c)
    heads = owned_heads(c, 0)
    received = (r0, r1, r2, r3)
    crossed = (b1, b2, b3)
    returned = (x0, x1, x2, x3)
    terms = (t1, t2, t3)
    live = (zh == 1, xh == 1, xh == 1)
    gains[...] = home_gains[...]
    row = lax.broadcasted_iota(jnp.int32, (TILE, TILE), 0)
    col = lax.broadcasted_iota(jnp.int32, (TILE, TILE), 1)
    lower = col <= row

    def rows_of(ref, tile, count=1):
        return ref[tile * TILE : (tile + count) * TILE, :]

    for e in range(2):
        base = 4 * e
        far = (e, e + 2)
        h = heads[e]
        qg = q_gain[pl.ds(h, 1), :]
        kg = k_gain[pl.ds(h, 1), :]
        q_raw = jnp.concatenate([rows_of(r, base) for r in received], axis=0)
        gb = jnp.concatenate([rows_of(r, base + 1) for r in received], axis=0)
        k_parts = [rows_of(r, base + 2) for r in received]
        v_parts = [rows_of(r, base + 3) for r in received]
        for b in crossed:
            k_parts += [rows_of(b, base), rows_of(b, base + 2)]
            v_parts += [rows_of(b, base + 1), rows_of(b, base + 3)]
        if e == 1:
            k_parts += [rows_of(r, 8) for r in received]
            v_parts += [rows_of(r, 9) for r in received]
        k_raw = jnp.concatenate(k_parts, axis=0)
        vb = jnp.concatenate(v_parts, axis=0)
        qn, q_inv, qb = normalize(q_raw, qg)
        kn, k_inv, kb = normalize(k_raw, kg)
        p_rows = []
        w_blocks = []
        ds_blocks = []
        for i in range(4):
            rows = slice(i * TILE, (i + 1) * TILE)
            is_far = i in far
            spans = [(0, 256)]
            if is_far:
                spans.append((256, 640))
            if e == 1:
                spans.append((640 + i * TILE, 640 + (i + 1) * TILE))
            counts = []
            for j in range(4):
                if i == j:
                    counts.append(jnp.where(lower, 3.0 if is_far else 2.0, 0.0))
                else:
                    both = 2.0 if is_far and j in far else 1.0
                    earlier = (zl ^ j) < (zl ^ i)
                    counts.append(jnp.full((TILE, TILE), jnp.where(earlier, both, 0.0), F32))
            if is_far:
                for m in range(3):
                    counts.append(jnp.full((TILE, 2 * TILE), jnp.where(live[m], 1.0, 0.0), F32))
            if e == 1:
                counts.append(jnp.ones((TILE, TILE), F32))
            count = jnp.concatenate(counts, axis=1)
            keys = jnp.concatenate([kb[a:b] for a, b in spans], axis=0)
            vals = jnp.concatenate([vb[a:b] for a, b in spans], axis=0)
            s = jnp.where(count > 0.0, dot_nt(qb[rows], keys) * SCALE, NEG)
            dp = dot_nt(gb[rows], vals)
            top = jnp.max(s, axis=1, keepdims=True)
            total = jnp.sum(count * jnp.exp(s - top), axis=1, keepdims=True)
            p = count * jnp.exp(s - (top + jnp.log(total)))
            w = p.astype(BF)
            row_dot = jnp.sum(w.astype(F32) * dp, axis=1, keepdims=True)
            ds = (p * (dp - row_dot)).astype(BF)
            p_rows.append(dot_nn(ds, keys))
            w_blocks.append(w)
            ds_blocks.append(ds)
        dq = jnp.concatenate(p_rows, axis=0) * SCALE
        ds_own = jnp.concatenate([d[:, :256] for d in ds_blocks], axis=0)
        w_own = jnp.concatenate([w[:, :256] for w in w_blocks], axis=0)
        dk_own = dot_tn(ds_own, qb) * SCALE
        dv_own = dot_tn(w_own, gb)
        ds_far = jnp.concatenate([ds_blocks[i][:, 256:640] for i in far], axis=0)
        w_far = jnp.concatenate([w_blocks[i][:, 256:640] for i in far], axis=0)
        q_far = jnp.concatenate([qb[i * TILE : (i + 1) * TILE] for i in far], axis=0)
        g_far = jnp.concatenate([gb[i * TILE : (i + 1) * TILE] for i in far], axis=0)
        dk_far = dot_tn(ds_far, q_far) * SCALE
        dv_far = dot_tn(w_far, g_far)
        key_sum = jnp.sum(dk_own * kn[:256], axis=0, keepdims=True)
        key_sum += jnp.sum(dk_far * kn[256:640], axis=0, keepdims=True)
        gq = norm_grad(dq, qn, q_inv, qg)
        for i in range(4):
            rows = slice(i * TILE, (i + 1) * TILE)
            out = returned[i]
            out[3 * e * TILE : (3 * e + 1) * TILE, :] = gq[rows]
            out[(3 * e + 1) * TILE : (3 * e + 2) * TILE, :] = dk_own[rows].astype(BF)
            out[(3 * e + 2) * TILE : (3 * e + 3) * TILE, :] = dv_own[rows].astype(BF)
            if i in far:
                far_k[i] = dk_own[rows]
                far_v[i] = dv_own[rows]
            if e == 1:
                ds_x = ds_blocks[i][:, -TILE:]
                dk_x = dot_tn(ds_x, qb[rows]) * SCALE
                dv_x = dot_tn(w_blocks[i][:, -TILE:], gb[rows])
                key_sum += jnp.sum(dk_x * kn[640 + i * TILE : 704 + i * TILE], axis=0, keepdims=True)
                out[6 * TILE : 7 * TILE, :] = dk_x.astype(BF)
                out[7 * TILE : 8 * TILE, :] = dv_x.astype(BF)
        for m in range(3):
            rows = slice(m * 128, (m + 1) * 128)
            terms[m][256 * e : 256 * e + 128, :] = dk_far[rows].astype(BF)
            terms[m][256 * e + 128 : 256 * e + 256, :] = dv_far[rows].astype(BF)
        gains[pl.ds(h, 1), :] += jnp.sum(dq * qn, axis=0, keepdims=True)
        gains[pl.ds(HEADS + h, 1), :] += key_sum


def return_pack_kernel(far_k, far_v, u1, u2, u3, x0, x1, x2, x3, y0, y1, y2, y3):
    for i, (x, y) in enumerate(((x0, y0), (x1, y1), (x2, y2), (x3, y3))):
        e = i & 1
        at = 256 * e + 64 * (i >> 1)
        dk = far_k[i]
        dv = far_v[i]
        for u in (u1, u2, u3):
            dk += u[at : at + TILE, :].astype(F32)
            dv += u[at + 128 : at + 128 + TILE, :].astype(F32)
        first = (3 * e + 1) * TILE
        y[0:first, :] = x[0:first, :]
        y[first : first + TILE, :] = dk.astype(BF)
        y[first + TILE : first + 2 * TILE, :] = dv.astype(BF)
        y[first + 2 * TILE :, :] = x[first + 2 * TILE :, :]


def final_kernel(
    c_ref, y0, y1, y2, y3, m0, m1, m2, m3, part_k, part_v, k_gain, gq_in, gk_in, gv_in,
    gq_out, gk_out, gv_out, raw, done_k, done_v, sems, raw_sems,
):
    c = c_ref[0]
    copies = []

    def send(src, dst, e, h, n):
        copy = pltpu.make_async_copy(
            src, dst.at[pl.ds(e * TILE, TILE), pl.ds(pl.multiple_of(h * HD, HD), HD)], sems.at[n]
        )
        copy.start()
        copies.append(copy)

    sent = (m0, m1, m2, m3)
    fetches = []
    for step in range(4):
        for i, tile in enumerate((2, 6, 8)):
            copy = pltpu.make_async_copy(
                sent[step].at[pl.ds(tile * TILE, TILE), :], raw.at[3 * step + i], raw_sems.at[3 * step + i]
            )
            copy.start()
            fetches.append(copy)
    for step, y in enumerate((y0, y1, y2, y3)):
        h0, h1 = owned_heads(c, step)
        send(y.at[pl.ds(0, TILE), :], gq_out, 0, h0, 8 * step)
        send(y.at[pl.ds(3 * TILE, TILE), :], gq_out, 1, h1, 8 * step + 1)
        for i, (h, e, at) in enumerate(((h0, 0, 1), (h1, 1, 4), (h1, 0, 6))):
            n = 3 * step + i
            fetches[n].wait()
            kg = k_gain[pl.ds(h, 1), :]
            kn, k_inv, _ = normalize(raw[n], kg)
            dk = part_k[n] + y[at * TILE : (at + 1) * TILE, :].astype(F32)
            dv = part_v[n] + y[(at + 1) * TILE : (at + 2) * TILE, :].astype(F32)
            done_k[n] = norm_grad(dk, kn, k_inv, kg)
            done_v[n] = dv.astype(BF)
            send(done_k.at[n], gk_out, e, h, 8 * step + 2 + 2 * i)
            send(done_v.at[n], gv_out, e, h, 8 * step + 3 + 2 * i)
    for copy in copies:
        copy.wait()


def per_device(q_raw, k_raw, values, d_out, q_gain, k_gain):
    ctx_count = lax.axis_size("ctx")
    dp_count = lax.axis_size("dp")
    here = lax.axis_index("ctx").astype(jnp.int32).reshape(1)
    flat = lambda a: a.reshape(ROWS, HEADS * HD)
    q, k, v, g = flat(q_raw), flat(k_raw), flat(values), flat(d_out)
    qg = q_gain.reshape(HEADS, HD)
    kg = k_gain.reshape(HEADS, HD)
    params = pltpu.CompilerParams(vmem_limit_bytes=48 * 1024 * 1024)
    shape = jax.ShapeDtypeStruct

    def swap(block, axis, mask):
        count = ctx_count if axis == "ctx" else dp_count
        return lax.ppermute(block, axis, [(i, i ^ mask) for i in range(count)])

    def sends_on(a, b):
        return ((a >> 3) & 3) < ((b >> 3) & 3)

    steps = (12, 16, 28)

    def forward(block, mask):
        route = [(i, i ^ mask) for i in range(ctx_count) if sends_on(i, i ^ mask)]
        return lax.ppermute(block, "ctx", route)

    def backward(block, mask):
        route = [(i, i ^ mask) for i in range(ctx_count) if sends_on(i ^ mask, i)]
        return lax.ppermute(block, "ctx", route)

    packed = pl.pallas_call(
        pack_kernel,
        in_specs=[smem_spec()] + [any_spec()] * 4,
        out_specs=[any_spec()] * 4,
        out_shape=[shape((10 * TILE, HD), BF)] * 4,
        scratch_shapes=[pltpu.SemaphoreType.DMA((4, 10))],
        compiler_params=params,
        name="pack_tiles",
    )(here, q, k, v, g)
    arrived = [packed[0]] + [swap(packed[i], "ctx", 2 * i) for i in (1, 2, 3)]

    gq_home, gk_home, gv_home, part_k, part_v, home_gains = pl.pallas_call(
        home_kernel,
        in_specs=[smem_spec()] + [vmem_spec()] * 6,
        out_specs=[vmem_spec()] * 6,
        out_shape=[shape((ROWS, HEADS * HD), BF)] * 3
        + [shape((12, TILE, HD), F32)] * 2
        + [shape((2 * HEADS, HD), F32)],
        scratch_shapes=[pltpu.VMEM((HEADS, ROWS, HD), F32)] * 2,
        compiler_params=params,
        name="home_slab",
    )(here, q, k, v, g, qg, kg)

    onward = pl.pallas_call(
        forward_pack_kernel,
        in_specs=[any_spec()] * 4,
        out_specs=any_spec(),
        out_shape=shape((8 * TILE, HD), BF),
        scratch_shapes=[pltpu.SemaphoreType.DMA((4,))],
        compiler_params=params,
        name="pack_far_rows",
    )(*arrived)
    crossed = [forward(onward, mask) for mask in steps]

    outs = pl.pallas_call(
        owner_kernel,
        in_specs=[smem_spec()] + [vmem_spec()] * 10,
        out_specs=[vmem_spec()] * 10,
        out_shape=[shape((8 * TILE, HD), BF)] * 7
        + [shape((4, TILE, HD), F32)] * 2
        + [shape((2 * HEADS, HD), F32)],
        compiler_params=params,
        name="owned_heads",
    )(here, *arrived, *crossed, qg, kg, home_gains)
    back, terms, far_k, far_v, gains = outs[:4], outs[4:7], outs[7], outs[8], outs[9]
    terms_in = [backward(terms[i], mask) for i, mask in enumerate(steps)]

    def pair_sum(x, axis, mask):
        return x + swap(x, axis, mask)

    def quad_sum(x, axis, mask):
        one, two, three = (swap(x, axis, i * mask) for i in (1, 2, 3))
        return (x + one) + (two + three)

    gains = pair_sum(gains, "ctx", 1)
    if dp_count == 8:
        gains = quad_sum(gains, "dp", 1)
        gains = pair_sum(gains, "dp", 4)
    gains = quad_sum(gains, "ctx", 2)
    gains = pair_sum(gains, "ctx", 12)
    gains = pair_sum(gains, "ctx", 16)

    back = pl.pallas_call(
        return_pack_kernel,
        in_specs=[vmem_spec()] * 9,
        out_specs=[vmem_spec()] * 4,
        out_shape=[shape((8 * TILE, HD), BF)] * 4,
        compiler_params=params,
        name="add_far_terms",
    )(far_k, far_v, *terms_in, *back)
    home = [back[0]] + [swap(back[i], "ctx", 2 * i) for i in (1, 2, 3)]

    gq, gk, gv = pl.pallas_call(
        final_kernel,
        in_specs=[smem_spec()]
        + [vmem_spec()] * 4
        + [any_spec()] * 4
        + [vmem_spec()] * 3
        + [any_spec()] * 3,
        out_specs=[any_spec()] * 3,
        out_shape=[shape((ROWS, HEADS * HD), BF)] * 3,
        scratch_shapes=[pltpu.VMEM((12, TILE, HD), BF)] * 3
        + [pltpu.SemaphoreType.DMA((32,)), pltpu.SemaphoreType.DMA((12,))],
        input_output_aliases={12: 0, 13: 1, 14: 2},
        compiler_params=params,
        name="finish_rows",
    )(here, *home, *packed, part_k, part_v, kg, gq_home, gk_home, gv_home)
    whole = lambda a: a.reshape(1, ROWS, HEADS * HD)
    return (
        whole(gq),
        whole(gk),
        whole(gv),
        gains[:HEADS].reshape(HEADS * HD),
        gains[HEADS:].reshape(HEADS * HD),
    )


def solution(mesh):
    rows = P("dp", "ctx", None)
    return jax.shard_map(
        per_device,
        mesh=mesh,
        in_specs=(rows, rows, rows, rows, P(), P()),
        out_specs=(rows, rows, rows, P(), P()),
        check_vma=False,
    )
```

time: 353 us -> 103 us (0.29)
  the two profiles are of different devices: /device:TPU:1 before, /device:TPU:4 now
where the time goes in v1:
time: 103 us
  starting transfers between devices  44.3 us (43%)
  waiting for transfers between devices  34.8 us (34%)
  Pallas kernels  18.1 us (18%)
  local copies, waits for them, and re-layouts  4.78 us (5%)
    ppermute x16, waiting for transfers between devices, swap(): return lax.ppermute(block, axis, [(i, i ^ mask) for i in range(count)])  34.7 us
    ppermute x16, starting transfers between devices, swap(): return lax.ppermute(block, axis, [(i, i ^ mask) for i in range(count)])  20.3 us
    ppermute x3, starting transfers between devices, backward(): return lax.ppermute(block, 'ctx', route)  12.8 us
    ppermute x3, starting transfers between devices, forward(): return lax.ppermute(block, 'ctx', route)  11.2 us
    pallas_call x1, Pallas kernels, per_device(): pl.pallas_call(home_kernel, in_specs=[smem_spec()] + [vmem_spec()] * 6, o...  9.36 us
    pallas_call x1, Pallas kernels, per_device(): pl.pallas_call(owner_kernel, in_specs=[smem_spec()] + [vmem_spec()] * 10,...  4.39 us
    unnamed x16, local copies, waits for them, and re-layouts  4.18 us
    pallas_call x1, Pallas kernels, per_device(): pl.pallas_call(final_kernel, in_specs=[smem_spec()] + [vmem_spec()] * 4 +...  3.39 us
  transfers between devices with their start and end apart: 22, of which 10 were waited for; matrix products, arithmetic and copies ran while one was open for 1% of the time, Pallas kernels for 9%

profile of v1, /device:TPU:4, one launch (start us, length us, event | category | flops | bytes accessed | tf_op | source)
XLA Modules:
  0.0 103.0 jit_solution(11705933095071637706)
XLA Ops:
  0.6 1.0 %copy-done = bf16[1,128,2048]{2,1,0:T(8,128)(2,1)S(1)} copy-done((bf16[1,128,2048]{2,1,0:T(8,128)(2,1)S(1)}, bf16[1,128,2048]{2,1,0:T(8,128)(2,1)}, u32[]{:S(2)}) %copy-start) | copy-done | bytes 524312
  1.7 1.0 %copy-done.2 = bf16[1,128,2048]{2,1,0:T(8,128)(2,1)S(1)} copy-done((bf16[1,128,2048]{2,1,0:T(8,128)(2,1)S(1)}, bf16[1,128,2048]{2,1,0:T(8,128)(2,1)}, u32[]{:S(2)}) %copy-start.2) | copy-done | bytes 524312
  2.7 1.0 %copy-done.4 = bf16[1,128,2048]{2,1,0:T(8,128)(2,1)S(1)} copy-done((bf16[1,128,2048]{2,1,0:T(8,128)(2,1)S(1)}, bf16[1,128,2048]{2,1,0:T(8,128)(2,1)}, u32[]{:S(2)}) %copy-start.4) | copy-done | bytes 524312
  3.8 1.0 %copy-done.5 = bf16[1,128,2048]{2,1,0:T(8,128)(2,1)S(1)} copy-done((bf16[1,128,2048]{2,1,0:T(8,128)(2,1)S(1)}, bf16[1,128,2048]{2,1,0:T(8,128)(2,1)}, u32[]{:S(2)}) %copy-start.5) | copy-done | bytes 524312
  5.5 2.0 %collective-permute-start = (bf16[640,128]{1,0:T(8,128)(2,1)S(1)}, bf16[640,128]{1,0:T(8,128)(2,1)S(1)}, u32[]{:S(2)}, u32[]{:S(2)}) collective-permute-start(bf16[640,128]{1,0:T(8,128)(2,1)S(1)} %get-tuple-element.33.m1), channel_id=1, source_target_pairs={{0,2},{1,3},{2,0},{3,1},{4,6},{5,7},{6,4},{7,5},{8,10},{9,11},{10,... | collective-permute-start | bytes 491528 | tf_op jit(solution)/shard_map/ppermute | solution.py:339
  7.5 3.3 %collective-permute-start.1 = (bf16[640,128]{1,0:T(8,128)(2,1)S(1)}, bf16[640,128]{1,0:T(8,128)(2,1)S(1)}, u32[]{:S(2)}, u32[]{:S(2)}) collective-permute-start(bf16[640,128]{1,0:T(8,128)(2,1)S(1)} %get-tuple-element.34.m2), channel_id=1, source_target_pairs={{0,4},{1,5},{2,6},{3,7},{4,0},{5,1},{6,2},{7,3},{8,12},{9,13},{10,... | collective-permute-start | bytes 491528 | tf_op jit(solution)/shard_map/ppermute | solution.py:339
  10.8 3.4 %collective-permute-done.r1 = bf16[640,128]{1,0:T(8,128)(2,1)S(1)} collective-permute-done((bf16[640,128]{1,0:T(8,128)(2,1)S(1)}, bf16[640,128]{1,0:T(8,128)(2,1)S(1)}, u32[]{:S(2)}, u32[]{:S(2)}) %collective-permute-start) | collective-permute-done | bytes 163872 | tf_op jit(solution)/shard_map/ppermute | solution.py:339
  14.2 8.7 %collective-permute-done.1.r2 = bf16[640,128]{1,0:T(8,128)(2,1)S(1)} collective-permute-done((bf16[640,128]{1,0:T(8,128)(2,1)S(1)}, bf16[640,128]{1,0:T(8,128)(2,1)S(1)}, u32[]{:S(2)}, u32[]{:S(2)}) %collective-permute-start.1) | collective-permute-done | bytes 163872 | tf_op jit(solution)/shard_map/ppermute | solution.py:339
  23.1 1.3 %collective-permute-start.5 = (bf16[512,128]{1,0:T(8,128)(2,1)S(1)}, bf16[512,128]{1,0:T(8,128)(2,1)S(1)}, u32[]{:S(2)}, u32[]{:S(2)}) collective-permute-start(bf16[512,128]{1,0:T(8,128)(2,1)S(1)} %pack_far_rows.1), channel_id=1, source_target_pairs={{0,28},{1,29},{2,30},{3,31},{4,24},{5,25},{6,26},{7,27},{8,20},{9,... | collective-permute-start | bytes 393224 | tf_op jit(solution)/shard_map/ppermute | solution.py:348
  24.4 1.3 %collective-permute-start.4 = (bf16[512,128]{1,0:T(8,128)(2,1)S(1)}, bf16[512,128]{1,0:T(8,128)(2,1)S(1)}, u32[]{:S(2)}, u32[]{:S(2)}) collective-permute-start(bf16[512,128]{1,0:T(8,128)(2,1)S(1)} %pack_far_rows.1), channel_id=1, source_target_pairs={{0,16},{1,17},{2,18},{3,19},{4,20},{5,21},{6,22},{7,23},{8,24},{9,... | collective-permute-start | bytes 393224 | tf_op jit(solution)/shard_map/ppermute | solution.py:348
  25.7 8.6 %collective-permute-start.3 = (bf16[512,128]{1,0:T(8,128)(2,1)S(1)}, bf16[512,128]{1,0:T(8,128)(2,1)S(1)}, u32[]{:S(2)}, u32[]{:S(2)}) collective-permute-start(bf16[512,128]{1,0:T(8,128)(2,1)S(1)} %pack_far_rows.1), channel_id=1, source_target_pairs={{0,12},{1,13},{2,14},{3,15},{4,8},{5,9},{6,10},{7,11},{16,28},{17,... | collective-permute-start | bytes 393224 | tf_op jit(solution)/shard_map/ppermute | solution.py:348
  34.3 9.4 %home_slab.1 = (bf16[128,2048]{1,0:T(8,128)(2,1)}, bf16[128,2048]{1,0:T(8,128)(2,1)}, bf16[128,2048]{1,0:T(8,128)(2,1)}, f32[12,64,128]{2,1,0:T(8,128)S(1)}, f32...) custom-call(s32[1]{0:T(128)} %bitcast.c_ref, bf16[128,2048]{1,0:T(8,128)(2,1)S(1)} %bitcast.15, ...), custom_call_target="tpu_custom_call" | custom-call | tf_op jit(solution)/shard_map/home_slab/pallas_call | solution.py:365
  43.7 4.4 %owned_heads.1 = (bf16[512,128]{1,0:T(8,128)(2,1)S(1)}, bf16[512,128]{1,0:T(8,128)(2,1)S(1)}, bf16[512,128]{1,0:T(8,128)(2,1)S(1)}, bf16[512,128]{1,0:T(8,128)(2...) custom-call(s32[1]{0:T(128)} %bitcast.c_ref, ...), custom_call_target="tpu_custom_call" | custom-call | tf_op jit(solution)/shard_map/owned_heads/pallas_call | solution.py:388
  48.2 1.2 %collective-permute-done.12 = f32[32,128]{1,0:T(8,128)S(1)} collective-permute-done((f32[32,128]{1,0:T(8,128)S(1)}, f32[32,128]{1,0:T(8,128)S(1)}, u32[]{:S(2)}, u32[]{:S(2)}) %collective-permute-start.12) | collective-permute-done | bytes 16416 | tf_op jit(solution)/shard_map/ppermute | solution.py:339
  49.4 3.0 %collective-permute-start.15 = (f32[32,128]{1,0:T(8,128)S(1)}, f32[32,128]{1,0:T(8,128)S(1)}, u32[]{:S(2)}, u32[]{:S(2)}) collective-permute-start(f32[32,128]{1,0:T(8,128)S(1)} %add.30), channel_id=1, source_target_pairs={{0,96},{32,64},{64,32},{96,0},{128,224},{160,192},{192,160},{224,1... | collective-permute-start | bytes 49160 | tf_op jit(solution)/shard_map/ppermute | solution.py:339
  53.5 0.8 collective-permute-done.15
  54.3 3.3 %collective-permute-done.14 = f32[32,128]{1,0:T(8,128)S(1)} collective-permute-done((f32[32,128]{1,0:T(8,128)S(1)}, f32[32,128]{1,0:T(8,128)S(1)}, u32[]{:S(2)}, u32[]{:S(2)}) %collective-permute-start.14) | collective-permute-done | bytes 16416 | tf_op jit(solution)/shard_map/ppermute | solution.py:339
  57.6 1.3 %collective-permute-start.16 = (f32[32,128]{1,0:T(8,128)S(1)}, f32[32,128]{1,0:T(8,128)S(1)}, u32[]{:S(2)}, u32[]{:S(2)}) collective-permute-start(f32[32,128]{1,0:T(8,128)S(1)} %add_add_fusion.1), channel_id=1, source_target_pairs={{0,128},{32,160},{64,192},{96,224},{128,0},{160,32},{192,64},{224,... | collective-permute-start | bytes 49160 | tf_op jit(solution)/shard_map/ppermute | solution.py:339
  58.9 2.5 %collective-permute-done.16 = f32[32,128]{1,0:T(8,128)S(1)} collective-permute-done((f32[32,128]{1,0:T(8,128)S(1)}, f32[32,128]{1,0:T(8,128)S(1)}, u32[]{:S(2)}, u32[]{:S(2)}) %collective-permute-start.16) | collective-permute-done | bytes 16416 | tf_op jit(solution)/shard_map/ppermute | solution.py:339
  61.5 1.9 %collective-permute-start.19 = (f32[32,128]{1,0:T(8,128)S(1)}, f32[32,128]{1,0:T(8,128)S(1)}, u32[]{:S(2)}, u32[]{:S(2)}) collective-permute-start(f32[32,128]{1,0:T(8,128)S(1)} %add.34), channel_id=1, source_target_pairs={{0,6},{1,7},{2,4},{3,5},{4,2},{5,3},{6,0},{7,1},{8,14},{9,15},{10,... | collective-permute-start | bytes 49160 | tf_op jit(solution)/shard_map/ppermute | solution.py:339
  63.4 2.5 %collective-permute-start.17 = (f32[32,128]{1,0:T(8,128)S(1)}, f32[32,128]{1,0:T(8,128)S(1)}, u32[]{:S(2)}, u32[]{:S(2)}) collective-permute-start(f32[32,128]{1,0:T(8,128)S(1)} %add.34), channel_id=1, source_target_pairs={{0,2},{1,3},{2,0},{3,1},{4,6},{5,7},{6,4},{7,5},{8,10},{9,11},{10,... | collective-permute-start | bytes 49160 | tf_op jit(solution)/shard_map/ppermute | solution.py:339
  65.9 1.3 %collective-permute-start.6 = (bf16[512,128]{1,0:T(8,128)(2,1)S(1)}, bf16[512,128]{1,0:T(8,128)(2,1)S(1)}, u32[]{:S(2)}, u32[]{:S(2)}) collective-permute-start(bf16[512,128]{1,0:T(8,128)(2,1)S(1)} %get-tuple-element.39), channel_id=1, source_target_pairs={{8,4},{9,5},{10,6},{11,7},{12,0},{13,1},{14,2},{15,3},{24,20},{25,... | collective-permute-start | bytes 393224 | tf_op jit(solution)/shard_map/ppermute | solution.py:352
  67.2 6.1 %collective-permute-start.7 = (bf16[512,128]{1,0:T(8,128)(2,1)S(1)}, bf16[512,128]{1,0:T(8,128)(2,1)S(1)}, u32[]{:S(2)}, u32[]{:S(2)}) collective-permute-start(bf16[512,128]{1,0:T(8,128)(2,1)S(1)} %get-tuple-element.40), channel_id=1, source_target_pairs={{16,0},{17,1},{18,2},{19,3},{20,4},{21,5},{22,6},{23,7},{24,8},{25... | collective-permute-start | bytes 393224 | tf_op jit(solution)/shard_map/ppermute | solution.py:352
  73.2 5.5 %collective-permute-start.8 = (bf16[512,128]{1,0:T(8,128)(2,1)S(1)}, bf16[512,128]{1,0:T(8,128)(2,1)S(1)}, u32[]{:S(2)}, u32[]{:S(2)}) collective-permute-start(bf16[512,128]{1,0:T(8,128)(2,1)S(1)} %get-tuple-element.41), channel_id=1, source_target_pairs={{16,12},{17,13},{18,14},{19,15},{20,8},{21,9},{22,10},{23,11},{24,... | collective-permute-start | bytes 393224 | tf_op jit(solution)/shard_map/ppermute | solution.py:352
  78.8 0.7 collective-permute-start.20
  79.4 5.3 %collective-permute-done.20 = f32[32,128]{1,0:T(8,128)S(1)} collective-permute-done((f32[32,128]{1,0:T(8,128)S(1)}, f32[32,128]{1,0:T(8,128)S(1)}, u32[]{:S(2)}, u32[]{:S(2)}) %collective-permute-start.20) | collective-permute-done | bytes 16416 | tf_op jit(solution)/shard_map/ppermute | solution.py:339
  84.7 5.2 %collective-permute-done.21 = f32[32,128]{1,0:T(8,128)S(1)} collective-permute-done((f32[32,128]{1,0:T(8,128)S(1)}, f32[32,128]{1,0:T(8,128)S(1)}, u32[]{:S(2)}, u32[]{:S(2)}) %collective-permute-start.21) | collective-permute-done | bytes 16416 | tf_op jit(solution)/shard_map/ppermute | solution.py:339
  90.2 2.5 %collective-permute-start.10 = (bf16[512,128]{1,0:T(8,128)(2,1)S(1)}, bf16[512,128]{1,0:T(8,128)(2,1)S(1)}, u32[]{:S(2)}, u32[]{:S(2)}) collective-permute-start(bf16[512,128]{1,0:T(8,128)(2,1)S(1)} %get-tuple-element.48), channel_id=1, source_target_pairs={{0,4},{1,5},{2,6},{3,7},{4,0},{5,1},{6,2},{7,3},{8,12},{9,13},{10,... | collective-permute-start | bytes 393224 | tf_op jit(solution)/shard_map/ppermute | solution.py:339
  92.6 1.9 %collective-permute-start.11 = (bf16[512,128]{1,0:T(8,128)(2,1)S(1)}, bf16[512,128]{1,0:T(8,128)(2,1)S(1)}, u32[]{:S(2)}, u32[]{:S(2)}) collective-permute-start(bf16[512,128]{1,0:T(8,128)(2,1)S(1)} %get-tuple-element.49), channel_id=1, source_target_pairs={{0,6},{1,7},{2,4},{3,5},{4,2},{5,3},{6,0},{7,1},{8,14},{9,15},{10,... | collective-permute-start | bytes 393224 | tf_op jit(solution)/shard_map/ppermute | solution.py:339
  95.2 1.4 %collective-permute-done.9.y1 = bf16[512,128]{1,0:T(8,128)(2,1)S(1)} collective-permute-done((bf16[512,128]{1,0:T(8,128)(2,1)S(1)}, bf16[512,128]{1,0:T(8,128)(2,1)S(1)}, u32[]{:S(2)}, u32[]{:S(2)}) %collective-permute-start.9) | collective-permute-done | bytes 131104 | tf_op jit(solution)/shard_map/ppermute | solution.py:339
  96.5 2.9 %collective-permute-done.11.y3 = bf16[512,128]{1,0:T(8,128)(2,1)S(1)} collective-permute-done((bf16[512,128]{1,0:T(8,128)(2,1)S(1)}, bf16[512,128]{1,0:T(8,128)(2,1)S(1)}, u32[]{:S(2)}, u32[]{:S(2)}) %collective-permute-start.11) | collective-permute-done | bytes 131104 | tf_op jit(solution)/shard_map/ppermute | solution.py:339
  99.5 3.4 %finish_rows.1 = (bf16[128,2048]{1,0:T(8,128)(2,1)}, bf16[128,2048]{1,0:T(8,128)(2,1)}, bf16[128,2048]{1,0:T(8,128)(2,1)}) custom-call(s32[1]{0:T(128)} %bitcast.c_ref, bf16[512,128]{1,0:T(8,128)(2,1)S(1)} %get-tuple-element.46.y0, bf16[512,128]{1,0:T(8,128)(2,1)S(1)} %collective-permute-done.9.y1, ...), custom_call_target="tpu_custom_call", output_to_operand_aliasing={{0}: (12, {}), {1}: (13, {}), {2}: (14, {})} | custom-call | tf_op jit(solution)/shard_map/finish_rows/pallas_call | solution.py:426
  (41 shorter events, 3.0 us)
Async XLA Ops:
  0.6 1.0 %copy-start = (bf16[1,128,2048]{2,1,0:T(8,128)(2,1)S(1)}, bf16[1,128,2048]{2,1,0:T(8,128)(2,1)}, u32[]{:S(2)}) copy-start(bf16[1,128,2048]{2,1,0:T(8,128)(2,1)} %param.6) | copy-start | bytes 1572868
  1.7 1.0 %copy-start.2 = (bf16[1,128,2048]{2,1,0:T(8,128)(2,1)S(1)}, bf16[1,128,2048]{2,1,0:T(8,128)(2,1)}, u32[]{:S(2)}) copy-start(bf16[1,128,2048]{2,1,0:T(8,128)(2,1)} %param.7) | copy-start | bytes 1572868
  2.7 1.0 %copy-start.4 = (bf16[1,128,2048]{2,1,0:T(8,128)(2,1)S(1)}, bf16[1,128,2048]{2,1,0:T(8,128)(2,1)}, u32[]{:S(2)}) copy-start(bf16[1,128,2048]{2,1,0:T(8,128)(2,1)} %param.8) | copy-start | bytes 1572868
  3.8 1.0 %copy-start.5 = (bf16[1,128,2048]{2,1,0:T(8,128)(2,1)S(1)}, bf16[1,128,2048]{2,1,0:T(8,128)(2,1)}, u32[]{:S(2)}) copy-start(bf16[1,128,2048]{2,1,0:T(8,128)(2,1)} %param.9) | copy-start | bytes 1572868
  4.8 29.5 %copy-start.3 = (bf16[1,128,2048]{2,1,0:T(8,128)(2,1)S(1)}, bf16[1,128,2048]{2,1,0:T(8,128)(2,1)}, u32[]{:S(2)}) copy-start(bf16[1,128,2048]{2,1,0:T(8,128)(2,1)} %param.7) | copy-start | bytes 1572868
  5.5 28.8 %copy-start.1 = (bf16[1,128,2048]{2,1,0:T(8,128)(2,1)S(1)}, bf16[1,128,2048]{2,1,0:T(8,128)(2,1)}, u32[]{:S(2)}) copy-start(bf16[1,128,2048]{2,1,0:T(8,128)(2,1)} %param.6) | copy-start | bytes 1572868
  5.5 8.7 %collective-permute-start = (bf16[640,128]{1,0:T(8,128)(2,1)S(1)}, bf16[640,128]{1,0:T(8,128)(2,1)S(1)}, u32[]{:S(2)}, u32[]{:S(2)}) collective-permute-start(bf16[640,128]{1,0:T(8,128)(2,1)S(1)} %get-tuple-element.33.m1), channel_id=1, source_target_pairs={{0,2},{1,3},{2,0},{3,1},{4,6},{5,7},{6,4},{7,5},{8,10},{9,11},{10,... | collective-permute-start | bytes 491528 | tf_op jit(solution)/shard_map/ppermute | solution.py:339
  7.5 15.4 %collective-permute-start.1 = (bf16[640,128]{1,0:T(8,128)(2,1)S(1)}, bf16[640,128]{1,0:T(8,128)(2,1)S(1)}, u32[]{:S(2)}, u32[]{:S(2)}) collective-permute-start(bf16[640,128]{1,0:T(8,128)(2,1)S(1)} %get-tuple-element.34.m2), channel_id=1, source_target_pairs={{0,4},{1,5},{2,6},{3,7},{4,0},{5,1},{6,2},{7,3},{8,12},{9,13},{10,... | collective-permute-start | bytes 491528 | tf_op jit(solution)/shard_map/ppermute | solution.py:339
  10.7 12.1 %collective-permute-start.2 = (bf16[640,128]{1,0:T(8,128)(2,1)S(1)}, bf16[640,128]{1,0:T(8,128)(2,1)S(1)}, u32[]{:S(2)}, u32[]{:S(2)}) collective-permute-start(bf16[640,128]{1,0:T(8,128)(2,1)S(1)} %get-tuple-element.35.m3), channel_id=1, source_target_pairs={{0,6},{1,7},{2,4},{3,5},{4,2},{5,3},{6,0},{7,1},{8,14},{9,15},{10,... | collective-permute-start | bytes 491528 | tf_op jit(solution)/shard_map/ppermute | solution.py:339
  22.8 11.5 %copy-start.6 = (f32[2048]{0:T(1024)S(1)}, f32[2048]{0:T(1024)}, u32[]{:S(2)}) copy-start(f32[2048]{0:T(1024)} %param.11) | copy-start | bytes 24580
  22.8 11.5 %copy-start.7 = (f32[2048]{0:T(1024)S(1)}, f32[2048]{0:T(1024)}, u32[]{:S(2)}) copy-start(f32[2048]{0:T(1024)} %param.10) | copy-start | bytes 24580
  23.1 20.6 %collective-permute-start.5 = (bf16[512,128]{1,0:T(8,128)(2,1)S(1)}, bf16[512,128]{1,0:T(8,128)(2,1)S(1)}, u32[]{:S(2)}, u32[]{:S(2)}) collective-permute-start(bf16[512,128]{1,0:T(8,128)(2,1)S(1)} %pack_far_rows.1), channel_id=1, source_target_pairs={{0,28},{1,29},{2,30},{3,31},{4,24},{5,25},{6,26},{7,27},{8,20},{9,... | collective-permute-start | bytes 393224 | tf_op jit(solution)/shard_map/ppermute | solution.py:348
  24.4 19.3 %collective-permute-start.4 = (bf16[512,128]{1,0:T(8,128)(2,1)S(1)}, bf16[512,128]{1,0:T(8,128)(2,1)S(1)}, u32[]{:S(2)}, u32[]{:S(2)}) collective-permute-start(bf16[512,128]{1,0:T(8,128)(2,1)S(1)} %pack_far_rows.1), channel_id=1, source_target_pairs={{0,16},{1,17},{2,18},{3,19},{4,20},{5,21},{6,22},{7,23},{8,24},{9,... | collective-permute-start | bytes 393224 | tf_op jit(solution)/shard_map/ppermute | solution.py:348
  25.7 18.0 %collective-permute-start.3 = (bf16[512,128]{1,0:T(8,128)(2,1)S(1)}, bf16[512,128]{1,0:T(8,128)(2,1)S(1)}, u32[]{:S(2)}, u32[]{:S(2)}) collective-permute-start(bf16[512,128]{1,0:T(8,128)(2,1)S(1)} %pack_far_rows.1), channel_id=1, source_target_pairs={{0,12},{1,13},{2,14},{3,15},{4,8},{5,9},{6,10},{7,11},{16,28},{17,... | collective-permute-start | bytes 393224 | tf_op jit(solution)/shard_map/ppermute | solution.py:348
  48.1 1.3 %collective-permute-start.12 = (f32[32,128]{1,0:T(8,128)S(1)}, f32[32,128]{1,0:T(8,128)S(1)}, u32[]{:S(2)}, u32[]{:S(2)}) collective-permute-start(f32[32,128]{1,0:T(8,128)S(1)} %get-tuple-element.58), channel_id=1, source_target_pairs={{0,1},{1,0},{2,3},{3,2},{4,5},{5,4},{6,7},{7,6},{8,9},{9,8},{10,11... | collective-permute-start | bytes 49160 | tf_op jit(solution)/shard_map/ppermute | solution.py:339
  49.4 4.9 %collective-permute-start.15 = (f32[32,128]{1,0:T(8,128)S(1)}, f32[32,128]{1,0:T(8,128)S(1)}, u32[]{:S(2)}, u32[]{:S(2)}) collective-permute-start(f32[32,128]{1,0:T(8,128)S(1)} %add.30), channel_id=1, source_target_pairs={{0,96},{32,64},{64,32},{96,0},{128,224},{160,192},{192,160},{224,1... | collective-permute-start | bytes 49160 | tf_op jit(solution)/shard_map/ppermute | solution.py:339
  52.4 5.2 %collective-permute-start.14 = (f32[32,128]{1,0:T(8,128)S(1)}, f32[32,128]{1,0:T(8,128)S(1)}, u32[]{:S(2)}, u32[]{:S(2)}) collective-permute-start(f32[32,128]{1,0:T(8,128)S(1)} %add.30), channel_id=1, source_target_pairs={{0,64},{32,96},{64,0},{96,32},{128,192},{160,224},{192,128},{224,1... | collective-permute-start | bytes 49160 | tf_op jit(solution)/shard_map/ppermute | solution.py:339
  53.0 4.6 %collective-permute-start.13 = (f32[32,128]{1,0:T(8,128)S(1)}, f32[32,128]{1,0:T(8,128)S(1)}, u32[]{:S(2)}, u32[]{:S(2)}) collective-permute-start(f32[32,128]{1,0:T(8,128)S(1)} %add.30), channel_id=1, source_target_pairs={{0,32},{32,0},{64,96},{96,64},{128,160},{160,128},{192,224},{224,1... | collective-permute-start | bytes 49160 | tf_op jit(solution)/shard_map/ppermute | solution.py:339
  57.6 3.8 %collective-permute-start.16 = (f32[32,128]{1,0:T(8,128)S(1)}, f32[32,128]{1,0:T(8,128)S(1)}, u32[]{:S(2)}, u32[]{:S(2)}) collective-permute-start(f32[32,128]{1,0:T(8,128)S(1)} %add_add_fusion.1), channel_id=1, source_target_pairs={{0,128},{32,160},{64,192},{96,224},{128,0},{160,32},{192,64},{224,... | collective-permute-start | bytes 49160 | tf_op jit(solution)/shard_map/ppermute | solution.py:339
  61.5 11.7 %collective-permute-start.19 = (f32[32,128]{1,0:T(8,128)S(1)}, f32[32,128]{1,0:T(8,128)S(1)}, u32[]{:S(2)}, u32[]{:S(2)}) collective-permute-start(f32[32,128]{1,0:T(8,128)S(1)} %add.34), channel_id=1, source_target_pairs={{0,6},{1,7},{2,4},{3,5},{4,2},{5,3},{6,0},{7,1},{8,14},{9,15},{10,... | collective-permute-start | bytes 49160 | tf_op jit(solution)/shard_map/ppermute | solution.py:339
  63.4 15.3 %collective-permute-start.18 = (f32[32,128]{1,0:T(8,128)S(1)}, f32[32,128]{1,0:T(8,128)S(1)}, u32[]{:S(2)}, u32[]{:S(2)}) collective-permute-start(f32[32,128]{1,0:T(8,128)S(1)} %add.34), channel_id=1, source_target_pairs={{0,4},{1,5},{2,6},{3,7},{4,0},{5,1},{6,2},{7,3},{8,12},{9,13},{10,... | collective-permute-start | bytes 49160 | tf_op jit(solution)/shard_map/ppermute | solution.py:339
  63.4 15.3 %collective-permute-start.17 = (f32[32,128]{1,0:T(8,128)S(1)}, f32[32,128]{1,0:T(8,128)S(1)}, u32[]{:S(2)}, u32[]{:S(2)}) collective-permute-start(f32[32,128]{1,0:T(8,128)S(1)} %add.34), channel_id=1, source_target_pairs={{0,2},{1,3},{2,0},{3,1},{4,6},{5,7},{6,4},{7,5},{8,10},{9,11},{10,... | collective-permute-start | bytes 49160 | tf_op jit(solution)/shard_map/ppermute | solution.py:339
  65.9 24.1 %collective-permute-start.6 = (bf16[512,128]{1,0:T(8,128)(2,1)S(1)}, bf16[512,128]{1,0:T(8,128)(2,1)S(1)}, u32[]{:S(2)}, u32[]{:S(2)}) collective-permute-start(bf16[512,128]{1,0:T(8,128)(2,1)S(1)} %get-tuple-element.39), channel_id=1, source_target_pairs={{8,4},{9,5},{10,6},{11,7},{12,0},{13,1},{14,2},{15,3},{24,20},{25,... | collective-permute-start | bytes 393224 | tf_op jit(solution)/shard_map/ppermute | solution.py:352
  67.2 22.8 %collective-permute-start.7 = (bf16[512,128]{1,0:T(8,128)(2,1)S(1)}, bf16[512,128]{1,0:T(8,128)(2,1)S(1)}, u32[]{:S(2)}, u32[]{:S(2)}) collective-permute-start(bf16[512,128]{1,0:T(8,128)(2,1)S(1)} %get-tuple-element.40), channel_id=1, source_target_pairs={{16,0},{17,1},{18,2},{19,3},{20,4},{21,5},{22,6},{23,7},{24,8},{25... | collective-permute-start | bytes 393224 | tf_op jit(solution)/shard_map/ppermute | solution.py:352
  73.2 16.7 %collective-permute-start.8 = (bf16[512,128]{1,0:T(8,128)(2,1)S(1)}, bf16[512,128]{1,0:T(8,128)(2,1)S(1)}, u32[]{:S(2)}, u32[]{:S(2)}) collective-permute-start(bf16[512,128]{1,0:T(8,128)(2,1)S(1)} %get-tuple-element.41), channel_id=1, source_target_pairs={{16,12},{17,13},{18,14},{19,15},{20,8},{21,9},{22,10},{23,11},{24,... | collective-permute-start | bytes 393224 | tf_op jit(solution)/shard_map/ppermute | solution.py:352
  78.8 5.9 %collective-permute-start.20 = (f32[32,128]{1,0:T(8,128)S(1)}, f32[32,128]{1,0:T(8,128)S(1)}, u32[]{:S(2)}, u32[]{:S(2)}) collective-permute-start(f32[32,128]{1,0:T(8,128)S(1)} %add_add_fusion), channel_id=1, source_target_pairs={{0,12},{1,13},{2,14},{3,15},{4,8},{5,9},{6,10},{7,11},{8,4},{9,5},... | collective-permute-start | bytes 49160 | tf_op jit(solution)/shard_map/ppermute | solution.py:339
  84.7 5.2 %collective-permute-start.21 = (f32[32,128]{1,0:T(8,128)S(1)}, f32[32,128]{1,0:T(8,128)S(1)}, u32[]{:S(2)}, u32[]{:S(2)}) collective-permute-start(f32[32,128]{1,0:T(8,128)S(1)} %add.38), channel_id=1, source_target_pairs={{0,16},{1,17},{2,18},{3,19},{4,20},{5,21},{6,22},{7,23},{8,24},{9,... | collective-permute-start | bytes 49160 | tf_op jit(solution)/shard_map/ppermute | solution.py:339
  90.1 6.5 %collective-permute-start.9 = (bf16[512,128]{1,0:T(8,128)(2,1)S(1)}, bf16[512,128]{1,0:T(8,128)(2,1)S(1)}, u32[]{:S(2)}, u32[]{:S(2)}) collective-permute-start(bf16[512,128]{1,0:T(8,128)(2,1)S(1)} %get-tuple-element.47), channel_id=1, source_target_pairs={{0,2},{1,3},{2,0},{3,1},{4,6},{5,7},{6,4},{7,5},{8,10},{9,11},{10,... | collective-permute-start | bytes 393224 | tf_op jit(solution)/shard_map/ppermute | solution.py:339
  90.2 6.4 %collective-permute-start.10 = (bf16[512,128]{1,0:T(8,128)(2,1)S(1)}, bf16[512,128]{1,0:T(8,128)(2,1)S(1)}, u32[]{:S(2)}, u32[]{:S(2)}) collective-permute-start(bf16[512,128]{1,0:T(8,128)(2,1)S(1)} %get-tuple-element.48), channel_id=1, source_target_pairs={{0,4},{1,5},{2,6},{3,7},{4,0},{5,1},{6,2},{7,3},{8,12},{9,13},{10,... | collective-permute-start | bytes 393224 | tf_op jit(solution)/shard_map/ppermute | solution.py:339
  92.6 6.8 %collective-permute-start.11 = (bf16[512,128]{1,0:T(8,128)(2,1)S(1)}, bf16[512,128]{1,0:T(8,128)(2,1)S(1)}, u32[]{:S(2)}, u32[]{:S(2)}) collective-permute-start(bf16[512,128]{1,0:T(8,128)(2,1)S(1)} %get-tuple-element.49), channel_id=1, source_target_pairs={{0,6},{1,7},{2,4},{3,5},{4,2},{5,3},{6,0},{7,1},{8,14},{9,15},{10,... | collective-permute-start | bytes 393224 | tf_op jit(solution)/shard_map/ppermute | solution.py:339

commit v2 on v1

v2 whole, which is shorter than its diff:
```python
import functools

import jax
import jax.numpy as jnp
from jax import lax
from jax.experimental import pallas as pl
from jax.experimental.pallas import tpu as pltpu
from jax.sharding import PartitionSpec as P

HEADS = 16
HD = 128
TILE = 64
ROWS = 128
EPS = 1e-06
SCALE = HD ** (-0.5)
BF = jnp.bfloat16
F32 = jnp.float32
NEG = -jnp.inf
LOG_SCALE = SCALE * 1.4426950408889634


def vmem_spec():
    return pl.BlockSpec(memory_space=pltpu.VMEM)


def smem_spec():
    return pl.BlockSpec(memory_space=pltpu.SMEM)


def hbm_spec():
    return pl.BlockSpec(memory_space=pltpu.HBM)


def any_spec():
    return pl.BlockSpec(memory_space=pl.ANY)


def place(c):
    core = c & 1
    zl = (c >> 1) & 3
    zh = (c >> 3) & 1
    xh = (c >> 4) & 1
    return core, zl, zh, xh


def owned_heads(c, k):
    core, zl, zh, xh = place(c)
    rank = (zl ^ (2 * zh)) ^ k
    par = rank & 1
    base = 2 * core + 8 * (rank >> 1)
    return base + 4 * par, base + 1 + 4 * (1 - par)


def normalize(raw, gain):
    x = raw.astype(F32)
    inverse = lax.rsqrt(jnp.mean(x * x, axis=-1, keepdims=True) + EPS)
    normed = x * inverse
    return normed, inverse, (normed * gain).astype(BF)


def norm_grad(upstream, normed, inverse, gain):
    weighted = upstream * gain
    inner = jnp.mean(weighted * normed, axis=-1, keepdims=True)
    return (inverse * (weighted - normed * inner)).astype(BF)


def dot_nt(a, b):
    return lax.dot_general(a, b, (((1,), (1,)), ((), ())), preferred_element_type=F32)


def dot_nn(a, b):
    return lax.dot_general(a, b, (((1,), (0,)), ((), ())), preferred_element_type=F32)


def dot_tn(a, b):
    return lax.dot_general(a, b, (((0,), (0,)), ((), ())), preferred_element_type=F32)


def pack_kernel(early, c_ref, q, k, v, g, *refs):
    outs, sems = refs[-5:-1], refs[-1]
    c = c_ref[0]
    copies = []
    for step, out in enumerate(outs):
        heads = owned_heads(c, step)
        far = step & 1
        near = 1 - far
        if early:
            tiles = ((k, far), (v, far))
        else:
            tiles = ((q, far), (g, far), (q, near), (g, near), (k, near), (v, near), (k, 2), (v, 2))
        for t, (src, e) in enumerate(tiles):
            row = 0 if e == 2 else e * TILE
            h = heads[min(e, 1)]
            copy = pltpu.make_async_copy(
                src.at[pl.ds(row, TILE), pl.ds(pl.multiple_of(h * HD, HD), HD)],
                out.at[pl.ds(t * TILE, TILE), :],
                sems.at[len(copies)],
            )
            copy.start()
            copies.append(copy)
    for copy in copies:
        copy.wait()


def split_gains(total):
    high = total.astype(BF)
    return high, (total - high.astype(F32)).astype(BF)


def joined_gains(ref):
    at = ref.shape[0] - 64
    return ref[at : at + 32, :].astype(F32) + ref[at + 32 : at + 64, :].astype(F32)


def forward_pack_kernel(f0, f2, f3, f1, out, sems):
    copies = []
    for k, src in enumerate((f0, f2, f1, f3)):
        copy = pltpu.make_async_copy(src, out.at[pl.ds(2 * k * TILE, 2 * TILE), :], sems.at[k])
        copy.start()
        copies.append(copy)
    for copy in copies:
        copy.wait()


def home_kernel(half, c_ref, q, k, v, g, q_gain, k_gain, *refs):
    refs = refs[3 * half :]
    outs, part_k, part_v, gains = refs[:3], refs[3], refs[4], refs[5]
    loads, stores, dk_all, dv_all, in_sems, out_sems = refs[6:]
    c = c_ref[0]
    core = c & 1
    count = HEADS // 2
    group = 4
    first = half * count
    for n in range(count // group):
        cols = pl.ds((first + n * group) * HD, group * HD)
        for i, src in enumerate((q, k, v, g)):
            pltpu.make_async_copy(
                src.at[:, cols], loads.at[i, :, pl.ds(n * group * HD, group * HD)], in_sems.at[n, i]
            ).start()
    row = lax.broadcasted_iota(jnp.int32, (ROWS, ROWS), 0)
    col = lax.broadcasted_iota(jnp.int32, (ROWS, ROWS), 1)
    causal = col <= row
    tile_of_row = lax.broadcasted_iota(jnp.int32, (ROWS, 1), 0) // TILE
    copies = []
    for n in range(count // group):
        cols = pl.ds((first + n * group) * HD, group * HD)
        here = pl.ds(n * group * HD, group * HD)
        for i, src in enumerate((q, k, v, g)):
            pltpu.make_async_copy(src.at[:, cols], loads.at[i, :, here], in_sems.at[n, i]).wait()
        locs = [n * group + i for i in range(group)]
        spans = [slice(l * HD, (l + 1) * HD) for l in locs]
        qg = [q_gain[first + l : first + l + 1, :] for l in locs]
        kg = [k_gain[first + l : first + l + 1, :] for l in locs]
        qs = [normalize(loads[0, :, sp], x) for sp, x in zip(spans, qg)]
        ks = [normalize(loads[1, :, sp], x) for sp, x in zip(spans, kg)]
        vb = [loads[2, :, sp] for sp in spans]
        gb = [loads[3, :, sp] for sp in spans]
        s = [jnp.where(causal, dot_nt(x[2], y[2]), NEG) for x, y in zip(qs, ks)]
        dp = [dot_nt(x, y) for x, y in zip(gb, vb)]
        top = [jnp.max(x, axis=1, keepdims=True) for x in s]
        p = [jnp.exp2((x - t) * LOG_SCALE) for x, t in zip(s, top)]
        total = [jnp.sum(x, axis=1, keepdims=True) for x in p]
        keep = []
        for l in locs:
            kind = (first + l) % 4
            owned = (tile_of_row == (kind & 1)) & (core == (kind >> 1))
            keep.append(jnp.where(owned, 0.0, 1.0))
        p = [x * (z / t) for x, z, t in zip(p, keep, total)]
        w = [x.astype(BF) for x in p]
        rd = [jnp.sum(x.astype(F32) * y, axis=1, keepdims=True) for x, y in zip(w, dp)]
        ds = [(x * (y - z)).astype(BF) for x, y, z in zip(p, dp, rd)]
        dq = [dot_nn(x, y[2]) * SCALE for x, y in zip(ds, ks)]
        dk = [dot_tn(x, y[2]) * SCALE for x, y in zip(ds, qs)]
        dv = [dot_tn(x, y) for x, y in zip(w, gb)]
        for i, (l, sp) in enumerate(zip(locs, spans)):
            stores[0, :, sp] = norm_grad(dq[i], qs[i][0], qs[i][1], qg[i])
            stores[1, :, sp] = norm_grad(dk[i], ks[i][0], ks[i][1], kg[i])
            stores[2, :, sp] = dv[i].astype(BF)
            dk_all[l] = dk[i]
            dv_all[l] = dv[i]
            gains[l : l + 1, :] = jnp.sum(dq[i] * qs[i][0], axis=0, keepdims=True)
            gains[count + l : count + l + 1, :] = jnp.sum(dk[i] * ks[i][0], axis=0, keepdims=True)
        for i, dst in enumerate(outs):
            copy = pltpu.make_async_copy(stores.at[i, :, here], dst.at[:, cols], out_sems.at[n, i])
            copy.start()
            copies.append(copy)
    for j in range(2):
        h0 = 2 * core + 4 * j
        h1 = 2 * core + 1 + 4 * (1 - j)
        for i, (h, e) in enumerate(((h0, 0), (h1, 1), (h1, 0))):
            rows = slice(e * TILE, (e + 1) * TILE)
            part_k[3 * j + i] = dk_all[h, rows, :]
            part_v[3 * j + i] = dv_all[h, rows, :]
    for copy in copies:
        copy.wait()


def owner_kernel(
    c_ref, f0, f2, f3, f1, r0, r2, r3, r1, b1, b2, b3, q_gain, k_gain, low_gains, high_gains,
    x0, x1, x2, x3, t1, t2, t3, far_k, far_v, gains_out, gains,
):
    c = c_ref[0]
    core, zl, zh, xh = place(c)
    heads = owned_heads(c, 0)
    early = (f0, f1, f2, f3)
    late = (r0, r1, r2, r3)
    crossed = (b1, b2, b3)
    returned = (x0, x1, x2, x3)
    terms = (t1, t2, t3)
    live = (xh == 1, zh == 1, xh == 1)
    half = HEADS // 2
    for at, src in ((0, low_gains), (half, high_gains)):
        gains[at : at + half, :] = src[0:half, :]
        gains[HEADS + at : HEADS + at + half, :] = src[half:, :]
    row = lax.broadcasted_iota(jnp.int32, (TILE, 4 * TILE), 0)
    col = lax.broadcasted_iota(jnp.int32, (TILE, 4 * TILE), 1)
    block = col >> 6
    lower = (col & (TILE - 1)) <= row
    far_block = lax.broadcasted_iota(jnp.int32, (1, 6 * TILE), 1) >> 7
    bias = [jnp.where(x, 0.0, NEG) for x in live]
    far_bias = jnp.where(far_block == 0, bias[0], jnp.where(far_block == 1, bias[1], bias[2]))

    def rows_of(ref, tile):
        return ref[tile * TILE : (tile + 1) * TILE, :]

    both = (0, 1)
    order = ((0, 2, 1, 3), (1, 3, 0, 2))
    qg = [q_gain[pl.ds(h, 1), :] for h in heads]
    kg = [k_gain[pl.ds(h, 1), :] for h in heads]


    def stack(e, t):
        parts = []
        for a, i in enumerate(order[e]):
            if a < 2:
                parts.append(rows_of(late[i], t) if t < 2 else rows_of(early[i], t - 2))
            else:
                parts.append(rows_of(late[i], 2 + t))
        return jnp.concatenate(parts, axis=0)

    qs = [normalize(stack(e, 0), qg[e]) for e in both]
    gb = [stack(e, 1) for e in both]
    ks = [normalize(stack(e, 2), kg[e]) for e in both]
    vb = [stack(e, 3) for e in both]
    cross = lambda e, t: jnp.concatenate(
        [rows_of(b, 4 * e + t + 2 * i) for b in crossed for i in range(2)], axis=0
    )
    kf = [normalize(cross(e, 0), kg[e]) for e in both]
    vf = [cross(e, 1) for e in both]
    kx = normalize(jnp.concatenate([rows_of(late[i], 6) for i in order[1]], axis=0), kg[1])
    vx = jnp.concatenate([rows_of(late[i], 7) for i in order[1]], axis=0)
    far = slice(0, 2 * TILE)
    tiles = [slice(i * TILE, (i + 1) * TILE) for i in range(4)]

    s_own = [dot_nt(qs[e][2], ks[e][2]) for e in both]
    s_far = [dot_nt(qs[e][2][far], kf[e][2]) + far_bias for e in both]
    s_x = jnp.concatenate([dot_nt(qs[1][2][t], kx[2][t]) for t in tiles], axis=0)
    d_own = [dot_nt(gb[e], vb[e]) for e in both]
    d_far = [dot_nt(gb[e][far], vf[e]) for e in both]
    d_x = jnp.concatenate([dot_nt(gb[1][t], vx[t]) for t in tiles], axis=0)
    count = []
    for e in both:
        rows = []
        for a in range(4):
            value = jnp.zeros((TILE, 4 * TILE), F32)
            for b in range(4):
                if a == b:
                    here = jnp.where(lower, 3.0 if a < 2 else 2.0, 0.0)
                else:
                    earlier = (zl ^ order[e][b]) < (zl ^ order[e][a])
                    here = jnp.where(earlier, 2.0 if a < 2 and b < 2 else 1.0, 0.0)
                value = jnp.where(block == b, here, value)
            rows.append(value)
        count.append(jnp.concatenate(rows, axis=0))
    s_own = [jnp.where(count[e] > 0.0, s_own[e], NEG) for e in both]
    peak = lambda x: jnp.max(x, axis=1, keepdims=True)
    add = lambda x: jnp.sum(x, axis=1, keepdims=True)
    top = [peak(x) for x in s_own]
    top[1] = jnp.maximum(top[1], peak(s_x))
    top_far = [jnp.maximum(top[e][far], peak(s_far[e])) for e in both]
    top = [jnp.concatenate([top_far[e], top[e][2 * TILE :]], axis=0) for e in both]
    p_own = [count[e] * jnp.exp2((s_own[e] - top[e]) * LOG_SCALE) for e in both]
    p_far = [jnp.exp2((s_far[e] - top_far[e]) * LOG_SCALE) for e in both]
    p_x = jnp.exp2((s_x - top[1]) * LOG_SCALE)
    total = [add(x) for x in p_own]
    total[1] = total[1] + add(p_x)
    total_far = [add(x) for x in p_far]
    total = [
        jnp.concatenate([total[e][far] + total_far[e], total[e][2 * TILE :]], axis=0) for e in both
    ]
    scale = [1.0 / x for x in total]
    p_own = [p_own[e] * scale[e] for e in both]
    p_far = [p_far[e] * scale[e][far] for e in both]
    p_x = p_x * scale[1]
    w_own = [x.astype(BF) for x in p_own]
    w_far = [x.astype(BF) for x in p_far]
    w_x = p_x.astype(BF)
    rd = [add(w_own[e].astype(F32) * d_own[e]) for e in both]
    rd[1] = rd[1] + add(w_x.astype(F32) * d_x)
    rd_far = [add(w_far[e].astype(F32) * d_far[e]) for e in both]
    rd = [jnp.concatenate([rd[e][far] + rd_far[e], rd[e][2 * TILE :]], axis=0) for e in both]
    ds_far = [(p_far[e] * (d_far[e] - rd[e][far])).astype(BF) for e in both]
    ds_own = [(p_own[e] * (d_own[e] - rd[e])).astype(BF) for e in both]
    ds_x = (p_x * (d_x - rd[1])).astype(BF)

    dk_far = [dot_tn(ds_far[e], qs[e][2][far]) * SCALE for e in both]
    dv_far = [dot_tn(w_far[e], gb[e][far]) for e in both]
    for e in both:
        for m in range(3):
            rows = slice(m * 128, (m + 1) * 128)
            terms[m][256 * e : 256 * e + 128, :] = dk_far[e][rows].astype(BF)
            terms[m][256 * e + 128 : 256 * e + 256, :] = dv_far[e][rows].astype(BF)
    dq = [dot_nn(ds_own[e], ks[e][2]) for e in both]
    dq_far = [dot_nn(ds_far[e], kf[e][2]) for e in both]
    dq_x = jnp.concatenate([dot_nn(ds_x[t], kx[2][t]) for t in tiles], axis=0)
    dq[1] = dq[1] + dq_x
    dq = [
        jnp.concatenate([dq[e][far] + dq_far[e], dq[e][2 * TILE :]], axis=0) * SCALE for e in both
    ]
    dk = [dot_tn(ds_own[e], qs[e][2]) * SCALE for e in both]
    dv = [dot_tn(w_own[e], gb[e]) for e in both]
    dk_x = [dot_tn(ds_x[t], qs[1][2][t]) * SCALE for t in tiles]
    dv_x = [dot_tn(w_x[t], gb[1][t]) for t in tiles]
    gq = [norm_grad(dq[e], qs[e][0], qs[e][1], qg[e]) for e in both]
    down = lambda x: jnp.sum(x, axis=0, keepdims=True)
    for e in both:
        for a, i in enumerate(order[e]):
            out = returned[i]
            if a < 2:
                out[0:TILE, :] = gq[e][tiles[a]]
                far_k[i] = dk[e][tiles[a]]
                far_v[i] = dv[e][tiles[a]]
            else:
                out[TILE : 2 * TILE, :] = gq[e][tiles[a]]
                out[2 * TILE : 3 * TILE, :] = dk[e][tiles[a]].astype(BF)
                out[3 * TILE : 4 * TILE, :] = dv[e][tiles[a]].astype(BF)
            if e == 1:
                out[4 * TILE : 5 * TILE, :] = dk_x[a].astype(BF)
                out[5 * TILE : 6 * TILE, :] = dv_x[a].astype(BF)
        key_sum = down(dk[e] * ks[e][0]) + down(dk_far[e] * kf[e][0])
        if e == 1:
            key_sum += sum(down(dk_x[a] * kx[0][tiles[a]]) for a in range(4))
        gains[pl.ds(heads[e], 1), :] += down(dq[e] * qs[e][0])
        gains[pl.ds(HEADS + heads[e], 1), :] += key_sum
    high, low = split_gains(gains[...])
    for out in (*terms, gains_out):
        at = out.shape[0] - 64
        out[at : at + 32, :] = high
        out[at + 32 :, :] = low


def return_pack_kernel(far_k, far_v, own, u1, u2, u3, y0, y1, y2, y3):
    total = (joined_gains(own) + joined_gains(u2)) + (joined_gains(u1) + joined_gains(u3))
    high, low = split_gains(total)
    for i, y in enumerate((y0, y1, y2, y3)):
        at = 256 * (i & 1) + 64 * (i >> 1)
        dk = far_k[i]
        dv = far_v[i]
        for u in (u1, u2, u3):
            dk += u[at : at + TILE, :].astype(F32)
            dv += u[at + 128 : at + 128 + TILE, :].astype(F32)
        y[0:TILE, :] = dk.astype(BF)
        y[TILE : 2 * TILE, :] = dv.astype(BF)
        y[2 * TILE : 2 * TILE + 32, :] = high
        y[2 * TILE + 32 :, :] = low


def gains_kernel(y0, y2, y3, y1, out):
    out[...] = (joined_gains(y0) + joined_gains(y1)) + (joined_gains(y2) + joined_gains(y3))


def final_kernel(
    c_ref, z0, z2, z3, z1, y0, y2, y3, y1, f0, f1, f2, f3, m0, m1, m2, m3,
    low_k, low_v, high_k, high_v, k_gain, gq_in, gk_in, gv_in,
    gq_out, gk_out, gv_out, done_k, done_v, sems,
):
    c = c_ref[0]
    core, zl, zh, xh = place(c)
    rank = zl ^ (2 * zh)
    copies = []

    def send(src, dst, e, h, n):
        copy = pltpu.make_async_copy(
            src, dst.at[pl.ds(e * TILE, TILE), pl.ds(pl.multiple_of(h * HD, HD), HD)], sems.at[n]
        )
        copy.start()
        copies.append(copy)

    def tile_of(ref, t):
        return ref[t * TILE : (t + 1) * TILE, :]

    jobs = []
    for step in range(4):
        heads = owned_heads(c, step)
        far = step & 1
        near = 1 - far
        y = (y0, y1, y2, y3)[step]
        z = (z0, z1, z2, z3)[step]
        f = (f0, f1, f2, f3)[step]
        m = (m0, m1, m2, m3)[step]
        send(y.at[pl.ds(0, TILE), :], gq_out, far, heads[far], 8 * step)
        send(y.at[pl.ds(TILE, TILE), :], gq_out, near, heads[near], 8 * step + 1)
        owner = rank ^ step
        for i, (h, e, back, at, raw) in enumerate((
            (heads[far], far, z, 0, tile_of(f, 0)),
            (heads[near], near, y, 2, tile_of(m, 4)),
            (heads[1], 0, y, 4, tile_of(m, 6)),
        )):
            part = 3 * (owner & 1) + (far, near, 2)[i]
            jobs.append((3 * step + i, 8 * step + 2 + 2 * i, part, owner < 2, h, e, back, at, raw))
    for n, sem, part, is_low, h, e, back, at, raw in jobs:
        dv = jnp.where(is_low, low_v[part], high_v[part])
        done_v[n] = (dv + tile_of(back, at + 1).astype(F32)).astype(BF)
        send(done_v.at[n], gv_out, e, h, sem + 1)
    kg = [k_gain[pl.ds(job[4], 1), :] for job in jobs]
    ks = [normalize(job[8], x) for job, x in zip(jobs, kg)]
    dk = [
        jnp.where(is_low, low_k[part], high_k[part]) + tile_of(back, at).astype(F32)
        for n, sem, part, is_low, h, e, back, at, raw in jobs
    ]
    done = [norm_grad(x, y[0], y[1], z) for x, y, z in zip(dk, ks, kg)]
    for (n, sem, part, is_low, h, e, back, at, raw), x in zip(jobs, done):
        done_k[n] = x
        send(done_k.at[n], gk_out, e, h, sem)
    for copy in copies:
        copy.wait()


def per_device(q_raw, k_raw, values, d_out, q_gain, k_gain):
    ctx_count = lax.axis_size("ctx")
    dp_count = lax.axis_size("dp")
    here = lax.axis_index("ctx").astype(jnp.int32).reshape(1)
    flat = lambda a: a.reshape(ROWS, HEADS * HD)
    q, k, v, g = (
        pltpu.with_memory_space_constraint(flat(a), pltpu.HBM) for a in (q_raw, k_raw, values, d_out)
    )
    qg = q_gain.reshape(HEADS, HD)
    kg = k_gain.reshape(HEADS, HD)
    params = pltpu.CompilerParams(vmem_limit_bytes=48 * 1024 * 1024)
    shape = jax.ShapeDtypeStruct

    def swap(block, axis, mask):
        count = ctx_count if axis == "ctx" else dp_count
        return lax.ppermute(block, axis, [(i, i ^ mask) for i in range(count)])

    steps = (16, 12, 28)

    def by_distance(blocks):
        return [blocks[i] for i in (0, 2, 3, 1)]

    def around(blocks):
        moved = {i: swap(blocks[i], "ctx", 2 * i) for i in (2, 3, 1)}
        return [blocks[0], moved[1], moved[2], moved[3]]

    def pack_call(early, *after):
        count = 2 if early else 8
        return pl.pallas_call(
            functools.partial(pack_kernel, early),
            in_specs=[smem_spec()] + [hbm_spec()] * 4 + [any_spec()] * len(after),
            out_specs=[any_spec()] * 4,
            out_shape=[shape((count * TILE, HD), BF)] * 4,
            scratch_shapes=[pltpu.SemaphoreType.DMA((4 * count,))],
            compiler_params=params,
            name="pack_early" if early else "pack_late",
        )(here, q, k, v, g, *after)

    packed_early = pack_call(True)
    early = around(packed_early)
    packed_late = pack_call(False, early[1])
    late = around(packed_late)

    def home_call(half, earlier):
        return pl.pallas_call(
            functools.partial(home_kernel, half),
            in_specs=[smem_spec()] + [hbm_spec()] * 4 + [vmem_spec()] * 2 + [hbm_spec()] * len(earlier),
            out_specs=[hbm_spec()] * 3 + [vmem_spec()] * 3,
            out_shape=[shape((ROWS, HEADS * HD), BF)] * 3
            + [shape((6, TILE, HD), F32)] * 2
            + [shape((HEADS, HD), F32)],
            scratch_shapes=[
                pltpu.VMEM((4, ROWS, HEADS * HD // 2), BF),
                pltpu.VMEM((3, ROWS, HEADS * HD // 2), BF),
                pltpu.VMEM((HEADS // 2, ROWS, HD), F32),
                pltpu.VMEM((HEADS // 2, ROWS, HD), F32),
                pltpu.SemaphoreType.DMA((2, 4)),
                pltpu.SemaphoreType.DMA((2, 3)),
            ],
            input_output_aliases={7 + i: i for i in range(len(earlier))},
            compiler_params=params,
            name="home_slab_high" if half else "home_slab_low",
        )(here, q, k, v, g, qg, kg, *earlier)

    low = home_call(0, ())
    high = home_call(1, low[:3])

    onward = pl.pallas_call(
        forward_pack_kernel,
        in_specs=[any_spec()] * 4,
        out_specs=any_spec(),
        out_shape=shape((8 * TILE, HD), BF),
        scratch_shapes=[pltpu.SemaphoreType.DMA((4,))],
        compiler_params=params,
        name="pack_far_rows",
    )(*by_distance(early))
    moved = {mask: swap(onward, "ctx", mask) for mask in (16, 12, 28)}
    crossed = [moved[mask] for mask in steps]

    outs = pl.pallas_call(
        owner_kernel,
        in_specs=[smem_spec()] + [vmem_spec()] * 15,
        out_specs=[vmem_spec()] * 10,
        out_shape=[shape((6 * TILE, HD), BF)] * 4
        + [shape((9 * TILE, HD), BF)] * 3
        + [shape((4, TILE, HD), F32)] * 2
        + [shape((TILE, HD), BF)],
        scratch_shapes=[pltpu.VMEM((2 * HEADS, HD), F32)],
        compiler_params=params,
        name="owned_heads",
    )(here, *by_distance(early), *by_distance(late), *crossed, qg, kg, low[5], high[5])
    back_early, terms, far_k, far_v, own_gains = outs[:4], outs[4:7], outs[7], outs[8], outs[9]
    moved = {mask: swap(terms[steps.index(mask)], "ctx", mask) for mask in (28, 12, 16)}
    terms_in = [moved[mask] for mask in steps]

    def pair_sum(x, axis, mask):
        return x + swap(x, axis, mask)

    def quad_sum(x, axis, mask):
        one, two, three = (swap(x, axis, i * mask) for i in (1, 2, 3))
        return (x + one) + (two + three)

    back_late = pl.pallas_call(
        return_pack_kernel,
        in_specs=[vmem_spec()] * 6,
        out_specs=[vmem_spec()] * 4,
        out_shape=[shape((3 * TILE, HD), BF)] * 4,
        compiler_params=params,
        name="add_far_terms",
    )(far_k, far_v, own_gains, *terms_in[::-1])
    home_early = around(back_early)
    home_late = around(back_late)

    gains = pl.pallas_call(
        gains_kernel,
        in_specs=[vmem_spec()] * 4,
        out_specs=vmem_spec(),
        out_shape=shape((2 * HEADS, HD), F32),
        compiler_params=params,
        name="sum_gains",
    )(*by_distance(home_late))
    gains = quad_sum(gains, "dp", 1)
    gains = pair_sum(gains, "dp", 4)
    gains = pair_sum(gains, "ctx", 1)

    gq, gk, gv = pl.pallas_call(
        final_kernel,
        in_specs=[smem_spec()] + [vmem_spec()] * 21 + [any_spec()] * 3,
        out_specs=[any_spec()] * 3,
        out_shape=[shape((ROWS, HEADS * HD), BF)] * 3,
        scratch_shapes=[pltpu.VMEM((12, TILE, HD), BF)] * 2 + [pltpu.SemaphoreType.DMA((32,))],
        input_output_aliases={22: 0, 23: 1, 24: 2},
        compiler_params=params,
        name="finish_rows",
    )(
        here, *by_distance(home_late), *by_distance(home_early), *packed_early, *packed_late,
        low[3], low[4], high[3], high[4], kg, *high[:3],
    )
    whole = lambda a: a.reshape(1, ROWS, HEADS * HD)
    return (
        whole(gq),
        whole(gk),
        whole(gv),
        gains[:HEADS].reshape(HEADS * HD),
        gains[HEADS:].reshape(HEADS * HD),
    )


def solution(mesh):
    rows = P("dp", "ctx", None)
    return jax.shard_map(
        per_device,
        mesh=mesh,
        in_specs=(rows, rows, rows, rows, P(), P()),
        out_specs=(rows, rows, rows, P(), P()),
        check_vma=False,
    )
```

time: 103 us -> 78.1 us (0.76)
  the two profiles are of different devices: /device:TPU:4 before, /device:TPU:1 now
where the time goes in v2:
time: 78.1 us; the launch traced here: 77.9 us
  starting transfers between devices  42.8 us (55%)
  waiting for transfers between devices  19.8 us (25%)
  Pallas kernels  13.8 us (18%)
    ppermute x23, starting transfers between devices, swap(): return lax.ppermute(block, axis, [(i, i ^ mask) for i in range(count)])  42.8 us
    ppermute x23, waiting for transfers between devices, swap(): return lax.ppermute(block, axis, [(i, i ^ mask) for i in range(count)])  19.8 us
    pallas_call x2, Pallas kernels, home_call(): pl.pallas_call(functools.partial(home_kernel, half), in_specs=[smem_spec(...  7.92 us
    pallas_call x2, Pallas kernels, pack_call(): pl.pallas_call(functools.partial(pack_kernel, early), in_specs=[smem_spec...  2.2 us
    pallas_call x1, Pallas kernels, per_device(): pl.pallas_call(owner_kernel, in_specs=[smem_spec()] + [vmem_spec()] * 15,...  2.12 us
  transfers between devices with their start and end apart: 23, of which 10 were waited for; matrix products, arithmetic and copies ran while one was open for 0% of the time, Pallas kernels for 13%

profile of v2, /device:TPU:1, one launch (start us, length us, event | category | flops | bytes accessed | tf_op | source)
XLA Modules:
  0.0 77.9 jit_solution(7997296244451627650)
XLA Ops:
  0.6 0.9 %pack_early.1 = (bf16[128,128]{1,0:T(8,128)(2,1)S(1)}, bf16[128,128]{1,0:T(8,128)(2,1)S(1)}, bf16[128,128]{1,0:T(8,128)(2,1)S(1)}, bf16[128,128]{1,0:T(8,128)(2,1)S(1)}) custom-call(s32[1]{0:T(128)} %bitcast.c_ref, bf16[128,2048]{1,0:T(8,128)(2,1)} %bitcast.21, bf16[128,2048]{1,0:T(8,128)(2,1)} %bitcast.25, bf16[128,2048]{1,0:T(8,128)(2,1)} %bitcast.29, ...), custom_call_target="tpu_custom_call" | custom-call | tf_op jit(solution)/shard_map/pack_early/pallas_call | solution.py:457
  1.6 2.6 %collective-permute-start.2 = (bf16[128,128]{1,0:T(8,128)(2,1)S(1)}, bf16[128,128]{1,0:T(8,128)(2,1)S(1)}, u32[]{:S(2)}, u32[]{:S(2)}) collective-permute-start(bf16[128,128]{1,0:T(8,128)(2,1)S(1)} %get-tuple-element.45.f1), channel_id=1, source_target_pairs={{0,2},{1,3},{2,0},{3,1},{4,6},{5,7},{6,4},{7,5},{8,10},{9,11},{10,... | collective-permute-start | bytes 98312 | tf_op jit(solution)/shard_map/ppermute | solution.py:444
  4.1 3.0 %collective-permute-start = (bf16[128,128]{1,0:T(8,128)(2,1)S(1)}, bf16[128,128]{1,0:T(8,128)(2,1)S(1)}, u32[]{:S(2)}, u32[]{:S(2)}) collective-permute-start(bf16[128,128]{1,0:T(8,128)(2,1)S(1)} %get-tuple-element.43.f2), channel_id=1, source_target_pairs={{0,4},{1,5},{2,6},{3,7},{4,0},{5,1},{6,2},{7,3},{8,12},{9,13},{10,... | collective-permute-start | bytes 98312 | tf_op jit(solution)/shard_map/ppermute | solution.py:444
  7.1 1.6 %collective-permute-done.f2 = bf16[128,128]{1,0:T(8,128)(2,1)S(1)} collective-permute-done((bf16[128,128]{1,0:T(8,128)(2,1)S(1)}, bf16[128,128]{1,0:T(8,128)(2,1)S(1)}, u32[]{:S(2)}, u32[]{:S(2)}) %collective-permute-start) | collective-permute-done | bytes 32800 | tf_op jit(solution)/shard_map/ppermute | solution.py:444
  8.8 2.9 %collective-permute-done.1.f3 = bf16[128,128]{1,0:T(8,128)(2,1)S(1)} collective-permute-done((bf16[128,128]{1,0:T(8,128)(2,1)S(1)}, bf16[128,128]{1,0:T(8,128)(2,1)S(1)}, u32[]{:S(2)}, u32[]{:S(2)}) %collective-permute-start.1) | collective-permute-done | bytes 32800 | tf_op jit(solution)/shard_map/ppermute | solution.py:444
  11.9 2.8 %collective-permute-start.6 = (bf16[512,128]{1,0:T(8,128)(2,1)S(1)}, bf16[512,128]{1,0:T(8,128)(2,1)S(1)}, u32[]{:S(2)}, u32[]{:S(2)}) collective-permute-start(bf16[512,128]{1,0:T(8,128)(2,1)S(1)} %pack_far_rows.1), channel_id=1, source_target_pairs={{0,16},{1,17},{2,18},{3,19},{4,20},{5,21},{6,22},{7,23},{8,24},{9,... | collective-permute-start | bytes 393224 | tf_op jit(solution)/shard_map/ppermute | solution.py:444
  14.7 1.7 %collective-permute-start.7 = (bf16[512,128]{1,0:T(8,128)(2,1)S(1)}, bf16[512,128]{1,0:T(8,128)(2,1)S(1)}, u32[]{:S(2)}, u32[]{:S(2)}) collective-permute-start(bf16[512,128]{1,0:T(8,128)(2,1)S(1)} %pack_far_rows.1), channel_id=1, source_target_pairs={{0,12},{1,13},{2,14},{3,15},{4,8},{5,9},{6,10},{7,11},{8,4},{9,5},... | collective-permute-start | bytes 393224 | tf_op jit(solution)/shard_map/ppermute | solution.py:444
  16.4 1.8 %collective-permute-start.8 = (bf16[512,128]{1,0:T(8,128)(2,1)S(1)}, bf16[512,128]{1,0:T(8,128)(2,1)S(1)}, u32[]{:S(2)}, u32[]{:S(2)}) collective-permute-start(bf16[512,128]{1,0:T(8,128)(2,1)S(1)} %pack_far_rows.1), channel_id=1, source_target_pairs={{0,28},{1,29},{2,30},{3,31},{4,24},{5,25},{6,26},{7,27},{8,20},{9,... | collective-permute-start | bytes 393224 | tf_op jit(solution)/shard_map/ppermute | solution.py:444
  18.2 1.3 %pack_late.1 = (bf16[512,128]{1,0:T(8,128)(2,1)S(1)}, bf16[512,128]{1,0:T(8,128)(2,1)S(1)}, bf16[512,128]{1,0:T(8,128)(2,1)S(1)}, bf16[512,128]{1,0:T(8,128)(2,1)S(1)}) custom-call(s32[1]{0:T(128)} %bitcast.c_ref, bf16[128,2048]{1,0:T(8,128)(2,1)} %bitcast.22, bf16[128,2048]{1,0:T(8,128)(2,1)} %bitcast.26, bf16[128,2048]{1,0:T(8,128)(2,1)} %bitcast.30, ...), custom_call_target="tpu_custom_call" | custom-call | tf_op jit(solution)/shard_map/pack_late/pallas_call | solution.py:457
  19.5 1.2 %collective-permute-start.3 = (bf16[512,128]{1,0:T(8,128)(2,1)S(1)}, bf16[512,128]{1,0:T(8,128)(2,1)S(1)}, u32[]{:S(2)}, u32[]{:S(2)}) collective-permute-start(bf16[512,128]{1,0:T(8,128)(2,1)S(1)} %get-tuple-element.47.m2), channel_id=1, source_target_pairs={{0,4},{1,5},{2,6},{3,7},{4,0},{5,1},{6,2},{7,3},{8,12},{9,13},{10,... | collective-permute-start | bytes 393224 | tf_op jit(solution)/shard_map/ppermute | solution.py:444
  20.7 1.6 %collective-permute-start.4 = (bf16[512,128]{1,0:T(8,128)(2,1)S(1)}, bf16[512,128]{1,0:T(8,128)(2,1)S(1)}, u32[]{:S(2)}, u32[]{:S(2)}) collective-permute-start(bf16[512,128]{1,0:T(8,128)(2,1)S(1)} %get-tuple-element.48.m3), channel_id=1, source_target_pairs={{0,6},{1,7},{2,4},{3,5},{4,2},{5,3},{6,0},{7,1},{8,14},{9,15},{10,... | collective-permute-start | bytes 393224 | tf_op jit(solution)/shard_map/ppermute | solution.py:444
  22.4 4.0 %home_slab_low.1 = (bf16[128,2048]{1,0:T(8,128)(2,1)}, bf16[128,2048]{1,0:T(8,128)(2,1)}, bf16[128,2048]{1,0:T(8,128)(2,1)}, f32[6,64,128]{2,1,0:T(8,128)S(1)}, ...) custom-call(s32[1]{0:T(128)} %bitcast.c_ref, bf16[128,2048]{1,0:T(8,128)(2,1)} %bitcast.23, bf16[128,2048]{1,0:T(8,128)(2,1)} %bitcast.27, ...), custom_call_target="tpu_custom_call" | custom-call | tf_op jit(solution)/shard_map/home_slab_low/pallas_call | solution.py:473
  26.3 4.0 %home_slab_high.1 = (bf16[128,2048]{1,0:T(8,128)(2,1)}, bf16[128,2048]{1,0:T(8,128)(2,1)}, bf16[128,2048]{1,0:T(8,128)(2,1)}, f32[6,64,128]{2,1,0:T(8,128)S(1)},...) custom-call(s32[1]{0:T(128)} %bitcast.c_ref, ...), custom_call_target="tpu_custom_call", output_to_operand_aliasing={{0}: (7, {}), {1}: (8, {}), {2}: (9, {})} | custom-call | tf_op jit(solution)/shard_map/home_slab_high/pallas_call | solution.py:473
  30.9 1.0 %collective-permute-done.5.r1 = bf16[512,128]{1,0:T(8,128)(2,1)S(1)} collective-permute-done((bf16[512,128]{1,0:T(8,128)(2,1)S(1)}, bf16[512,128]{1,0:T(8,128)(2,1)S(1)}, u32[]{:S(2)}, u32[]{:S(2)}) %collective-permute-start.5) | collective-permute-done | bytes 131104 | tf_op jit(solution)/shard_map/ppermute | solution.py:444
  31.9 2.1 %owned_heads.1 = (bf16[384,128]{1,0:T(8,128)(2,1)S(1)}, bf16[384,128]{1,0:T(8,128)(2,1)S(1)}, bf16[384,128]{1,0:T(8,128)(2,1)S(1)}, bf16[384,128]{1,0:T(8,128)(2...) custom-call(s32[1]{0:T(128)} %bitcast.c_ref, ...), custom_call_target="tpu_custom_call" | custom-call | tf_op jit(solution)/shard_map/owned_heads/pallas_call | solution.py:508
  34.0 2.9 %collective-permute-start.10 = (bf16[576,128]{1,0:T(8,128)(2,1)S(1)}, bf16[576,128]{1,0:T(8,128)(2,1)S(1)}, u32[]{:S(2)}, u32[]{:S(2)}) collective-permute-start(bf16[576,128]{1,0:T(8,128)(2,1)S(1)} %get-tuple-element.59), channel_id=1, source_target_pairs={{0,12},{1,13},{2,14},{3,15},{4,8},{5,9},{6,10},{7,11},{8,4},{9,5},... | collective-permute-start | bytes 442376 | tf_op jit(solution)/shard_map/ppermute | solution.py:444
  37.0 2.5 %collective-permute-start.11 = (bf16[576,128]{1,0:T(8,128)(2,1)S(1)}, bf16[576,128]{1,0:T(8,128)(2,1)S(1)}, u32[]{:S(2)}, u32[]{:S(2)}) collective-permute-start(bf16[576,128]{1,0:T(8,128)(2,1)S(1)} %get-tuple-element.60), channel_id=1, source_target_pairs={{0,16},{1,17},{2,18},{3,19},{4,20},{5,21},{6,22},{7,23},{8,24},{9,... | collective-permute-start | bytes 442376 | tf_op jit(solution)/shard_map/ppermute | solution.py:444
  39.5 0.9 %collective-permute-start.9 = (bf16[576,128]{1,0:T(8,128)(2,1)S(1)}, bf16[576,128]{1,0:T(8,128)(2,1)S(1)}, u32[]{:S(2)}, u32[]{:S(2)}) collective-permute-start(bf16[576,128]{1,0:T(8,128)(2,1)S(1)} %get-tuple-element.58), channel_id=1, source_target_pairs={{0,28},{1,29},{2,30},{3,31},{4,24},{5,25},{6,26},{7,27},{8,20},{9,... | collective-permute-start | bytes 442376 | tf_op jit(solution)/shard_map/ppermute | solution.py:444
  40.4 2.1 %collective-permute-done.11.u3 = bf16[576,128]{1,0:T(8,128)(2,1)S(1)} collective-permute-done((bf16[576,128]{1,0:T(8,128)(2,1)S(1)}, bf16[576,128]{1,0:T(8,128)(2,1)S(1)}, u32[]{:S(2)}, u32[]{:S(2)}) %collective-permute-start.11) | collective-permute-done | bytes 147488 | tf_op jit(solution)/shard_map/ppermute | solution.py:444
  42.4 5.5 %collective-permute-done.9.u1 = bf16[576,128]{1,0:T(8,128)(2,1)S(1)} collective-permute-done((bf16[576,128]{1,0:T(8,128)(2,1)S(1)}, bf16[576,128]{1,0:T(8,128)(2,1)S(1)}, u32[]{:S(2)}, u32[]{:S(2)}) %collective-permute-start.9) | collective-permute-done | bytes 147488 | tf_op jit(solution)/shard_map/ppermute | solution.py:444
  48.1 6.5 %collective-permute-start.12 = (bf16[192,128]{1,0:T(8,128)(2,1)S(1)}, bf16[192,128]{1,0:T(8,128)(2,1)S(1)}, u32[]{:S(2)}, u32[]{:S(2)}) collective-permute-start(bf16[192,128]{1,0:T(8,128)(2,1)S(1)} %get-tuple-element.62), channel_id=1, source_target_pairs={{0,4},{1,5},{2,6},{3,7},{4,0},{5,1},{6,2},{7,3},{8,12},{9,13},{10,... | collective-permute-start | bytes 147464 | tf_op jit(solution)/shard_map/ppermute | solution.py:444
  55.0 1.2 %collective-permute-done.12.z2.y2 = bf16[192,128]{1,0:T(8,128)(2,1)S(1)} collective-permute-done((bf16[192,128]{1,0:T(8,128)(2,1)S(1)}, bf16[192,128]{1,0:T(8,128)(2,1)S(1)}, u32[]{:S(2)}, u32[]{:S(2)}) %collective-permute-start.12) | collective-permute-done | bytes 49184 | tf_op jit(solution)/shard_map/ppermute | solution.py:444
  56.2 3.4 %collective-permute-done.13.z3.y3 = bf16[192,128]{1,0:T(8,128)(2,1)S(1)} collective-permute-done((bf16[192,128]{1,0:T(8,128)(2,1)S(1)}, bf16[192,128]{1,0:T(8,128)(2,1)S(1)}, u32[]{:S(2)}, u32[]{:S(2)}) %collective-permute-start.13) | collective-permute-done | bytes 49184 | tf_op jit(solution)/shard_map/ppermute | solution.py:444
  60.1 2.6 %collective-permute-start.19 = (f32[32,128]{1,0:T(8,128)S(1)}, f32[32,128]{1,0:T(8,128)S(1)}, u32[]{:S(2)}, u32[]{:S(2)}) collective-permute-start(f32[32,128]{1,0:T(8,128)S(1)} %sum_gains.1), channel_id=1, source_target_pairs={{0,64},{32,96},{64,0},{96,32},{128,192},{160,224},{192,128},{224,1... | collective-permute-start | bytes 49160 | tf_op jit(solution)/shard_map/ppermute | solution.py:444
  62.7 0.9 %collective-permute-start.20 = (f32[32,128]{1,0:T(8,128)S(1)}, f32[32,128]{1,0:T(8,128)S(1)}, u32[]{:S(2)}, u32[]{:S(2)}) collective-permute-start(f32[32,128]{1,0:T(8,128)S(1)} %sum_gains.1), channel_id=1, source_target_pairs={{0,96},{32,64},{64,32},{96,0},{128,224},{160,192},{192,160},{224,1... | collective-permute-start | bytes 49160 | tf_op jit(solution)/shard_map/ppermute | solution.py:444
  63.6 1.3 %collective-permute-start.15 = (bf16[384,128]{1,0:T(8,128)(2,1)S(1)}, bf16[384,128]{1,0:T(8,128)(2,1)S(1)}, u32[]{:S(2)}, u32[]{:S(2)}) collective-permute-start(bf16[384,128]{1,0:T(8,128)(2,1)S(1)} %get-tuple-element.66), channel_id=1, source_target_pairs={{0,4},{1,5},{2,6},{3,7},{4,0},{5,1},{6,2},{7,3},{8,12},{9,13},{10,... | collective-permute-start | bytes 294920 | tf_op jit(solution)/shard_map/ppermute | solution.py:444
  65.0 1.3 %collective-permute-start.17 = (bf16[384,128]{1,0:T(8,128)(2,1)S(1)}, bf16[384,128]{1,0:T(8,128)(2,1)S(1)}, u32[]{:S(2)}, u32[]{:S(2)}) collective-permute-start(bf16[384,128]{1,0:T(8,128)(2,1)S(1)} %get-tuple-element.68), channel_id=1, source_target_pairs={{0,2},{1,3},{2,0},{3,1},{4,6},{5,7},{6,4},{7,5},{8,10},{9,11},{10,... | collective-permute-start | bytes 294920 | tf_op jit(solution)/shard_map/ppermute | solution.py:444
  66.5 1.9 %collective-permute-start.21 = (f32[32,128]{1,0:T(8,128)S(1)}, f32[32,128]{1,0:T(8,128)S(1)}, u32[]{:S(2)}, u32[]{:S(2)}) collective-permute-start(f32[32,128]{1,0:T(8,128)S(1)} %add_add_fusion), channel_id=1, source_target_pairs={{0,128},{32,160},{64,192},{96,224},{128,0},{160,32},{192,64},{224,... | collective-permute-start | bytes 49160 | tf_op jit(solution)/shard_map/ppermute | solution.py:444
  68.5 1.1 %collective-permute-done.21 = f32[32,128]{1,0:T(8,128)S(1)} collective-permute-done((f32[32,128]{1,0:T(8,128)S(1)}, f32[32,128]{1,0:T(8,128)S(1)}, u32[]{:S(2)}, u32[]{:S(2)}) %collective-permute-start.21) | collective-permute-done | bytes 16416 | tf_op jit(solution)/shard_map/ppermute | solution.py:444
  69.6 6.3 %collective-permute-start.22 = (f32[32,128]{1,0:T(8,128)S(1)}, f32[32,128]{1,0:T(8,128)S(1)}, u32[]{:S(2)}, u32[]{:S(2)}) collective-permute-start(f32[32,128]{1,0:T(8,128)S(1)} %add.18), channel_id=1, source_target_pairs={{0,1},{1,0},{2,3},{3,2},{4,5},{5,4},{6,7},{7,6},{8,9},{9,8},{10,11... | collective-permute-start | bytes 49160 | tf_op jit(solution)/shard_map/ppermute | solution.py:444
  76.0 1.3 %finish_rows.1 = (bf16[128,2048]{1,0:T(8,128)(2,1)}, bf16[128,2048]{1,0:T(8,128)(2,1)}, bf16[128,2048]{1,0:T(8,128)(2,1)}) custom-call(s32[1]{0:T(128)} %bitcast.c_ref, bf16[192,128]{1,0:T(8,128)(2,1)S(1)} %get-tuple-element.61.z0.y0, ...), custom_call_target="tpu_custom_call", output_to_operand_aliasing={{0}: (22, {}), {1}: (23, {}), {2}: (24, {})} | custom-call | tf_op jit(solution)/shard_map/finish_rows/pallas_call | solution.py:554
  77.3 0.6 slice_bitcast_fusion
  (31 shorter events, 2.1 us)
Async XLA Ops:
  1.6 5.6 %collective-permute-start.2 = (bf16[128,128]{1,0:T(8,128)(2,1)S(1)}, bf16[128,128]{1,0:T(8,128)(2,1)S(1)}, u32[]{:S(2)}, u32[]{:S(2)}) collective-permute-start(bf16[128,128]{1,0:T(8,128)(2,1)S(1)} %get-tuple-element.45.f1), channel_id=1, source_target_pairs={{0,2},{1,3},{2,0},{3,1},{4,6},{5,7},{6,4},{7,5},{8,10},{9,11},{10,... | collective-permute-start | bytes 98312 | tf_op jit(solution)/shard_map/ppermute | solution.py:444
  4.1 4.6 %collective-permute-start = (bf16[128,128]{1,0:T(8,128)(2,1)S(1)}, bf16[128,128]{1,0:T(8,128)(2,1)S(1)}, u32[]{:S(2)}, u32[]{:S(2)}) collective-permute-start(bf16[128,128]{1,0:T(8,128)(2,1)S(1)} %get-tuple-element.43.f2), channel_id=1, source_target_pairs={{0,4},{1,5},{2,6},{3,7},{4,0},{5,1},{6,2},{7,3},{8,12},{9,13},{10,... | collective-permute-start | bytes 98312 | tf_op jit(solution)/shard_map/ppermute | solution.py:444
  7.1 4.6 %collective-permute-start.1 = (bf16[128,128]{1,0:T(8,128)(2,1)S(1)}, bf16[128,128]{1,0:T(8,128)(2,1)S(1)}, u32[]{:S(2)}, u32[]{:S(2)}) collective-permute-start(bf16[128,128]{1,0:T(8,128)(2,1)S(1)} %get-tuple-element.44.f3), channel_id=1, source_target_pairs={{0,6},{1,7},{2,4},{3,5},{4,2},{5,3},{6,0},{7,1},{8,14},{9,15},{10,... | collective-permute-start | bytes 98312 | tf_op jit(solution)/shard_map/ppermute | solution.py:444
  11.9 10.5 %collective-permute-start.6 = (bf16[512,128]{1,0:T(8,128)(2,1)S(1)}, bf16[512,128]{1,0:T(8,128)(2,1)S(1)}, u32[]{:S(2)}, u32[]{:S(2)}) collective-permute-start(bf16[512,128]{1,0:T(8,128)(2,1)S(1)} %pack_far_rows.1), channel_id=1, source_target_pairs={{0,16},{1,17},{2,18},{3,19},{4,20},{5,21},{6,22},{7,23},{8,24},{9,... | collective-permute-start | bytes 393224 | tf_op jit(solution)/shard_map/ppermute | solution.py:444
  14.7 15.6 %collective-permute-start.7 = (bf16[512,128]{1,0:T(8,128)(2,1)S(1)}, bf16[512,128]{1,0:T(8,128)(2,1)S(1)}, u32[]{:S(2)}, u32[]{:S(2)}) collective-permute-start(bf16[512,128]{1,0:T(8,128)(2,1)S(1)} %pack_far_rows.1), channel_id=1, source_target_pairs={{0,12},{1,13},{2,14},{3,15},{4,8},{5,9},{6,10},{7,11},{8,4},{9,5},... | collective-permute-start | bytes 393224 | tf_op jit(solution)/shard_map/ppermute | solution.py:444
  16.4 13.9 %collective-permute-start.8 = (bf16[512,128]{1,0:T(8,128)(2,1)S(1)}, bf16[512,128]{1,0:T(8,128)(2,1)S(1)}, u32[]{:S(2)}, u32[]{:S(2)}) collective-permute-start(bf16[512,128]{1,0:T(8,128)(2,1)S(1)} %pack_far_rows.1), channel_id=1, source_target_pairs={{0,28},{1,29},{2,30},{3,31},{4,24},{5,25},{6,26},{7,27},{8,20},{9,... | collective-permute-start | bytes 393224 | tf_op jit(solution)/shard_map/ppermute | solution.py:444
  18.2 4.2 %copy-start.1 = (f32[2048]{0:T(1024)S(1)}, f32[2048]{0:T(1024)}, u32[]{:S(2)}) copy-start(f32[2048]{0:T(1024)} %param.10) | copy-start | bytes 24580
  19.5 2.9 %copy-start = (f32[2048]{0:T(1024)S(1)}, f32[2048]{0:T(1024)}, u32[]{:S(2)}) copy-start(f32[2048]{0:T(1024)} %param.11) | copy-start | bytes 24580
  19.5 10.8 %collective-permute-start.3 = (bf16[512,128]{1,0:T(8,128)(2,1)S(1)}, bf16[512,128]{1,0:T(8,128)(2,1)S(1)}, u32[]{:S(2)}, u32[]{:S(2)}) collective-permute-start(bf16[512,128]{1,0:T(8,128)(2,1)S(1)} %get-tuple-element.47.m2), channel_id=1, source_target_pairs={{0,4},{1,5},{2,6},{3,7},{4,0},{5,1},{6,2},{7,3},{8,12},{9,13},{10,... | collective-permute-start | bytes 393224 | tf_op jit(solution)/shard_map/ppermute | solution.py:444
  20.7 10.2 %collective-permute-start.4 = (bf16[512,128]{1,0:T(8,128)(2,1)S(1)}, bf16[512,128]{1,0:T(8,128)(2,1)S(1)}, u32[]{:S(2)}, u32[]{:S(2)}) collective-permute-start(bf16[512,128]{1,0:T(8,128)(2,1)S(1)} %get-tuple-element.48.m3), channel_id=1, source_target_pairs={{0,6},{1,7},{2,4},{3,5},{4,2},{5,3},{6,0},{7,1},{8,14},{9,15},{10,... | collective-permute-start | bytes 393224 | tf_op jit(solution)/shard_map/ppermute | solution.py:444
  22.4 9.5 %collective-permute-start.5 = (bf16[512,128]{1,0:T(8,128)(2,1)S(1)}, bf16[512,128]{1,0:T(8,128)(2,1)S(1)}, u32[]{:S(2)}, u32[]{:S(2)}) collective-permute-start(bf16[512,128]{1,0:T(8,128)(2,1)S(1)} %get-tuple-element.49.m1), channel_id=1, source_target_pairs={{0,2},{1,3},{2,0},{3,1},{4,6},{5,7},{6,4},{7,5},{8,10},{9,11},{10,... | collective-permute-start | bytes 393224 | tf_op jit(solution)/shard_map/ppermute | solution.py:444
  34.0 6.4 %collective-permute-start.10 = (bf16[576,128]{1,0:T(8,128)(2,1)S(1)}, bf16[576,128]{1,0:T(8,128)(2,1)S(1)}, u32[]{:S(2)}, u32[]{:S(2)}) collective-permute-start(bf16[576,128]{1,0:T(8,128)(2,1)S(1)} %get-tuple-element.59), channel_id=1, source_target_pairs={{0,12},{1,13},{2,14},{3,15},{4,8},{5,9},{6,10},{7,11},{8,4},{9,5},... | collective-permute-start | bytes 442376 | tf_op jit(solution)/shard_map/ppermute | solution.py:444
  37.0 5.5 %collective-permute-start.11 = (bf16[576,128]{1,0:T(8,128)(2,1)S(1)}, bf16[576,128]{1,0:T(8,128)(2,1)S(1)}, u32[]{:S(2)}, u32[]{:S(2)}) collective-permute-start(bf16[576,128]{1,0:T(8,128)(2,1)S(1)} %get-tuple-element.60), channel_id=1, source_target_pairs={{0,16},{1,17},{2,18},{3,19},{4,20},{5,21},{6,22},{7,23},{8,24},{9,... | collective-permute-start | bytes 442376 | tf_op jit(solution)/shard_map/ppermute | solution.py:444
  39.5 8.5 %collective-permute-start.9 = (bf16[576,128]{1,0:T(8,128)(2,1)S(1)}, bf16[576,128]{1,0:T(8,128)(2,1)S(1)}, u32[]{:S(2)}, u32[]{:S(2)}) collective-permute-start(bf16[576,128]{1,0:T(8,128)(2,1)S(1)} %get-tuple-element.58), channel_id=1, source_target_pairs={{0,28},{1,29},{2,30},{3,31},{4,24},{5,25},{6,26},{7,27},{8,20},{9,... | collective-permute-start | bytes 442376 | tf_op jit(solution)/shard_map/ppermute | solution.py:444
  48.1 8.1 %collective-permute-start.12 = (bf16[192,128]{1,0:T(8,128)(2,1)S(1)}, bf16[192,128]{1,0:T(8,128)(2,1)S(1)}, u32[]{:S(2)}, u32[]{:S(2)}) collective-permute-start(bf16[192,128]{1,0:T(8,128)(2,1)S(1)} %get-tuple-element.62), channel_id=1, source_target_pairs={{0,4},{1,5},{2,6},{3,7},{4,0},{5,1},{6,2},{7,3},{8,12},{9,13},{10,... | collective-permute-start | bytes 147464 | tf_op jit(solution)/shard_map/ppermute | solution.py:444
  54.6 5.1 %collective-permute-start.13 = (bf16[192,128]{1,0:T(8,128)(2,1)S(1)}, bf16[192,128]{1,0:T(8,128)(2,1)S(1)}, u32[]{:S(2)}, u32[]{:S(2)}) collective-permute-start(bf16[192,128]{1,0:T(8,128)(2,1)S(1)} %get-tuple-element.63), channel_id=1, source_target_pairs={{0,6},{1,7},{2,4},{3,5},{4,2},{5,3},{6,0},{7,1},{8,14},{9,15},{10,... | collective-permute-start | bytes 147464 | tf_op jit(solution)/shard_map/ppermute | solution.py:444
  54.6 5.1 %collective-permute-start.14 = (bf16[192,128]{1,0:T(8,128)(2,1)S(1)}, bf16[192,128]{1,0:T(8,128)(2,1)S(1)}, u32[]{:S(2)}, u32[]{:S(2)}) collective-permute-start(bf16[192,128]{1,0:T(8,128)(2,1)S(1)} %get-tuple-element.64), channel_id=1, source_target_pairs={{0,2},{1,3},{2,0},{3,1},{4,6},{5,7},{6,4},{7,5},{8,10},{9,11},{10,... | collective-permute-start | bytes 147464 | tf_op jit(solution)/shard_map/ppermute | solution.py:444
  59.6 5.3 %collective-permute-start.18 = (f32[32,128]{1,0:T(8,128)S(1)}, f32[32,128]{1,0:T(8,128)S(1)}, u32[]{:S(2)}, u32[]{:S(2)}) collective-permute-start(f32[32,128]{1,0:T(8,128)S(1)} %sum_gains.1), channel_id=1, source_target_pairs={{0,32},{32,0},{64,96},{96,64},{128,160},{160,128},{192,224},{224,1... | collective-permute-start | bytes 49160 | tf_op jit(solution)/shard_map/ppermute | solution.py:444
  60.1 6.1 %collective-permute-start.19 = (f32[32,128]{1,0:T(8,128)S(1)}, f32[32,128]{1,0:T(8,128)S(1)}, u32[]{:S(2)}, u32[]{:S(2)}) collective-permute-start(f32[32,128]{1,0:T(8,128)S(1)} %sum_gains.1), channel_id=1, source_target_pairs={{0,64},{32,96},{64,0},{96,32},{128,192},{160,224},{192,128},{224,1... | collective-permute-start | bytes 49160 | tf_op jit(solution)/shard_map/ppermute | solution.py:444
  62.7 3.8 %collective-permute-start.20 = (f32[32,128]{1,0:T(8,128)S(1)}, f32[32,128]{1,0:T(8,128)S(1)}, u32[]{:S(2)}, u32[]{:S(2)}) collective-permute-start(f32[32,128]{1,0:T(8,128)S(1)} %sum_gains.1), channel_id=1, source_target_pairs={{0,96},{32,64},{64,32},{96,0},{128,224},{160,192},{192,160},{224,1... | collective-permute-start | bytes 49160 | tf_op jit(solution)/shard_map/ppermute | solution.py:444
  63.6 12.4 %collective-permute-start.15 = (bf16[384,128]{1,0:T(8,128)(2,1)S(1)}, bf16[384,128]{1,0:T(8,128)(2,1)S(1)}, u32[]{:S(2)}, u32[]{:S(2)}) collective-permute-start(bf16[384,128]{1,0:T(8,128)(2,1)S(1)} %get-tuple-element.66), channel_id=1, source_target_pairs={{0,4},{1,5},{2,6},{3,7},{4,0},{5,1},{6,2},{7,3},{8,12},{9,13},{10,... | collective-permute-start | bytes 294920 | tf_op jit(solution)/shard_map/ppermute | solution.py:444
  64.9 11.1 %collective-permute-start.16 = (bf16[384,128]{1,0:T(8,128)(2,1)S(1)}, bf16[384,128]{1,0:T(8,128)(2,1)S(1)}, u32[]{:S(2)}, u32[]{:S(2)}) collective-permute-start(bf16[384,128]{1,0:T(8,128)(2,1)S(1)} %get-tuple-element.67), channel_id=1, source_target_pairs={{0,6},{1,7},{2,4},{3,5},{4,2},{5,3},{6,0},{7,1},{8,14},{9,15},{10,... | collective-permute-start | bytes 294920 | tf_op jit(solution)/shard_map/ppermute | solution.py:444
  65.0 11.0 %collective-permute-start.17 = (bf16[384,128]{1,0:T(8,128)(2,1)S(1)}, bf16[384,128]{1,0:T(8,128)(2,1)S(1)}, u32[]{:S(2)}, u32[]{:S(2)}) collective-permute-start(bf16[384,128]{1,0:T(8,128)(2,1)S(1)} %get-tuple-element.68), channel_id=1, source_target_pairs={{0,2},{1,3},{2,0},{3,1},{4,6},{5,7},{6,4},{7,5},{8,10},{9,11},{10,... | collective-permute-start | bytes 294920 | tf_op jit(solution)/shard_map/ppermute | solution.py:444
  66.5 3.1 %collective-permute-start.21 = (f32[32,128]{1,0:T(8,128)S(1)}, f32[32,128]{1,0:T(8,128)S(1)}, u32[]{:S(2)}, u32[]{:S(2)}) collective-permute-start(f32[32,128]{1,0:T(8,128)S(1)} %add_add_fusion), channel_id=1, source_target_pairs={{0,128},{32,160},{64,192},{96,224},{128,0},{160,32},{192,64},{224,... | collective-permute-start | bytes 49160 | tf_op jit(solution)/shard_map/ppermute | solution.py:444
  69.6 7.6 %collective-permute-start.22 = (f32[32,128]{1,0:T(8,128)S(1)}, f32[32,128]{1,0:T(8,128)S(1)}, u32[]{:S(2)}, u32[]{:S(2)}) collective-permute-start(f32[32,128]{1,0:T(8,128)S(1)} %add.18), channel_id=1, source_target_pairs={{0,1},{1,0},{2,3},{3,2},{4,5},{5,4},{6,7},{7,6},{8,9},{9,8},{10,11... | collective-permute-start | bytes 49160 | tf_op jit(solution)/shard_map/ppermute | solution.py:444

commit v3 on v2

--- a/solution.py
+++ b/solution.py
@@ -76,23 +76,30 @@
     return lax.dot_general(a, b, (((0,), (0,)), ((), ())), preferred_element_type=F32)
 
 
-def pack_kernel(early, c_ref, q, k, v, g, *refs):
-    outs, sems = refs[-5:-1], refs[-1]
+def early_tiles(step):
+    far = step & 1
+    tiles = (("k", far), ("v", far))
+    return tiles + late_tiles(step) if step == 1 else tiles
+
+
+def late_tiles(step):
+    far = step & 1
+    near = 1 - far
+    return (("q", far), ("g", far), ("q", near), ("g", near), ("k", near), ("v", near), ("k", 2), ("v", 2))
+
+
+def pack_kernel(plan, c_ref, q, k, v, g, *refs):
+    outs, sems = refs[-1 - len(plan) : -1], refs[-1]
+    sources = {"q": q, "k": k, "v": v, "g": g}
     c = c_ref[0]
     copies = []
-    for step, out in enumerate(outs):
+    for (step, tiles), out in zip(plan, outs):
         heads = owned_heads(c, step)
-        far = step & 1
-        near = 1 - far
-        if early:
-            tiles = ((k, far), (v, far))
-        else:
-            tiles = ((q, far), (g, far), (q, near), (g, near), (k, near), (v, near), (k, 2), (v, 2))
-        for t, (src, e) in enumerate(tiles):
+        for t, (name, e) in enumerate(tiles):
             row = 0 if e == 2 else e * TILE
             h = heads[min(e, 1)]
             copy = pltpu.make_async_copy(
-                src.at[pl.ds(row, TILE), pl.ds(pl.multiple_of(h * HD, HD), HD)],
+                sources[name].at[pl.ds(row, TILE), pl.ds(pl.multiple_of(h * HD, HD), HD)],
                 out.at[pl.ds(t * TILE, TILE), :],
                 sems.at[len(copies)],
             )
@@ -112,25 +119,28 @@
     return ref[at : at + 32, :].astype(F32) + ref[at + 32 : at + 64, :].astype(F32)
 
 
-def forward_pack_kernel(f0, f2, f3, f1, out, sems):
+def forward_pack_kernel(f0, f2, f3, f1, ready, out, sems):
     copies = []
     for k, src in enumerate((f0, f2, f1, f3)):
-        copy = pltpu.make_async_copy(src, out.at[pl.ds(2 * k * TILE, 2 * TILE), :], sems.at[k])
+        copy = pltpu.make_async_copy(
+            src.at[pl.ds(0, 2 * TILE), :], out.at[pl.ds(2 * k * TILE, 2 * TILE), :], sems.at[k]
+        )
         copy.start()
         copies.append(copy)
     for copy in copies:
         copy.wait()
 
 
-def home_kernel(half, c_ref, q, k, v, g, q_gain, k_gain, *refs):
-    refs = refs[3 * half :]
-    outs, part_k, part_v, gains = refs[:3], refs[3], refs[4], refs[5]
-    loads, stores, dk_all, dv_all, in_sems, out_sems = refs[6:]
+def home_kernel(
+    c_ref, q, k, v, g, q_gain, k_gain, gq_out, gk_out, gv_out, part_k, part_v, gains,
+    loads, stores, dk_all, dv_all, in_sems, out_sems,
+):
+    outs = (gq_out, gk_out, gv_out)
     c = c_ref[0]
     core = c & 1
-    count = HEADS // 2
-    group = 4
-    first = half * count
+    count = HEADS
+    group = 8
+    first = 0
     for n in range(count // group):
         cols = pl.ds((first + n * group) * HD, group * HD)
         for i, src in enumerate((q, k, v, g)):
@@ -184,9 +194,9 @@
             copy = pltpu.make_async_copy(stores.at[i, :, here], dst.at[:, cols], out_sems.at[n, i])
             copy.start()
             copies.append(copy)
-    for j in range(2):
-        h0 = 2 * core + 4 * j
-        h1 = 2 * core + 1 + 4 * (1 - j)
+    for j in range(4):
+        h0 = 2 * core + 8 * (j >> 1) + 4 * (j & 1)
+        h1 = 2 * core + 1 + 8 * (j >> 1) + 4 * (1 - (j & 1))
         for i, (h, e) in enumerate(((h0, 0), (h1, 1), (h1, 0))):
             rows = slice(e * TILE, (e + 1) * TILE)
             part_k[3 * j + i] = dk_all[h, rows, :]
@@ -196,22 +206,19 @@
 
 
 def owner_kernel(
-    c_ref, f0, f2, f3, f1, r0, r2, r3, r1, b1, b2, b3, q_gain, k_gain, low_gains, high_gains,
+    c_ref, f0, f2, f3, f1, r0, r2, r3, b3, b2, b1, q_gain, k_gain, home_gains,
     x0, x1, x2, x3, t1, t2, t3, far_k, far_v, gains_out, gains,
 ):
     c = c_ref[0]
     core, zl, zh, xh = place(c)
     heads = owned_heads(c, 0)
     early = (f0, f1, f2, f3)
-    late = (r0, r1, r2, r3)
+    late = (r0, f1.at[pl.ds(2 * TILE, 8 * TILE), :], r2, r3)
     crossed = (b1, b2, b3)
     returned = (x0, x1, x2, x3)
     terms = (t1, t2, t3)
     live = (xh == 1, zh == 1, xh == 1)
-    half = HEADS // 2
-    for at, src in ((0, low_gains), (half, high_gains)):
-        gains[at : at + half, :] = src[0:half, :]
-        gains[HEADS + at : HEADS + at + half, :] = src[half:, :]
+    gains[...] = home_gains[...]
     row = lax.broadcasted_iota(jnp.int32, (TILE, 4 * TILE), 0)
     col = lax.broadcasted_iota(jnp.int32, (TILE, 4 * TILE), 1)
     block = col >> 6
@@ -349,7 +356,8 @@
         out[at + 32 :, :] = low
 
 
-def return_pack_kernel(far_k, far_v, own, u1, u2, u3, y0, y1, y2, y3):
+def return_pack_kernel(far_k, far_v, own, u1, u2, u3, x1, *refs):
+    y0, y1, y2, y3 = refs[-4:]
     total = (joined_gains(own) + joined_gains(u2)) + (joined_gains(u1) + joined_gains(u3))
     high, low = split_gains(total)
     for i, y in enumerate((y0, y1, y2, y3)):
@@ -361,17 +369,24 @@
             dv += u[at + 128 : at + 128 + TILE, :].astype(F32)
         y[0:TILE, :] = dk.astype(BF)
         y[TILE : 2 * TILE, :] = dv.astype(BF)
-        y[2 * TILE : 2 * TILE + 32, :] = high
-        y[2 * TILE + 32 :, :] = low
+        at = y.shape[0] - 64
+        y[at : at + 32, :] = high
+        y[at + 32 :, :] = low
+    y1[2 * TILE : 8 * TILE, :] = x1[...]
 
 
 def gains_kernel(y0, y2, y3, y1, out):
     out[...] = (joined_gains(y0) + joined_gains(y1)) + (joined_gains(y2) + joined_gains(y3))
 
 
+def last_sum_kernel(mine, other, q_out, k_out):
+    q_out[...] = mine[0:HEADS, :] + other[0:HEADS, :]
+    k_out[...] = mine[HEADS:, :] + other[HEADS:, :]
+
+
 def final_kernel(
-    c_ref, z0, z2, z3, z1, y0, y2, y3, y1, f0, f1, f2, f3, m0, m1, m2, m3,
-    low_k, low_v, high_k, high_v, k_gain, gq_in, gk_in, gv_in,
+    c_ref, z0, z2, z3, z1, y0, y2, y3, f0, f1, f2, f3, m0, m2, m3,
+    part_k, part_v, k_gain, gq_in, gk_in, gv_in,
     gq_out, gk_out, gv_out, done_k, done_v, sems,
 ):
     c = c_ref[0]
@@ -389,6 +404,8 @@
     def tile_of(ref, t):
         return ref[t * TILE : (t + 1) * TILE, :]
 
+    y1 = z1.at[pl.ds(2 * TILE, 6 * TILE), :]
+    m1 = f1.at[pl.ds(2 * TILE, 8 * TILE), :]
     jobs = []
     for step in range(4):
         heads = owned_heads(c, step)
@@ -406,20 +423,19 @@
             (heads[near], near, y, 2, tile_of(m, 4)),
             (heads[1], 0, y, 4, tile_of(m, 6)),
         )):
-            part = 3 * (owner & 1) + (far, near, 2)[i]
-            jobs.append((3 * step + i, 8 * step + 2 + 2 * i, part, owner < 2, h, e, back, at, raw))
-    for n, sem, part, is_low, h, e, back, at, raw in jobs:
-        dv = jnp.where(is_low, low_v[part], high_v[part])
-        done_v[n] = (dv + tile_of(back, at + 1).astype(F32)).astype(BF)
+            part = 3 * owner + (far, near, 2)[i]
+            jobs.append((3 * step + i, 8 * step + 2 + 2 * i, part, h, e, back, at, raw))
+    for n, sem, part, h, e, back, at, raw in jobs:
+        done_v[n] = (part_v[part] + tile_of(back, at + 1).astype(F32)).astype(BF)
         send(done_v.at[n], gv_out, e, h, sem + 1)
-    kg = [k_gain[pl.ds(job[4], 1), :] for job in jobs]
-    ks = [normalize(job[8], x) for job, x in zip(jobs, kg)]
+    kg = [k_gain[pl.ds(job[3], 1), :] for job in jobs]
+    ks = [normalize(job[7], x) for job, x in zip(jobs, kg)]
     dk = [
-        jnp.where(is_low, low_k[part], high_k[part]) + tile_of(back, at).astype(F32)
-        for n, sem, part, is_low, h, e, back, at, raw in jobs
+        part_k[part] + tile_of(back, at).astype(F32)
+        for n, sem, part, h, e, back, at, raw in jobs
     ]
     done = [norm_grad(x, y[0], y[1], z) for x, y, z in zip(dk, ks, kg)]
-    for (n, sem, part, is_low, h, e, back, at, raw), x in zip(jobs, done):
+    for (n, sem, part, h, e, back, at, raw), x in zip(jobs, done):
         done_k[n] = x
         send(done_k.at[n], gk_out, e, h, sem)
     for copy in copies:
@@ -452,62 +468,56 @@
         moved = {i: swap(blocks[i], "ctx", 2 * i) for i in (2, 3, 1)}
         return [blocks[0], moved[1], moved[2], moved[3]]
 
-    def pack_call(early, *after):
-        count = 2 if early else 8
+    def pack_call(name, plan, *after):
         return pl.pallas_call(
-            functools.partial(pack_kernel, early),
+            functools.partial(pack_kernel, plan),
             in_specs=[smem_spec()] + [hbm_spec()] * 4 + [any_spec()] * len(after),
-            out_specs=[any_spec()] * 4,
-            out_shape=[shape((count * TILE, HD), BF)] * 4,
-            scratch_shapes=[pltpu.SemaphoreType.DMA((4 * count,))],
+            out_specs=[any_spec()] * len(plan),
+            out_shape=[shape((len(tiles) * TILE, HD), BF) for _, tiles in plan],
+            scratch_shapes=[pltpu.SemaphoreType.DMA((sum(len(tiles) for _, tiles in plan),))],
             compiler_params=params,
-            name="pack_early" if early else "pack_late",
+            name=name,
         )(here, q, k, v, g, *after)
 
-    packed_early = pack_call(True)
+    packed_early = pack_call("pack_early", tuple((i, early_tiles(i)) for i in range(4)))
     early = around(packed_early)
-    packed_late = pack_call(False, early[1])
-    late = around(packed_late)
-
-    def home_call(half, earlier):
-        return pl.pallas_call(
-            functools.partial(home_kernel, half),
-            in_specs=[smem_spec()] + [hbm_spec()] * 4 + [vmem_spec()] * 2 + [hbm_spec()] * len(earlier),
-            out_specs=[hbm_spec()] * 3 + [vmem_spec()] * 3,
-            out_shape=[shape((ROWS, HEADS * HD), BF)] * 3
-            + [shape((6, TILE, HD), F32)] * 2
-            + [shape((HEADS, HD), F32)],
-            scratch_shapes=[
-                pltpu.VMEM((4, ROWS, HEADS * HD // 2), BF),
-                pltpu.VMEM((3, ROWS, HEADS * HD // 2), BF),
-                pltpu.VMEM((HEADS // 2, ROWS, HD), F32),
-                pltpu.VMEM((HEADS // 2, ROWS, HD), F32),
-                pltpu.SemaphoreType.DMA((2, 4)),
-                pltpu.SemaphoreType.DMA((2, 3)),
-            ],
-            input_output_aliases={7 + i: i for i in range(len(earlier))},
-            compiler_params=params,
-            name="home_slab_high" if half else "home_slab_low",
-        )(here, q, k, v, g, qg, kg, *earlier)
-
-    low = home_call(0, ())
-    high = home_call(1, low[:3])
+    packed_late = pack_call("pack_late", tuple((i, late_tiles(i)) for i in (0, 2, 3)), early[1])
+    late = [packed_late[0], swap(packed_late[1], "ctx", 4), swap(packed_late[2], "ctx", 6)]
+
+    gq_home, gk_home, gv_home, part_k, part_v, home_gains = pl.pallas_call(
+        home_kernel,
+        in_specs=[smem_spec()] + [hbm_spec()] * 4 + [vmem_spec()] * 2,
+        out_specs=[hbm_spec()] * 3 + [vmem_spec()] * 3,
+        out_shape=[shape((ROWS, HEADS * HD), BF)] * 3
+        + [shape((12, TILE, HD), F32)] * 2
+        + [shape((2 * HEADS, HD), F32)],
+        scratch_shapes=[
+            pltpu.VMEM((4, ROWS, HEADS * HD), BF),
+            pltpu.VMEM((3, ROWS, HEADS * HD), BF),
+            pltpu.VMEM((HEADS, ROWS, HD), F32),
+            pltpu.VMEM((HEADS, ROWS, HD), F32),
+            pltpu.SemaphoreType.DMA((2, 4)),
+            pltpu.SemaphoreType.DMA((2, 3)),
+        ],
+        compiler_params=params,
+        name="home_slab",
+    )(here, q, k, v, g, qg, kg)
 
     onward = pl.pallas_call(
         forward_pack_kernel,
-        in_specs=[any_spec()] * 4,
+        in_specs=[any_spec()] * 5,
         out_specs=any_spec(),
         out_shape=shape((8 * TILE, HD), BF),
         scratch_shapes=[pltpu.SemaphoreType.DMA((4,))],
         compiler_params=params,
         name="pack_far_rows",
-    )(*by_distance(early))
+    )(*by_distance(early), packed_late[0])
     moved = {mask: swap(onward, "ctx", mask) for mask in (16, 12, 28)}
     crossed = [moved[mask] for mask in steps]
 
     outs = pl.pallas_call(
         owner_kernel,
-        in_specs=[smem_spec()] + [vmem_spec()] * 15,
+        in_specs=[smem_spec()] + [vmem_spec()] * 13,
         out_specs=[vmem_spec()] * 10,
         out_shape=[shape((6 * TILE, HD), BF)] * 4
         + [shape((9 * TILE, HD), BF)] * 3
@@ -516,7 +526,7 @@
         scratch_shapes=[pltpu.VMEM((2 * HEADS, HD), F32)],
         compiler_params=params,
         name="owned_heads",
-    )(here, *by_distance(early), *by_distance(late), *crossed, qg, kg, low[5], high[5])
+    )(here, *by_distance(early), *late, crossed[2], crossed[1], crossed[0], qg, kg, home_gains)
     back_early, terms, far_k, far_v, own_gains = outs[:4], outs[4:7], outs[7], outs[8], outs[9]
     moved = {mask: swap(terms[steps.index(mask)], "ctx", mask) for mask in (28, 12, 16)}
     terms_in = [moved[mask] for mask in steps]
@@ -528,15 +538,16 @@
         one, two, three = (swap(x, axis, i * mask) for i in (1, 2, 3))
         return (x + one) + (two + three)
 
+    home_early = [back_early[0], swap(back_early[2], "ctx", 4), swap(back_early[3], "ctx", 6)]
+    waits = ()
     back_late = pl.pallas_call(
         return_pack_kernel,
-        in_specs=[vmem_spec()] * 6,
+        in_specs=[vmem_spec()] * 7 + [any_spec()] * len(waits),
         out_specs=[vmem_spec()] * 4,
-        out_shape=[shape((3 * TILE, HD), BF)] * 4,
+        out_shape=[shape((count * TILE, HD), BF) for count in (3, 9, 3, 3)],
         compiler_params=params,
         name="add_far_terms",
-    )(far_k, far_v, own_gains, *terms_in[::-1])
-    home_early = around(back_early)
+    )(far_k, far_v, own_gains, *terms_in[::-1], back_early[1], *waits)
     home_late = around(back_late)
 
     gains = pl.pallas_call(
@@ -549,28 +560,35 @@
     )(*by_distance(home_late))
     gains = quad_sum(gains, "dp", 1)
     gains = pair_sum(gains, "dp", 4)
-    gains = pair_sum(gains, "ctx", 1)
+    q_sum, k_sum = pl.pallas_call(
+        last_sum_kernel,
+        in_specs=[vmem_spec()] * 2,
+        out_specs=[vmem_spec()] * 2,
+        out_shape=[shape((HEADS, HD), F32)] * 2,
+        compiler_params=params,
+        name="last_sum",
+    )(gains, swap(gains, "ctx", 1))
 
     gq, gk, gv = pl.pallas_call(
         final_kernel,
-        in_specs=[smem_spec()] + [vmem_spec()] * 21 + [any_spec()] * 3,
+        in_specs=[smem_spec()] + [vmem_spec()] * 17 + [any_spec()] * 3,
         out_specs=[any_spec()] * 3,
         out_shape=[shape((ROWS, HEADS * HD), BF)] * 3,
         scratch_shapes=[pltpu.VMEM((12, TILE, HD), BF)] * 2 + [pltpu.SemaphoreType.DMA((32,))],
-        input_output_aliases={22: 0, 23: 1, 24: 2},
+        input_output_aliases={18: 0, 19: 1, 20: 2},
         compiler_params=params,
         name="finish_rows",
     )(
-        here, *by_distance(home_late), *by_distance(home_early), *packed_early, *packed_late,
-        low[3], low[4], high[3], high[4], kg, *high[:3],
+        here, *by_distance(home_late), *home_early, *packed_early, *packed_late,
+        part_k, part_v, kg, gq_home, gk_home, gv_home,
     )
     whole = lambda a: a.reshape(1, ROWS, HEADS * HD)
     return (
         whole(gq),
         whole(gk),
         whole(gv),
-        gains[:HEADS].reshape(HEADS * HD),
-        gains[HEADS:].reshape(HEADS * HD),
+        q_sum.reshape(HEADS * HD),
+        k_sum.reshape(HEADS * HD),
     )
 
 

time: 78.1 us -> 75.5 us (0.967)
  Pallas kernels: 13.8 us -> 11.6 us
  waiting for transfers between devices: 19.8 us -> 20.9 us
  starting transfers between devices: 42.8 us -> 41.9 us
    pallas_call x8, Pallas kernels: 13.8 us -> 11.6 us  [the longest x1 5.18 us: per_device(): pl.pallas_call(home_kernel, in_specs=[smem_spec()] + [hbm_spec()] * 4 + [...]
    ppermute x23 -> x21, waiting for transfers between devices: 19.8 us -> 20.9 us  [swap(): return lax.ppermute(block, axis, [(i, i ^ mask) for i in range(count)])]
    ppermute x23 -> x21, starting transfers between devices: 42.8 us -> 41.9 us  [swap(): return lax.ppermute(block, axis, [(i, i ^ mask) for i in range(count)])]
  transfers between devices with their start and end apart: 23 -> 21, of which waited for: 10 -> 10; matrix products, arithmetic and copies ran while one was open for 0% -> 0% of each run, Pallas kernels for 13% -> 10%
where the time goes in v3:
time: 75.5 us; the launch traced here: 75.3 us
  starting transfers between devices  41.9 us (55%)
  waiting for transfers between devices  20.9 us (28%)
  Pallas kernels  11.6 us (15%)
    ppermute x21, starting transfers between devices, swap(): return lax.ppermute(block, axis, [(i, i ^ mask) for i in range(count)])  41.9 us
    ppermute x21, waiting for transfers between devices, swap(): return lax.ppermute(block, axis, [(i, i ^ mask) for i in range(count)])  20.9 us
    pallas_call x1, Pallas kernels, per_device(): pl.pallas_call(home_kernel, in_specs=[smem_spec()] + [hbm_spec()] * 4 + [...  5.18 us
    pallas_call x2, Pallas kernels, pack_call(): pl.pallas_call(functools.partial(pack_kernel, plan), in_specs=[smem_spec(...  2.21 us
    pallas_call x1, Pallas kernels, per_device(): pl.pallas_call(owner_kernel, in_specs=[smem_spec()] + [vmem_spec()] * 13,...  2.13 us
  transfers between devices with their start and end apart: 21, of which 10 were waited for; matrix products, arithmetic and copies ran while one was open for 0% of the time, Pallas kernels for 10%

profile of v3, /device:TPU:1, one launch (start us, length us, event | category | flops | bytes accessed | tf_op | source)
XLA Modules:
  0.0 75.3 jit_solution(16488333043319209274)
XLA Ops:
  0.6 1.0 %pack_early.1 = (bf16[128,128]{1,0:T(8,128)(2,1)S(1)}, bf16[640,128]{1,0:T(8,128)(2,1)S(1)}, bf16[128,128]{1,0:T(8,128)(2,1)S(1)}, bf16[128,128]{1,0:T(8,128)(2,1)S(1)}) custom-call(s32[1]{0:T(128)} %bitcast.c_ref, bf16[128,2048]{1,0:T(8,128)(2,1)} %bitcast.17, bf16[128,2048]{1,0:T(8,128)(2,1)} %bitcast.20, bf16[128,2048]{1,0:T(8,128)(2,1)} %bitcast.23, ...), custom_call_target="tpu_custom_call" | custom-call | tf_op jit(solution)/shard_map/pack_early/pallas_call | solution.py:472
  1.7 2.6 %collective-permute-start.2 = (bf16[640,128]{1,0:T(8,128)(2,1)S(1)}, bf16[640,128]{1,0:T(8,128)(2,1)S(1)}, u32[]{:S(2)}, u32[]{:S(2)}) collective-permute-start(bf16[640,128]{1,0:T(8,128)(2,1)S(1)} %get-tuple-element.40.f1), channel_id=1, source_target_pairs={{0,2},{1,3},{2,0},{3,1},{4,6},{5,7},{6,4},{7,5},{8,10},{9,11},{10,... | collective-permute-start | bytes 491528 | tf_op jit(solution)/shard_map/ppermute | solution.py:460
  4.2 3.0 %collective-permute-start = (bf16[128,128]{1,0:T(8,128)(2,1)S(1)}, bf16[128,128]{1,0:T(8,128)(2,1)S(1)}, u32[]{:S(2)}, u32[]{:S(2)}) collective-permute-start(bf16[128,128]{1,0:T(8,128)(2,1)S(1)} %get-tuple-element.38.f2), channel_id=1, source_target_pairs={{0,4},{1,5},{2,6},{3,7},{4,0},{5,1},{6,2},{7,3},{8,12},{9,13},{10,... | collective-permute-start | bytes 98312 | tf_op jit(solution)/shard_map/ppermute | solution.py:460
  7.2 1.2 %pack_late.1 = (bf16[512,128]{1,0:T(8,128)(2,1)S(1)}, bf16[512,128]{1,0:T(8,128)(2,1)S(1)}, bf16[512,128]{1,0:T(8,128)(2,1)S(1)}) custom-call(s32[1]{0:T(128)} %bitcast.c_ref, bf16[128,2048]{1,0:T(8,128)(2,1)} %bitcast.18, bf16[128,2048]{1,0:T(8,128)(2,1)} %bitcast.21, bf16[128,2048]{1,0:T(8,128)(2,1)} %bitcast.24, bf16[128,2048]{1,0:T(8,128)(2,1)} %bitcast.27, ...), custom_call_target="tpu_custom_call" | custom-call | tf_op jit(solution)/shard_map/pack_late/pallas_call | solution.py:472
  8.6 3.6 %collective-permute-done.1.f3 = bf16[128,128]{1,0:T(8,128)(2,1)S(1)} collective-permute-done((bf16[128,128]{1,0:T(8,128)(2,1)S(1)}, bf16[128,128]{1,0:T(8,128)(2,1)S(1)}, u32[]{:S(2)}, u32[]{:S(2)}) %collective-permute-start.1) | collective-permute-done | bytes 32800 | tf_op jit(solution)/shard_map/ppermute | solution.py:460
  12.4 2.8 %collective-permute-start.7 = (bf16[512,128]{1,0:T(8,128)(2,1)S(1)}, bf16[512,128]{1,0:T(8,128)(2,1)S(1)}, u32[]{:S(2)}, u32[]{:S(2)}) collective-permute-start(bf16[512,128]{1,0:T(8,128)(2,1)S(1)} %pack_far_rows.1), channel_id=1, source_target_pairs={{0,16},{1,17},{2,18},{3,19},{4,20},{5,21},{6,22},{7,23},{8,24},{9,... | collective-permute-start | bytes 393224 | tf_op jit(solution)/shard_map/ppermute | solution.py:460
  15.3 2.7 %collective-permute-start.6 = (bf16[512,128]{1,0:T(8,128)(2,1)S(1)}, bf16[512,128]{1,0:T(8,128)(2,1)S(1)}, u32[]{:S(2)}, u32[]{:S(2)}) collective-permute-start(bf16[512,128]{1,0:T(8,128)(2,1)S(1)} %pack_far_rows.1), channel_id=1, source_target_pairs={{0,12},{1,13},{2,14},{3,15},{4,8},{5,9},{6,10},{7,11},{8,4},{9,5},... | collective-permute-start | bytes 393224 | tf_op jit(solution)/shard_map/ppermute | solution.py:460
  18.0 0.8 %collective-permute-start.5 = (bf16[512,128]{1,0:T(8,128)(2,1)S(1)}, bf16[512,128]{1,0:T(8,128)(2,1)S(1)}, u32[]{:S(2)}, u32[]{:S(2)}) collective-permute-start(bf16[512,128]{1,0:T(8,128)(2,1)S(1)} %pack_far_rows.1), channel_id=1, source_target_pairs={{0,28},{1,29},{2,30},{3,31},{4,24},{5,25},{6,26},{7,27},{8,20},{9,... | collective-permute-start | bytes 393224 | tf_op jit(solution)/shard_map/ppermute | solution.py:460
  18.8 1.2 %collective-permute-start.3 = (bf16[512,128]{1,0:T(8,128)(2,1)S(1)}, bf16[512,128]{1,0:T(8,128)(2,1)S(1)}, u32[]{:S(2)}, u32[]{:S(2)}) collective-permute-start(bf16[512,128]{1,0:T(8,128)(2,1)S(1)} %get-tuple-element.42.m2), channel_id=1, source_target_pairs={{0,4},{1,5},{2,6},{3,7},{4,0},{5,1},{6,2},{7,3},{8,12},{9,13},{10,... | collective-permute-start | bytes 393224 | tf_op jit(solution)/shard_map/ppermute | solution.py:460
  19.9 1.6 %collective-permute-start.4 = (bf16[512,128]{1,0:T(8,128)(2,1)S(1)}, bf16[512,128]{1,0:T(8,128)(2,1)S(1)}, u32[]{:S(2)}, u32[]{:S(2)}) collective-permute-start(bf16[512,128]{1,0:T(8,128)(2,1)S(1)} %get-tuple-element.43.m3), channel_id=1, source_target_pairs={{0,6},{1,7},{2,4},{3,5},{4,2},{5,3},{6,0},{7,1},{8,14},{9,15},{10,... | collective-permute-start | bytes 393224 | tf_op jit(solution)/shard_map/ppermute | solution.py:460
  21.6 5.2 %home_slab.1 = (bf16[128,2048]{1,0:T(8,128)(2,1)}, bf16[128,2048]{1,0:T(8,128)(2,1)}, bf16[128,2048]{1,0:T(8,128)(2,1)}, f32[12,64,128]{2,1,0:T(8,128)S(1)}, f32...) custom-call(s32[1]{0:T(128)} %bitcast.c_ref, bf16[128,2048]{1,0:T(8,128)(2,1)} %bitcast.19, bf16[128,2048]{1,0:T(8,128)(2,1)} %bitcast.22, ...), custom_call_target="tpu_custom_call" | custom-call | tf_op jit(solution)/shard_map/home_slab/pallas_call | solution.py:487
  26.8 0.6 collective-permute-done.3.r2
  27.4 0.7 collective-permute-done.4.r3
  28.1 2.1 %owned_heads.1 = (bf16[384,128]{1,0:T(8,128)(2,1)S(1)}, bf16[384,128]{1,0:T(8,128)(2,1)S(1)}, bf16[384,128]{1,0:T(8,128)(2,1)S(1)}, bf16[384,128]{1,0:T(8,128)(2...) custom-call(s32[1]{0:T(128)} %bitcast.c_ref, ...), custom_call_target="tpu_custom_call" | custom-call | tf_op jit(solution)/shard_map/owned_heads/pallas_call | solution.py:518
  30.3 9.4 %collective-permute-start.8 = (bf16[576,128]{1,0:T(8,128)(2,1)S(1)}, bf16[576,128]{1,0:T(8,128)(2,1)S(1)}, u32[]{:S(2)}, u32[]{:S(2)}) collective-permute-start(bf16[576,128]{1,0:T(8,128)(2,1)S(1)} %get-tuple-element.48), channel_id=1, source_target_pairs={{0,28},{1,29},{2,30},{3,31},{4,24},{5,25},{6,26},{7,27},{8,20},{9,... | collective-permute-start | bytes 442376 | tf_op jit(solution)/shard_map/ppermute | solution.py:460
  39.7 0.4 collective-permute-start.10
  40.1 6.4 %collective-permute-done.8.u1 = bf16[576,128]{1,0:T(8,128)(2,1)S(1)} collective-permute-done((bf16[576,128]{1,0:T(8,128)(2,1)S(1)}, bf16[576,128]{1,0:T(8,128)(2,1)S(1)}, u32[]{:S(2)}, u32[]{:S(2)}) %collective-permute-start.8) | collective-permute-done | bytes 147488 | tf_op jit(solution)/shard_map/ppermute | solution.py:460
  46.6 3.3 %collective-permute-done.9.u2 = bf16[576,128]{1,0:T(8,128)(2,1)S(1)} collective-permute-done((bf16[576,128]{1,0:T(8,128)(2,1)S(1)}, bf16[576,128]{1,0:T(8,128)(2,1)S(1)}, u32[]{:S(2)}, u32[]{:S(2)}) %collective-permute-start.9) | collective-permute-done | bytes 147488 | tf_op jit(solution)/shard_map/ppermute | solution.py:460
  50.0 2.9 %collective-permute-start.13 = (bf16[576,128]{1,0:T(8,128)(2,1)S(1)}, bf16[576,128]{1,0:T(8,128)(2,1)S(1)}, u32[]{:S(2)}, u32[]{:S(2)}) collective-permute-start(bf16[576,128]{1,0:T(8,128)(2,1)S(1)} %get-tuple-element.55), channel_id=1, source_target_pairs={{0,2},{1,3},{2,0},{3,1},{4,6},{5,7},{6,4},{7,5},{8,10},{9,11},{10,... | collective-permute-start | bytes 442376 | tf_op jit(solution)/shard_map/ppermute | solution.py:460
  53.2 1.9 %collective-permute-start.12 = (bf16[192,128]{1,0:T(8,128)(2,1)S(1)}, bf16[192,128]{1,0:T(8,128)(2,1)S(1)}, u32[]{:S(2)}, u32[]{:S(2)}) collective-permute-start(bf16[192,128]{1,0:T(8,128)(2,1)S(1)} %get-tuple-element.54), channel_id=1, source_target_pairs={{0,6},{1,7},{2,4},{3,5},{4,2},{5,3},{6,0},{7,1},{8,14},{9,15},{10,... | collective-permute-start | bytes 147464 | tf_op jit(solution)/shard_map/ppermute | solution.py:460
  55.1 2.2 %collective-permute-done.11.z2.y2 = bf16[192,128]{1,0:T(8,128)(2,1)S(1)} collective-permute-done((bf16[192,128]{1,0:T(8,128)(2,1)S(1)}, bf16[192,128]{1,0:T(8,128)(2,1)S(1)}, u32[]{:S(2)}, u32[]{:S(2)}) %collective-permute-start.11) | collective-permute-done | bytes 49184 | tf_op jit(solution)/shard_map/ppermute | solution.py:460
  57.3 1.2 %collective-permute-done.12.z3.y3 = bf16[192,128]{1,0:T(8,128)(2,1)S(1)} collective-permute-done((bf16[192,128]{1,0:T(8,128)(2,1)S(1)}, bf16[192,128]{1,0:T(8,128)(2,1)S(1)}, u32[]{:S(2)}, u32[]{:S(2)}) %collective-permute-start.12) | collective-permute-done | bytes 49184 | tf_op jit(solution)/shard_map/ppermute | solution.py:460
  58.4 2.8 %collective-permute-start.18 = (f32[32,128]{1,0:T(8,128)S(1)}, f32[32,128]{1,0:T(8,128)S(1)}, u32[]{:S(2)}, u32[]{:S(2)}) collective-permute-start(f32[32,128]{1,0:T(8,128)S(1)} %sum_gains.1), channel_id=1, source_target_pairs={{0,96},{32,64},{64,32},{96,0},{128,224},{160,192},{192,160},{224,1... | collective-permute-start | bytes 49160 | tf_op jit(solution)/shard_map/ppermute | solution.py:460
  61.3 0.3 collective-permute-start.17
  62.0 0.8 %collective-permute-start.14 = (bf16[384,128]{1,0:T(8,128)(2,1)S(1)}, bf16[384,128]{1,0:T(8,128)(2,1)S(1)}, u32[]{:S(2)}, u32[]{:S(2)}) collective-permute-start(bf16[384,128]{1,0:T(8,128)(2,1)S(1)} %get-tuple-element.57), channel_id=1, source_target_pairs={{0,4},{1,5},{2,6},{3,7},{4,0},{5,1},{6,2},{7,3},{8,12},{9,13},{10,... | collective-permute-start | bytes 294920 | tf_op jit(solution)/shard_map/ppermute | solution.py:460
  62.8 1.4 %collective-permute-start.15 = (bf16[384,128]{1,0:T(8,128)(2,1)S(1)}, bf16[384,128]{1,0:T(8,128)(2,1)S(1)}, u32[]{:S(2)}, u32[]{:S(2)}) collective-permute-start(bf16[384,128]{1,0:T(8,128)(2,1)S(1)} %get-tuple-element.58), channel_id=1, source_target_pairs={{0,6},{1,7},{2,4},{3,5},{4,2},{5,3},{6,0},{7,1},{8,14},{9,15},{10,... | collective-permute-start | bytes 294920 | tf_op jit(solution)/shard_map/ppermute | solution.py:460
  64.2 1.2 %collective-permute-done.17 = f32[32,128]{1,0:T(8,128)S(1)} collective-permute-done((f32[32,128]{1,0:T(8,128)S(1)}, f32[32,128]{1,0:T(8,128)S(1)}, u32[]{:S(2)}, u32[]{:S(2)}) %collective-permute-start.17) | collective-permute-done | bytes 16416 | tf_op jit(solution)/shard_map/ppermute | solution.py:460
  65.4 1.6 %collective-permute-start.19 = (f32[32,128]{1,0:T(8,128)S(1)}, f32[32,128]{1,0:T(8,128)S(1)}, u32[]{:S(2)}, u32[]{:S(2)}) collective-permute-start(f32[32,128]{1,0:T(8,128)S(1)} %add_add_fusion), channel_id=1, source_target_pairs={{0,128},{32,160},{64,192},{96,224},{128,0},{160,32},{192,64},{224,... | collective-permute-start | bytes 49160 | tf_op jit(solution)/shard_map/ppermute | solution.py:460
  67.0 1.4 %collective-permute-done.19 = f32[32,128]{1,0:T(8,128)S(1)} collective-permute-done((f32[32,128]{1,0:T(8,128)S(1)}, f32[32,128]{1,0:T(8,128)S(1)}, u32[]{:S(2)}, u32[]{:S(2)}) %collective-permute-start.19) | collective-permute-done | bytes 16416 | tf_op jit(solution)/shard_map/ppermute | solution.py:460
  68.4 5.0 %collective-permute-start.20 = (f32[32,128]{1,0:T(8,128)S(1)}, f32[32,128]{1,0:T(8,128)S(1)}, u32[]{:S(2)}, u32[]{:S(2)}) collective-permute-start(f32[32,128]{1,0:T(8,128)S(1)} %add.15.mine), channel_id=1, source_target_pairs={{0,1},{1,0},{2,3},{3,2},{4,5},{5,4},{6,7},{7,6},{8,9},{9,8},{10,11... | collective-permute-start | bytes 49160 | tf_op jit(solution)/shard_map/ppermute | solution.py:460
  73.4 1.2 %finish_rows.1 = (bf16[128,2048]{1,0:T(8,128)(2,1)}, bf16[128,2048]{1,0:T(8,128)(2,1)}, bf16[128,2048]{1,0:T(8,128)(2,1)}) custom-call(s32[1]{0:T(128)} %bitcast.c_ref, bf16[192,128]{1,0:T(8,128)(2,1)S(1)} %get-tuple-element.52.z0.y0, ...), custom_call_target="tpu_custom_call", output_to_operand_aliasing={{0}: (18, {}), {1}: (19, {}), {2}: (20, {})} | custom-call | tf_op jit(solution)/shard_map/finish_rows/pallas_call | solution.py:572
  74.7 0.6 last_sum.1
  (25 shorter events, 1.2 us)
Async XLA Ops:
  1.7 5.6 %collective-permute-start.2 = (bf16[640,128]{1,0:T(8,128)(2,1)S(1)}, bf16[640,128]{1,0:T(8,128)(2,1)S(1)}, u32[]{:S(2)}, u32[]{:S(2)}) collective-permute-start(bf16[640,128]{1,0:T(8,128)(2,1)S(1)} %get-tuple-element.40.f1), channel_id=1, source_target_pairs={{0,2},{1,3},{2,0},{3,1},{4,6},{5,7},{6,4},{7,5},{8,10},{9,11},{10,... | collective-permute-start | bytes 491528 | tf_op jit(solution)/shard_map/ppermute | solution.py:460
  4.2 4.4 %collective-permute-start = (bf16[128,128]{1,0:T(8,128)(2,1)S(1)}, bf16[128,128]{1,0:T(8,128)(2,1)S(1)}, u32[]{:S(2)}, u32[]{:S(2)}) collective-permute-start(bf16[128,128]{1,0:T(8,128)(2,1)S(1)} %get-tuple-element.38.f2), channel_id=1, source_target_pairs={{0,4},{1,5},{2,6},{3,7},{4,0},{5,1},{6,2},{7,3},{8,12},{9,13},{10,... | collective-permute-start | bytes 98312 | tf_op jit(solution)/shard_map/ppermute | solution.py:460
  7.2 5.0 %collective-permute-start.1 = (bf16[128,128]{1,0:T(8,128)(2,1)S(1)}, bf16[128,128]{1,0:T(8,128)(2,1)S(1)}, u32[]{:S(2)}, u32[]{:S(2)}) collective-permute-start(bf16[128,128]{1,0:T(8,128)(2,1)S(1)} %get-tuple-element.39.f3), channel_id=1, source_target_pairs={{0,6},{1,7},{2,4},{3,5},{4,2},{5,3},{6,0},{7,1},{8,14},{9,15},{10,... | collective-permute-start | bytes 98312 | tf_op jit(solution)/shard_map/ppermute | solution.py:460
  12.2 9.4 %copy-start = (f32[2048]{0:T(1024)S(1)}, f32[2048]{0:T(1024)}, u32[]{:S(2)}) copy-start(f32[2048]{0:T(1024)} %param.11) | copy-start | bytes 24580
  12.2 9.4 %copy-start.1 = (f32[2048]{0:T(1024)S(1)}, f32[2048]{0:T(1024)}, u32[]{:S(2)}) copy-start(f32[2048]{0:T(1024)} %param.10) | copy-start | bytes 24580
  12.4 14.3 %collective-permute-start.7 = (bf16[512,128]{1,0:T(8,128)(2,1)S(1)}, bf16[512,128]{1,0:T(8,128)(2,1)S(1)}, u32[]{:S(2)}, u32[]{:S(2)}) collective-permute-start(bf16[512,128]{1,0:T(8,128)(2,1)S(1)} %pack_far_rows.1), channel_id=1, source_target_pairs={{0,16},{1,17},{2,18},{3,19},{4,20},{5,21},{6,22},{7,23},{8,24},{9,... | collective-permute-start | bytes 393224 | tf_op jit(solution)/shard_map/ppermute | solution.py:460
  15.3 11.5 %collective-permute-start.6 = (bf16[512,128]{1,0:T(8,128)(2,1)S(1)}, bf16[512,128]{1,0:T(8,128)(2,1)S(1)}, u32[]{:S(2)}, u32[]{:S(2)}) collective-permute-start(bf16[512,128]{1,0:T(8,128)(2,1)S(1)} %pack_far_rows.1), channel_id=1, source_target_pairs={{0,12},{1,13},{2,14},{3,15},{4,8},{5,9},{6,10},{7,11},{8,4},{9,5},... | collective-permute-start | bytes 393224 | tf_op jit(solution)/shard_map/ppermute | solution.py:460
  18.0 8.8 %collective-permute-start.5 = (bf16[512,128]{1,0:T(8,128)(2,1)S(1)}, bf16[512,128]{1,0:T(8,128)(2,1)S(1)}, u32[]{:S(2)}, u32[]{:S(2)}) collective-permute-start(bf16[512,128]{1,0:T(8,128)(2,1)S(1)} %pack_far_rows.1), channel_id=1, source_target_pairs={{0,28},{1,29},{2,30},{3,31},{4,24},{5,25},{6,26},{7,27},{8,20},{9,... | collective-permute-start | bytes 393224 | tf_op jit(solution)/shard_map/ppermute | solution.py:460
  18.8 8.7 %collective-permute-start.3 = (bf16[512,128]{1,0:T(8,128)(2,1)S(1)}, bf16[512,128]{1,0:T(8,128)(2,1)S(1)}, u32[]{:S(2)}, u32[]{:S(2)}) collective-permute-start(bf16[512,128]{1,0:T(8,128)(2,1)S(1)} %get-tuple-element.42.m2), channel_id=1, source_target_pairs={{0,4},{1,5},{2,6},{3,7},{4,0},{5,1},{6,2},{7,3},{8,12},{9,13},{10,... | collective-permute-start | bytes 393224 | tf_op jit(solution)/shard_map/ppermute | solution.py:460
  19.9 8.2 %collective-permute-start.4 = (bf16[512,128]{1,0:T(8,128)(2,1)S(1)}, bf16[512,128]{1,0:T(8,128)(2,1)S(1)}, u32[]{:S(2)}, u32[]{:S(2)}) collective-permute-start(bf16[512,128]{1,0:T(8,128)(2,1)S(1)} %get-tuple-element.43.m3), channel_id=1, source_target_pairs={{0,6},{1,7},{2,4},{3,5},{4,2},{5,3},{6,0},{7,1},{8,14},{9,15},{10,... | collective-permute-start | bytes 393224 | tf_op jit(solution)/shard_map/ppermute | solution.py:460
  30.3 16.3 %collective-permute-start.8 = (bf16[576,128]{1,0:T(8,128)(2,1)S(1)}, bf16[576,128]{1,0:T(8,128)(2,1)S(1)}, u32[]{:S(2)}, u32[]{:S(2)}) collective-permute-start(bf16[576,128]{1,0:T(8,128)(2,1)S(1)} %get-tuple-element.48), channel_id=1, source_target_pairs={{0,28},{1,29},{2,30},{3,31},{4,24},{5,25},{6,26},{7,27},{8,20},{9,... | collective-permute-start | bytes 442376 | tf_op jit(solution)/shard_map/ppermute | solution.py:460
  39.7 10.2 %collective-permute-start.9 = (bf16[576,128]{1,0:T(8,128)(2,1)S(1)}, bf16[576,128]{1,0:T(8,128)(2,1)S(1)}, u32[]{:S(2)}, u32[]{:S(2)}) collective-permute-start(bf16[576,128]{1,0:T(8,128)(2,1)S(1)} %get-tuple-element.49), channel_id=1, source_target_pairs={{0,12},{1,13},{2,14},{3,15},{4,8},{5,9},{6,10},{7,11},{8,4},{9,5},... | collective-permute-start | bytes 442376 | tf_op jit(solution)/shard_map/ppermute | solution.py:460
  39.7 10.2 %collective-permute-start.10 = (bf16[576,128]{1,0:T(8,128)(2,1)S(1)}, bf16[576,128]{1,0:T(8,128)(2,1)S(1)}, u32[]{:S(2)}, u32[]{:S(2)}) collective-permute-start(bf16[576,128]{1,0:T(8,128)(2,1)S(1)} %get-tuple-element.50), channel_id=1, source_target_pairs={{0,16},{1,17},{2,18},{3,19},{4,20},{5,21},{6,22},{7,23},{8,24},{9,... | collective-permute-start | bytes 442376 | tf_op jit(solution)/shard_map/ppermute | solution.py:460
  50.0 8.4 %collective-permute-start.13 = (bf16[576,128]{1,0:T(8,128)(2,1)S(1)}, bf16[576,128]{1,0:T(8,128)(2,1)S(1)}, u32[]{:S(2)}, u32[]{:S(2)}) collective-permute-start(bf16[576,128]{1,0:T(8,128)(2,1)S(1)} %get-tuple-element.55), channel_id=1, source_target_pairs={{0,2},{1,3},{2,0},{3,1},{4,6},{5,7},{6,4},{7,5},{8,10},{9,11},{10,... | collective-permute-start | bytes 442376 | tf_op jit(solution)/shard_map/ppermute | solution.py:460
  52.9 4.4 %collective-permute-start.11 = (bf16[192,128]{1,0:T(8,128)(2,1)S(1)}, bf16[192,128]{1,0:T(8,128)(2,1)S(1)}, u32[]{:S(2)}, u32[]{:S(2)}) collective-permute-start(bf16[192,128]{1,0:T(8,128)(2,1)S(1)} %get-tuple-element.53), channel_id=1, source_target_pairs={{0,4},{1,5},{2,6},{3,7},{4,0},{5,1},{6,2},{7,3},{8,12},{9,13},{10,... | collective-permute-start | bytes 147464 | tf_op jit(solution)/shard_map/ppermute | solution.py:460
  53.2 5.3 %collective-permute-start.12 = (bf16[192,128]{1,0:T(8,128)(2,1)S(1)}, bf16[192,128]{1,0:T(8,128)(2,1)S(1)}, u32[]{:S(2)}, u32[]{:S(2)}) collective-permute-start(bf16[192,128]{1,0:T(8,128)(2,1)S(1)} %get-tuple-element.54), channel_id=1, source_target_pairs={{0,6},{1,7},{2,4},{3,5},{4,2},{5,3},{6,0},{7,1},{8,14},{9,15},{10,... | collective-permute-start | bytes 147464 | tf_op jit(solution)/shard_map/ppermute | solution.py:460
  58.4 5.7 %collective-permute-start.18 = (f32[32,128]{1,0:T(8,128)S(1)}, f32[32,128]{1,0:T(8,128)S(1)}, u32[]{:S(2)}, u32[]{:S(2)}) collective-permute-start(f32[32,128]{1,0:T(8,128)S(1)} %sum_gains.1), channel_id=1, source_target_pairs={{0,96},{32,64},{64,32},{96,0},{128,224},{160,192},{192,160},{224,1... | collective-permute-start | bytes 49160 | tf_op jit(solution)/shard_map/ppermute | solution.py:460
  61.3 4.1 %collective-permute-start.17 = (f32[32,128]{1,0:T(8,128)S(1)}, f32[32,128]{1,0:T(8,128)S(1)}, u32[]{:S(2)}, u32[]{:S(2)}) collective-permute-start(f32[32,128]{1,0:T(8,128)S(1)} %sum_gains.1), channel_id=1, source_target_pairs={{0,64},{32,96},{64,0},{96,32},{128,192},{160,224},{192,128},{224,1... | collective-permute-start | bytes 49160 | tf_op jit(solution)/shard_map/ppermute | solution.py:460
  61.6 3.7 %collective-permute-start.16 = (f32[32,128]{1,0:T(8,128)S(1)}, f32[32,128]{1,0:T(8,128)S(1)}, u32[]{:S(2)}, u32[]{:S(2)}) collective-permute-start(f32[32,128]{1,0:T(8,128)S(1)} %sum_gains.1), channel_id=1, source_target_pairs={{0,32},{32,0},{64,96},{96,64},{128,160},{160,128},{192,224},{224,1... | collective-permute-start | bytes 49160 | tf_op jit(solution)/shard_map/ppermute | solution.py:460
  62.0 11.5 %collective-permute-start.14 = (bf16[384,128]{1,0:T(8,128)(2,1)S(1)}, bf16[384,128]{1,0:T(8,128)(2,1)S(1)}, u32[]{:S(2)}, u32[]{:S(2)}) collective-permute-start(bf16[384,128]{1,0:T(8,128)(2,1)S(1)} %get-tuple-element.57), channel_id=1, source_target_pairs={{0,4},{1,5},{2,6},{3,7},{4,0},{5,1},{6,2},{7,3},{8,12},{9,13},{10,... | collective-permute-start | bytes 294920 | tf_op jit(solution)/shard_map/ppermute | solution.py:460
  62.8 10.7 %collective-permute-start.15 = (bf16[384,128]{1,0:T(8,128)(2,1)S(1)}, bf16[384,128]{1,0:T(8,128)(2,1)S(1)}, u32[]{:S(2)}, u32[]{:S(2)}) collective-permute-start(bf16[384,128]{1,0:T(8,128)(2,1)S(1)} %get-tuple-element.58), channel_id=1, source_target_pairs={{0,6},{1,7},{2,4},{3,5},{4,2},{5,3},{6,0},{7,1},{8,14},{9,15},{10,... | collective-permute-start | bytes 294920 | tf_op jit(solution)/shard_map/ppermute | solution.py:460
  65.4 3.0 %collective-permute-start.19 = (f32[32,128]{1,0:T(8,128)S(1)}, f32[32,128]{1,0:T(8,128)S(1)}, u32[]{:S(2)}, u32[]{:S(2)}) collective-permute-start(f32[32,128]{1,0:T(8,128)S(1)} %add_add_fusion), channel_id=1, source_target_pairs={{0,128},{32,160},{64,192},{96,224},{128,0},{160,32},{192,64},{224,... | collective-permute-start | bytes 49160 | tf_op jit(solution)/shard_map/ppermute | solution.py:460
  68.4 6.2 %collective-permute-start.20 = (f32[32,128]{1,0:T(8,128)S(1)}, f32[32,128]{1,0:T(8,128)S(1)}, u32[]{:S(2)}, u32[]{:S(2)}) collective-permute-start(f32[32,128]{1,0:T(8,128)S(1)} %add.15.mine), channel_id=1, source_target_pairs={{0,1},{1,0},{2,3},{3,2},{4,5},{5,4},{6,7},{7,6},{8,9},{9,8},{10,11... | collective-permute-start | bytes 49160 | tf_op jit(solution)/shard_map/ppermute | solution.py:460

commit v4 on v3

--- a/solution.py
+++ b/solution.py
@@ -119,7 +119,7 @@
     return ref[at : at + 32, :].astype(F32) + ref[at + 32 : at + 64, :].astype(F32)
 
 
-def forward_pack_kernel(f0, f2, f3, f1, ready, out, sems):
+def forward_pack_kernel(f0, f3, f2, f1, ready, out, sems):
     copies = []
     for k, src in enumerate((f0, f2, f1, f3)):
         copy = pltpu.make_async_copy(
@@ -206,7 +206,7 @@
 
 
 def owner_kernel(
-    c_ref, f0, f2, f3, f1, r0, r2, r3, b3, b2, b1, q_gain, k_gain, home_gains,
+    c_ref, f0, f3, f2, f1, r0, r2, r3, b3, b2, b1, q_gain, k_gain, home_gains,
     x0, x1, x2, x3, t1, t2, t3, far_k, far_v, gains_out, gains,
 ):
     c = c_ref[0]
@@ -379,6 +379,14 @@
     out[...] = (joined_gains(y0) + joined_gains(y1)) + (joined_gains(y2) + joined_gains(y3))
 
 
+def after_kernel(x, *refs):
+    refs[-1][...] = x[...]
+
+
+def pair_sum_kernel(mine, other, ready, out):
+    out[...] = mine[...] + other[...]
+
+
 def last_sum_kernel(mine, other, q_out, k_out):
     q_out[...] = mine[0:HEADS, :] + other[0:HEADS, :]
     k_out[...] = mine[HEADS:, :] + other[HEADS:, :]
@@ -387,7 +395,7 @@
 def final_kernel(
     c_ref, z0, z2, z3, z1, y0, y2, y3, f0, f1, f2, f3, m0, m2, m3,
     part_k, part_v, k_gain, gq_in, gk_in, gv_in,
-    gq_out, gk_out, gv_out, done_k, done_v, sems,
+    gq_out, gk_out, gv_out, ready, done_k, done_v, sems,
 ):
     c = c_ref[0]
     core, zl, zh, xh = place(c)
@@ -438,6 +446,7 @@
     for (n, sem, part, h, e, back, at, raw), x in zip(jobs, done):
         done_k[n] = x
         send(done_k.at[n], gk_out, e, h, sem)
+    ready[...] = jnp.zeros_like(ready)
     for copy in copies:
         copy.wait()
 
@@ -511,7 +520,7 @@
         scratch_shapes=[pltpu.SemaphoreType.DMA((4,))],
         compiler_params=params,
         name="pack_far_rows",
-    )(*by_distance(early), packed_late[0])
+    )(early[0], early[3], early[2], early[1], packed_late[0])
     moved = {mask: swap(onward, "ctx", mask) for mask in (16, 12, 28)}
     crossed = [moved[mask] for mask in steps]
 
@@ -526,7 +535,7 @@
         scratch_shapes=[pltpu.VMEM((2 * HEADS, HD), F32)],
         compiler_params=params,
         name="owned_heads",
-    )(here, *by_distance(early), *late, crossed[2], crossed[1], crossed[0], qg, kg, home_gains)
+    )(here, early[0], early[3], early[2], early[1], *late, crossed[2], crossed[1], crossed[0], qg, kg, home_gains)
     back_early, terms, far_k, far_v, own_gains = outs[:4], outs[4:7], outs[7], outs[8], outs[9]
     moved = {mask: swap(terms[steps.index(mask)], "ctx", mask) for mask in (28, 12, 16)}
     terms_in = [moved[mask] for mask in steps]
@@ -536,7 +545,7 @@
 
     def quad_sum(x, axis, mask):
         one, two, three = (swap(x, axis, i * mask) for i in (1, 2, 3))
-        return (x + one) + (two + three)
+        return (x + one) + (three + two)
 
     home_early = [back_early[0], swap(back_early[2], "ctx", 4), swap(back_early[3], "ctx", 6)]
     waits = ()
@@ -548,6 +557,15 @@
         compiler_params=params,
         name="add_far_terms",
     )(far_k, far_v, own_gains, *terms_in[::-1], back_early[1], *waits)
+    back_late = list(back_late)
+    back_late[2] = pl.pallas_call(
+        after_kernel,
+        in_specs=[vmem_spec()] + [any_spec()] * 2,
+        out_specs=vmem_spec(),
+        out_shape=shape(back_late[2].shape, BF),
+        compiler_params=params,
+        name="after_early",
+    )(back_late[2], home_early[1], home_early[2])
     home_late = around(back_late)
 
     gains = pl.pallas_call(
@@ -559,7 +577,28 @@
         name="sum_gains",
     )(*by_distance(home_late))
     gains = quad_sum(gains, "dp", 1)
-    gains = pair_sum(gains, "dp", 4)
+    other_gains = swap(gains, "dp", 4)
+    gq, gk, gv, ready = pl.pallas_call(
+        final_kernel,
+        in_specs=[smem_spec()] + [vmem_spec()] * 17 + [any_spec()] * 3,
+        out_specs=[any_spec()] * 3 + [vmem_spec()],
+        out_shape=[shape((ROWS, HEADS * HD), BF)] * 3 + [shape((8, HD), F32)],
+        scratch_shapes=[pltpu.VMEM((12, TILE, HD), BF)] * 2 + [pltpu.SemaphoreType.DMA((32,))],
+        input_output_aliases={18: 0, 19: 1, 20: 2},
+        compiler_params=params,
+        name="finish_rows",
+    )(
+        here, *by_distance(home_late), *home_early, *packed_early, *packed_late,
+        part_k, part_v, kg, gq_home, gk_home, gv_home,
+    )
+    gains = pl.pallas_call(
+        pair_sum_kernel,
+        in_specs=[vmem_spec()] * 3,
+        out_specs=vmem_spec(),
+        out_shape=shape((2 * HEADS, HD), F32),
+        compiler_params=params,
+        name="pair_sum",
+    )(gains, other_gains, ready)
     q_sum, k_sum = pl.pallas_call(
         last_sum_kernel,
         in_specs=[vmem_spec()] * 2,
@@ -569,19 +608,6 @@
         name="last_sum",
     )(gains, swap(gains, "ctx", 1))
 
-    gq, gk, gv = pl.pallas_call(
-        final_kernel,
-        in_specs=[smem_spec()] + [vmem_spec()] * 17 + [any_spec()] * 3,
-        out_specs=[any_spec()] * 3,
-        out_shape=[shape((ROWS, HEADS * HD), BF)] * 3,
-        scratch_shapes=[pltpu.VMEM((12, TILE, HD), BF)] * 2 + [pltpu.SemaphoreType.DMA((32,))],
-        input_output_aliases={18: 0, 19: 1, 20: 2},
-        compiler_params=params,
-        name="finish_rows",
-    )(
-        here, *by_distance(home_late), *home_early, *packed_early, *packed_late,
-        part_k, part_v, kg, gq_home, gk_home, gv_home,
-    )
     whole = lambda a: a.reshape(1, ROWS, HEADS * HD)
     return (
         whole(gq),

time: 75.5 us -> 74.6 us (0.988)
  starting transfers between devices: 41.9 us -> 40.8 us
    ppermute x21, starting transfers between devices: 41.9 us -> 40.8 us  [swap(): return lax.ppermute(block, axis, [(i, i ^ mask) for i in range(count)])]
  transfers between devices with their start and end apart: 21 -> 21, of which waited for: 10 -> 9; matrix products, arithmetic and copies ran while one was open for 0% -> 0% of each run, Pallas kernels for 10% -> 10%
where the time goes in v4:
time: 74.6 us; the launch traced here: 74.3 us
  starting transfers between devices  40.8 us (55%)
  waiting for transfers between devices  21.1 us (28%)
  Pallas kernels  11.6 us (16%)
    ppermute x21, starting transfers between devices, swap(): return lax.ppermute(block, axis, [(i, i ^ mask) for i in range(count)])  40.8 us
    ppermute x21, waiting for transfers between devices, swap(): return lax.ppermute(block, axis, [(i, i ^ mask) for i in range(count)])  21.1 us
    pallas_call x1, Pallas kernels, per_device(): pl.pallas_call(home_kernel, in_specs=[smem_spec()] + [hbm_spec()] * 4 + [...  5.18 us
    pallas_call x2, Pallas kernels, pack_call(): pl.pallas_call(functools.partial(pack_kernel, plan), in_specs=[smem_spec(...  2.21 us
    pallas_call x1, Pallas kernels, per_device(): pl.pallas_call(owner_kernel, in_specs=[smem_spec()] + [vmem_spec()] * 13,...  2.13 us
  transfers between devices with their start and end apart: 21, of which 9 were waited for; matrix products, arithmetic and copies ran while one was open for 0% of the time, Pallas kernels for 10%

profile of v4, /device:TPU:1, one launch (start us, length us, event | category | flops | bytes accessed | tf_op | source)
XLA Modules:
  0.0 74.3 jit_solution(2980310616313248789)
XLA Ops:
  0.6 1.0 %pack_early.1 = (bf16[128,128]{1,0:T(8,128)(2,1)S(1)}, bf16[640,128]{1,0:T(8,128)(2,1)S(1)}, bf16[128,128]{1,0:T(8,128)(2,1)S(1)}, bf16[128,128]{1,0:T(8,128)(2,1)S(1)}) custom-call(s32[1]{0:T(128)} %bitcast.c_ref, bf16[128,2048]{1,0:T(8,128)(2,1)} %bitcast.17, bf16[128,2048]{1,0:T(8,128)(2,1)} %bitcast.20, bf16[128,2048]{1,0:T(8,128)(2,1)} %bitcast.23, ...), custom_call_target="tpu_custom_call" | custom-call | tf_op jit(solution)/shard_map/pack_early/pallas_call | solution.py:481
  1.7 2.6 %collective-permute-start.2 = (bf16[640,128]{1,0:T(8,128)(2,1)S(1)}, bf16[640,128]{1,0:T(8,128)(2,1)S(1)}, u32[]{:S(2)}, u32[]{:S(2)}) collective-permute-start(bf16[640,128]{1,0:T(8,128)(2,1)S(1)} %get-tuple-element.41.f1), channel_id=1, source_target_pairs={{0,2},{1,3},{2,0},{3,1},{4,6},{5,7},{6,4},{7,5},{8,10},{9,11},{10,... | collective-permute-start | bytes 491528 | tf_op jit(solution)/shard_map/ppermute | solution.py:469
  4.2 2.8 %collective-permute-start = (bf16[128,128]{1,0:T(8,128)(2,1)S(1)}, bf16[128,128]{1,0:T(8,128)(2,1)S(1)}, u32[]{:S(2)}, u32[]{:S(2)}) collective-permute-start(bf16[128,128]{1,0:T(8,128)(2,1)S(1)} %get-tuple-element.39.f3), channel_id=1, source_target_pairs={{0,6},{1,7},{2,4},{3,5},{4,2},{5,3},{6,0},{7,1},{8,14},{9,15},{10,... | collective-permute-start | bytes 98312 | tf_op jit(solution)/shard_map/ppermute | solution.py:469
  7.2 1.2 %pack_late.1 = (bf16[512,128]{1,0:T(8,128)(2,1)S(1)}, bf16[512,128]{1,0:T(8,128)(2,1)S(1)}, bf16[512,128]{1,0:T(8,128)(2,1)S(1)}) custom-call(s32[1]{0:T(128)} %bitcast.c_ref, bf16[128,2048]{1,0:T(8,128)(2,1)} %bitcast.18, bf16[128,2048]{1,0:T(8,128)(2,1)} %bitcast.21, bf16[128,2048]{1,0:T(8,128)(2,1)} %bitcast.24, bf16[128,2048]{1,0:T(8,128)(2,1)} %bitcast.27, ...), custom_call_target="tpu_custom_call" | custom-call | tf_op jit(solution)/shard_map/pack_late/pallas_call | solution.py:481
  8.4 2.8 %collective-permute-done.f3 = bf16[128,128]{1,0:T(8,128)(2,1)S(1)} collective-permute-done((bf16[128,128]{1,0:T(8,128)(2,1)S(1)}, bf16[128,128]{1,0:T(8,128)(2,1)S(1)}, u32[]{:S(2)}, u32[]{:S(2)}) %collective-permute-start) | collective-permute-done | bytes 32800 | tf_op jit(solution)/shard_map/ppermute | solution.py:469
  11.4 2.8 %collective-permute-start.7 = (bf16[512,128]{1,0:T(8,128)(2,1)S(1)}, bf16[512,128]{1,0:T(8,128)(2,1)S(1)}, u32[]{:S(2)}, u32[]{:S(2)}) collective-permute-start(bf16[512,128]{1,0:T(8,128)(2,1)S(1)} %pack_far_rows.1), channel_id=1, source_target_pairs={{0,16},{1,17},{2,18},{3,19},{4,20},{5,21},{6,22},{7,23},{8,24},{9,... | collective-permute-start | bytes 393224 | tf_op jit(solution)/shard_map/ppermute | solution.py:469
  14.2 4.1 %collective-permute-start.6 = (bf16[512,128]{1,0:T(8,128)(2,1)S(1)}, bf16[512,128]{1,0:T(8,128)(2,1)S(1)}, u32[]{:S(2)}, u32[]{:S(2)}) collective-permute-start(bf16[512,128]{1,0:T(8,128)(2,1)S(1)} %pack_far_rows.1), channel_id=1, source_target_pairs={{0,12},{1,13},{2,14},{3,15},{4,8},{5,9},{6,10},{7,11},{8,4},{9,5},... | collective-permute-start | bytes 393224 | tf_op jit(solution)/shard_map/ppermute | solution.py:469
  18.3 1.1 %collective-permute-start.3 = (bf16[512,128]{1,0:T(8,128)(2,1)S(1)}, bf16[512,128]{1,0:T(8,128)(2,1)S(1)}, u32[]{:S(2)}, u32[]{:S(2)}) collective-permute-start(bf16[512,128]{1,0:T(8,128)(2,1)S(1)} %get-tuple-element.43.m2), channel_id=1, source_target_pairs={{0,4},{1,5},{2,6},{3,7},{4,0},{5,1},{6,2},{7,3},{8,12},{9,13},{10,... | collective-permute-start | bytes 393224 | tf_op jit(solution)/shard_map/ppermute | solution.py:469
  19.3 1.6 %collective-permute-start.4 = (bf16[512,128]{1,0:T(8,128)(2,1)S(1)}, bf16[512,128]{1,0:T(8,128)(2,1)S(1)}, u32[]{:S(2)}, u32[]{:S(2)}) collective-permute-start(bf16[512,128]{1,0:T(8,128)(2,1)S(1)} %get-tuple-element.44.m3), channel_id=1, source_target_pairs={{0,6},{1,7},{2,4},{3,5},{4,2},{5,3},{6,0},{7,1},{8,14},{9,15},{10,... | collective-permute-start | bytes 393224 | tf_op jit(solution)/shard_map/ppermute | solution.py:469
  21.0 5.2 %home_slab.1 = (bf16[128,2048]{1,0:T(8,128)(2,1)}, bf16[128,2048]{1,0:T(8,128)(2,1)}, bf16[128,2048]{1,0:T(8,128)(2,1)}, f32[12,64,128]{2,1,0:T(8,128)S(1)}, f32...) custom-call(s32[1]{0:T(128)} %bitcast.c_ref, bf16[128,2048]{1,0:T(8,128)(2,1)} %bitcast.19, bf16[128,2048]{1,0:T(8,128)(2,1)} %bitcast.22, ...), custom_call_target="tpu_custom_call" | custom-call | tf_op jit(solution)/shard_map/home_slab/pallas_call | solution.py:496
  26.2 2.7 %collective-permute-done.5.b3 = bf16[512,128]{1,0:T(8,128)(2,1)S(1)} collective-permute-done((bf16[512,128]{1,0:T(8,128)(2,1)S(1)}, bf16[512,128]{1,0:T(8,128)(2,1)S(1)}, u32[]{:S(2)}, u32[]{:S(2)}) %collective-permute-start.5) | collective-permute-done | bytes 131104 | tf_op jit(solution)/shard_map/ppermute | solution.py:469
  28.9 2.1 %owned_heads.1 = (bf16[384,128]{1,0:T(8,128)(2,1)S(1)}, bf16[384,128]{1,0:T(8,128)(2,1)S(1)}, bf16[384,128]{1,0:T(8,128)(2,1)S(1)}, bf16[384,128]{1,0:T(8,128)(2...) custom-call(s32[1]{0:T(128)} %bitcast.c_ref, ...), custom_call_target="tpu_custom_call" | custom-call | tf_op jit(solution)/shard_map/owned_heads/pallas_call | solution.py:527
  31.1 7.0 %collective-permute-start.8 = (bf16[576,128]{1,0:T(8,128)(2,1)S(1)}, bf16[576,128]{1,0:T(8,128)(2,1)S(1)}, u32[]{:S(2)}, u32[]{:S(2)}) collective-permute-start(bf16[576,128]{1,0:T(8,128)(2,1)S(1)} %get-tuple-element.49), channel_id=1, source_target_pairs={{0,28},{1,29},{2,30},{3,31},{4,24},{5,25},{6,26},{7,27},{8,20},{9,... | collective-permute-start | bytes 442376 | tf_op jit(solution)/shard_map/ppermute | solution.py:469
  38.1 0.4 collective-permute-start.10
  38.5 2.2 %collective-permute-start.11 = (bf16[384,128]{1,0:T(8,128)(2,1)S(1)}, bf16[384,128]{1,0:T(8,128)(2,1)S(1)}, u32[]{:S(2)}, u32[]{:S(2)}) collective-permute-start(bf16[384,128]{1,0:T(8,128)(2,1)S(1)} %get-tuple-element.55), channel_id=1, source_target_pairs={{0,4},{1,5},{2,6},{3,7},{4,0},{5,1},{6,2},{7,3},{8,12},{9,13},{10,... | collective-permute-start | bytes 294920 | tf_op jit(solution)/shard_map/ppermute | solution.py:469
  40.7 1.8 %collective-permute-start.12 = (bf16[384,128]{1,0:T(8,128)(2,1)S(1)}, bf16[384,128]{1,0:T(8,128)(2,1)S(1)}, u32[]{:S(2)}, u32[]{:S(2)}) collective-permute-start(bf16[384,128]{1,0:T(8,128)(2,1)S(1)} %get-tuple-element.56), channel_id=1, source_target_pairs={{0,6},{1,7},{2,4},{3,5},{4,2},{5,3},{6,0},{7,1},{8,14},{9,15},{10,... | collective-permute-start | bytes 294920 | tf_op jit(solution)/shard_map/ppermute | solution.py:469
  42.4 6.9 %collective-permute-done.9.u2 = bf16[576,128]{1,0:T(8,128)(2,1)S(1)} collective-permute-done((bf16[576,128]{1,0:T(8,128)(2,1)S(1)}, bf16[576,128]{1,0:T(8,128)(2,1)S(1)}, u32[]{:S(2)}, u32[]{:S(2)}) %collective-permute-start.9) | collective-permute-done | bytes 147488 | tf_op jit(solution)/shard_map/ppermute | solution.py:469
  49.5 1.6 %collective-permute-start.15 = (bf16[576,128]{1,0:T(8,128)(2,1)S(1)}, bf16[576,128]{1,0:T(8,128)(2,1)S(1)}, u32[]{:S(2)}, u32[]{:S(2)}) collective-permute-start(bf16[576,128]{1,0:T(8,128)(2,1)S(1)} %get-tuple-element.58), channel_id=1, source_target_pairs={{0,2},{1,3},{2,0},{3,1},{4,6},{5,7},{6,4},{7,5},{8,10},{9,11},{10,... | collective-permute-start | bytes 442376 | tf_op jit(solution)/shard_map/ppermute | solution.py:469
  51.1 1.4 %collective-permute-start.13 = (bf16[192,128]{1,0:T(8,128)(2,1)S(1)}, bf16[192,128]{1,0:T(8,128)(2,1)S(1)}, u32[]{:S(2)}, u32[]{:S(2)}) collective-permute-start(bf16[192,128]{1,0:T(8,128)(2,1)S(1)} %after_early.1), channel_id=1, source_target_pairs={{0,4},{1,5},{2,6},{3,7},{4,0},{5,1},{6,2},{7,3},{8,12},{9,13},{10,... | collective-permute-start | bytes 147464 | tf_op jit(solution)/shard_map/ppermute | solution.py:469
  52.5 1.1 %collective-permute-start.14 = (bf16[192,128]{1,0:T(8,128)(2,1)S(1)}, bf16[192,128]{1,0:T(8,128)(2,1)S(1)}, u32[]{:S(2)}, u32[]{:S(2)}) collective-permute-start(bf16[192,128]{1,0:T(8,128)(2,1)S(1)} %get-tuple-element.57), channel_id=1, source_target_pairs={{0,6},{1,7},{2,4},{3,5},{4,2},{5,3},{6,0},{7,1},{8,14},{9,15},{10,... | collective-permute-start | bytes 147464 | tf_op jit(solution)/shard_map/ppermute | solution.py:469
  53.6 1.5 %collective-permute-done.13.z2.y2 = bf16[192,128]{1,0:T(8,128)(2,1)S(1)} collective-permute-done((bf16[192,128]{1,0:T(8,128)(2,1)S(1)}, bf16[192,128]{1,0:T(8,128)(2,1)S(1)}, u32[]{:S(2)}, u32[]{:S(2)}) %collective-permute-start.13) | collective-permute-done | bytes 49184 | tf_op jit(solution)/shard_map/ppermute | solution.py:469
  55.0 2.4 %collective-permute-done.14.z3.y3 = bf16[192,128]{1,0:T(8,128)(2,1)S(1)} collective-permute-done((bf16[192,128]{1,0:T(8,128)(2,1)S(1)}, bf16[192,128]{1,0:T(8,128)(2,1)S(1)}, u32[]{:S(2)}, u32[]{:S(2)}) %collective-permute-start.14) | collective-permute-done | bytes 49184 | tf_op jit(solution)/shard_map/ppermute | solution.py:469
  57.4 3.0 %collective-permute-start.18 = (f32[32,128]{1,0:T(8,128)S(1)}, f32[32,128]{1,0:T(8,128)S(1)}, u32[]{:S(2)}, u32[]{:S(2)}) collective-permute-start(f32[32,128]{1,0:T(8,128)S(1)} %sum_gains.1), channel_id=1, source_target_pairs={{0,64},{32,96},{64,0},{96,32},{128,192},{160,224},{192,128},{224,1... | collective-permute-start | bytes 49160 | tf_op jit(solution)/shard_map/ppermute | solution.py:469
  60.5 0.7 collective-permute-start.17
  61.2 0.4 collective-permute-done.18
  61.6 2.7 %collective-permute-done.17 = f32[32,128]{1,0:T(8,128)S(1)} collective-permute-done((f32[32,128]{1,0:T(8,128)S(1)}, f32[32,128]{1,0:T(8,128)S(1)}, u32[]{:S(2)}, u32[]{:S(2)}) %collective-permute-start.17) | collective-permute-done | bytes 16416 | tf_op jit(solution)/shard_map/ppermute | solution.py:469
  64.3 0.6 collective-permute-start.19
  64.9 1.2 %finish_rows.1 = (bf16[128,2048]{1,0:T(8,128)(2,1)}, bf16[128,2048]{1,0:T(8,128)(2,1)}, bf16[128,2048]{1,0:T(8,128)(2,1)}, f32[8,128]{1,0:T(8,128)S(1)}) custom-call(s32[1]{0:T(128)} %bitcast.c_ref, bf16[192,128]{1,0:T(8,128)(2,1)S(1)} %get-tuple-element.53.z0.y0, ...), custom_call_target="tpu_custom_call", output_to_operand_aliasing={{0}: (18, {}), {1}: (19, {}), {2}: (20, {})} | custom-call | tf_op jit(solution)/shard_map/finish_rows/pallas_call | solution.py:581
  66.1 0.9 %collective-permute-done.19.other = f32[32,128]{1,0:T(8,128)S(1)} collective-permute-done((f32[32,128]{1,0:T(8,128)S(1)}, f32[32,128]{1,0:T(8,128)S(1)}, u32[]{:S(2)}, u32[]{:S(2)}) %collective-permute-start.19) | collective-permute-done | bytes 16416 | tf_op jit(solution)/shard_map/ppermute | solution.py:469
  67.0 5.9 %collective-permute-start.20 = (f32[32,128]{1,0:T(8,128)S(1)}, f32[32,128]{1,0:T(8,128)S(1)}, u32[]{:S(2)}, u32[]{:S(2)}) collective-permute-start(f32[32,128]{1,0:T(8,128)S(1)} %pair_sum.1.mine), channel_id=1, source_target_pairs={{0,1},{1,0},{2,3},{3,2},{4,5},{5,4},{6,7},{7,6},{8,9},{9,8},{10,11... | collective-permute-start | bytes 49160 | tf_op jit(solution)/shard_map/ppermute | solution.py:469
  72.9 0.8 %collective-permute-done.20.other = f32[32,128]{1,0:T(8,128)S(1)} collective-permute-done((f32[32,128]{1,0:T(8,128)S(1)}, f32[32,128]{1,0:T(8,128)S(1)}, u32[]{:S(2)}, u32[]{:S(2)}) %collective-permute-start.20) | collective-permute-done | bytes 16416 | tf_op jit(solution)/shard_map/ppermute | solution.py:469
  73.7 0.6 last_sum.1
  (26 shorter events, 0.6 us)
Async XLA Ops:
  1.7 5.6 %collective-permute-start.2 = (bf16[640,128]{1,0:T(8,128)(2,1)S(1)}, bf16[640,128]{1,0:T(8,128)(2,1)S(1)}, u32[]{:S(2)}, u32[]{:S(2)}) collective-permute-start(bf16[640,128]{1,0:T(8,128)(2,1)S(1)} %get-tuple-element.41.f1), channel_id=1, source_target_pairs={{0,2},{1,3},{2,0},{3,1},{4,6},{5,7},{6,4},{7,5},{8,10},{9,11},{10,... | collective-permute-start | bytes 491528 | tf_op jit(solution)/shard_map/ppermute | solution.py:469
  4.2 6.9 %collective-permute-start = (bf16[128,128]{1,0:T(8,128)(2,1)S(1)}, bf16[128,128]{1,0:T(8,128)(2,1)S(1)}, u32[]{:S(2)}, u32[]{:S(2)}) collective-permute-start(bf16[128,128]{1,0:T(8,128)(2,1)S(1)} %get-tuple-element.39.f3), channel_id=1, source_target_pairs={{0,6},{1,7},{2,4},{3,5},{4,2},{5,3},{6,0},{7,1},{8,14},{9,15},{10,... | collective-permute-start | bytes 98312 | tf_op jit(solution)/shard_map/ppermute | solution.py:469
  7.1 4.1 %collective-permute-start.1 = (bf16[128,128]{1,0:T(8,128)(2,1)S(1)}, bf16[128,128]{1,0:T(8,128)(2,1)S(1)}, u32[]{:S(2)}, u32[]{:S(2)}) collective-permute-start(bf16[128,128]{1,0:T(8,128)(2,1)S(1)} %get-tuple-element.40.f2), channel_id=1, source_target_pairs={{0,4},{1,5},{2,6},{3,7},{4,0},{5,1},{6,2},{7,3},{8,12},{9,13},{10,... | collective-permute-start | bytes 98312 | tf_op jit(solution)/shard_map/ppermute | solution.py:469
  11.2 9.8 %copy-start = (f32[2048]{0:T(1024)S(1)}, f32[2048]{0:T(1024)}, u32[]{:S(2)}) copy-start(f32[2048]{0:T(1024)} %param.11) | copy-start | bytes 24580
  11.2 9.8 %copy-start.1 = (f32[2048]{0:T(1024)S(1)}, f32[2048]{0:T(1024)}, u32[]{:S(2)}) copy-start(f32[2048]{0:T(1024)} %param.10) | copy-start | bytes 24580
  11.4 14.8 %collective-permute-start.7 = (bf16[512,128]{1,0:T(8,128)(2,1)S(1)}, bf16[512,128]{1,0:T(8,128)(2,1)S(1)}, u32[]{:S(2)}, u32[]{:S(2)}) collective-permute-start(bf16[512,128]{1,0:T(8,128)(2,1)S(1)} %pack_far_rows.1), channel_id=1, source_target_pairs={{0,16},{1,17},{2,18},{3,19},{4,20},{5,21},{6,22},{7,23},{8,24},{9,... | collective-permute-start | bytes 393224 | tf_op jit(solution)/shard_map/ppermute | solution.py:469
  14.2 12.0 %collective-permute-start.6 = (bf16[512,128]{1,0:T(8,128)(2,1)S(1)}, bf16[512,128]{1,0:T(8,128)(2,1)S(1)}, u32[]{:S(2)}, u32[]{:S(2)}) collective-permute-start(bf16[512,128]{1,0:T(8,128)(2,1)S(1)} %pack_far_rows.1), channel_id=1, source_target_pairs={{0,12},{1,13},{2,14},{3,15},{4,8},{5,9},{6,10},{7,11},{8,4},{9,5},... | collective-permute-start | bytes 393224 | tf_op jit(solution)/shard_map/ppermute | solution.py:469
  18.3 10.6 %collective-permute-start.5 = (bf16[512,128]{1,0:T(8,128)(2,1)S(1)}, bf16[512,128]{1,0:T(8,128)(2,1)S(1)}, u32[]{:S(2)}, u32[]{:S(2)}) collective-permute-start(bf16[512,128]{1,0:T(8,128)(2,1)S(1)} %pack_far_rows.1), channel_id=1, source_target_pairs={{0,28},{1,29},{2,30},{3,31},{4,24},{5,25},{6,26},{7,27},{8,20},{9,... | collective-permute-start | bytes 393224 | tf_op jit(solution)/shard_map/ppermute | solution.py:469
  18.3 10.6 %collective-permute-start.3 = (bf16[512,128]{1,0:T(8,128)(2,1)S(1)}, bf16[512,128]{1,0:T(8,128)(2,1)S(1)}, u32[]{:S(2)}, u32[]{:S(2)}) collective-permute-start(bf16[512,128]{1,0:T(8,128)(2,1)S(1)} %get-tuple-element.43.m2), channel_id=1, source_target_pairs={{0,4},{1,5},{2,6},{3,7},{4,0},{5,1},{6,2},{7,3},{8,12},{9,13},{10,... | collective-permute-start | bytes 393224 | tf_op jit(solution)/shard_map/ppermute | solution.py:469
  19.3 9.6 %collective-permute-start.4 = (bf16[512,128]{1,0:T(8,128)(2,1)S(1)}, bf16[512,128]{1,0:T(8,128)(2,1)S(1)}, u32[]{:S(2)}, u32[]{:S(2)}) collective-permute-start(bf16[512,128]{1,0:T(8,128)(2,1)S(1)} %get-tuple-element.44.m3), channel_id=1, source_target_pairs={{0,6},{1,7},{2,4},{3,5},{4,2},{5,3},{6,0},{7,1},{8,14},{9,15},{10,... | collective-permute-start | bytes 393224 | tf_op jit(solution)/shard_map/ppermute | solution.py:469
  31.1 11.4 %collective-permute-start.8 = (bf16[576,128]{1,0:T(8,128)(2,1)S(1)}, bf16[576,128]{1,0:T(8,128)(2,1)S(1)}, u32[]{:S(2)}, u32[]{:S(2)}) collective-permute-start(bf16[576,128]{1,0:T(8,128)(2,1)S(1)} %get-tuple-element.49), channel_id=1, source_target_pairs={{0,28},{1,29},{2,30},{3,31},{4,24},{5,25},{6,26},{7,27},{8,20},{9,... | collective-permute-start | bytes 442376 | tf_op jit(solution)/shard_map/ppermute | solution.py:469
  38.1 11.3 %collective-permute-start.9 = (bf16[576,128]{1,0:T(8,128)(2,1)S(1)}, bf16[576,128]{1,0:T(8,128)(2,1)S(1)}, u32[]{:S(2)}, u32[]{:S(2)}) collective-permute-start(bf16[576,128]{1,0:T(8,128)(2,1)S(1)} %get-tuple-element.50), channel_id=1, source_target_pairs={{0,12},{1,13},{2,14},{3,15},{4,8},{5,9},{6,10},{7,11},{8,4},{9,5},... | collective-permute-start | bytes 442376 | tf_op jit(solution)/shard_map/ppermute | solution.py:469
  38.1 11.3 %collective-permute-start.10 = (bf16[576,128]{1,0:T(8,128)(2,1)S(1)}, bf16[576,128]{1,0:T(8,128)(2,1)S(1)}, u32[]{:S(2)}, u32[]{:S(2)}) collective-permute-start(bf16[576,128]{1,0:T(8,128)(2,1)S(1)} %get-tuple-element.51), channel_id=1, source_target_pairs={{0,16},{1,17},{2,18},{3,19},{4,20},{5,21},{6,22},{7,23},{8,24},{9,... | collective-permute-start | bytes 442376 | tf_op jit(solution)/shard_map/ppermute | solution.py:469
  38.5 12.6 %collective-permute-start.11 = (bf16[384,128]{1,0:T(8,128)(2,1)S(1)}, bf16[384,128]{1,0:T(8,128)(2,1)S(1)}, u32[]{:S(2)}, u32[]{:S(2)}) collective-permute-start(bf16[384,128]{1,0:T(8,128)(2,1)S(1)} %get-tuple-element.55), channel_id=1, source_target_pairs={{0,4},{1,5},{2,6},{3,7},{4,0},{5,1},{6,2},{7,3},{8,12},{9,13},{10,... | collective-permute-start | bytes 294920 | tf_op jit(solution)/shard_map/ppermute | solution.py:469
  40.7 10.4 %collective-permute-start.12 = (bf16[384,128]{1,0:T(8,128)(2,1)S(1)}, bf16[384,128]{1,0:T(8,128)(2,1)S(1)}, u32[]{:S(2)}, u32[]{:S(2)}) collective-permute-start(bf16[384,128]{1,0:T(8,128)(2,1)S(1)} %get-tuple-element.56), channel_id=1, source_target_pairs={{0,6},{1,7},{2,4},{3,5},{4,2},{5,3},{6,0},{7,1},{8,14},{9,15},{10,... | collective-permute-start | bytes 294920 | tf_op jit(solution)/shard_map/ppermute | solution.py:469
  49.5 8.0 %collective-permute-start.15 = (bf16[576,128]{1,0:T(8,128)(2,1)S(1)}, bf16[576,128]{1,0:T(8,128)(2,1)S(1)}, u32[]{:S(2)}, u32[]{:S(2)}) collective-permute-start(bf16[576,128]{1,0:T(8,128)(2,1)S(1)} %get-tuple-element.58), channel_id=1, source_target_pairs={{0,2},{1,3},{2,0},{3,1},{4,6},{5,7},{6,4},{7,5},{8,10},{9,11},{10,... | collective-permute-start | bytes 442376 | tf_op jit(solution)/shard_map/ppermute | solution.py:469
  51.1 4.0 %collective-permute-start.13 = (bf16[192,128]{1,0:T(8,128)(2,1)S(1)}, bf16[192,128]{1,0:T(8,128)(2,1)S(1)}, u32[]{:S(2)}, u32[]{:S(2)}) collective-permute-start(bf16[192,128]{1,0:T(8,128)(2,1)S(1)} %after_early.1), channel_id=1, source_target_pairs={{0,4},{1,5},{2,6},{3,7},{4,0},{5,1},{6,2},{7,3},{8,12},{9,13},{10,... | collective-permute-start | bytes 147464 | tf_op jit(solution)/shard_map/ppermute | solution.py:469
  52.5 4.9 %collective-permute-start.14 = (bf16[192,128]{1,0:T(8,128)(2,1)S(1)}, bf16[192,128]{1,0:T(8,128)(2,1)S(1)}, u32[]{:S(2)}, u32[]{:S(2)}) collective-permute-start(bf16[192,128]{1,0:T(8,128)(2,1)S(1)} %get-tuple-element.57), channel_id=1, source_target_pairs={{0,6},{1,7},{2,4},{3,5},{4,2},{5,3},{6,0},{7,1},{8,14},{9,15},{10,... | collective-permute-start | bytes 147464 | tf_op jit(solution)/shard_map/ppermute | solution.py:469
  57.4 4.2 %collective-permute-start.18 = (f32[32,128]{1,0:T(8,128)S(1)}, f32[32,128]{1,0:T(8,128)S(1)}, u32[]{:S(2)}, u32[]{:S(2)}) collective-permute-start(f32[32,128]{1,0:T(8,128)S(1)} %sum_gains.1), channel_id=1, source_target_pairs={{0,64},{32,96},{64,0},{96,32},{128,192},{160,224},{192,128},{224,1... | collective-permute-start | bytes 49160 | tf_op jit(solution)/shard_map/ppermute | solution.py:469
  60.5 3.8 %collective-permute-start.17 = (f32[32,128]{1,0:T(8,128)S(1)}, f32[32,128]{1,0:T(8,128)S(1)}, u32[]{:S(2)}, u32[]{:S(2)}) collective-permute-start(f32[32,128]{1,0:T(8,128)S(1)} %sum_gains.1), channel_id=1, source_target_pairs={{0,96},{32,64},{64,32},{96,0},{128,224},{160,192},{192,160},{224,1... | collective-permute-start | bytes 49160 | tf_op jit(solution)/shard_map/ppermute | solution.py:469
  61.2 3.1 %collective-permute-start.16 = (f32[32,128]{1,0:T(8,128)S(1)}, f32[32,128]{1,0:T(8,128)S(1)}, u32[]{:S(2)}, u32[]{:S(2)}) collective-permute-start(f32[32,128]{1,0:T(8,128)S(1)} %sum_gains.1), channel_id=1, source_target_pairs={{0,32},{32,0},{64,96},{96,64},{128,160},{160,128},{192,224},{224,1... | collective-permute-start | bytes 49160 | tf_op jit(solution)/shard_map/ppermute | solution.py:469
  64.3 2.7 %collective-permute-start.19 = (f32[32,128]{1,0:T(8,128)S(1)}, f32[32,128]{1,0:T(8,128)S(1)}, u32[]{:S(2)}, u32[]{:S(2)}) collective-permute-start(f32[32,128]{1,0:T(8,128)S(1)} %add_add_fusion.mine), channel_id=1, source_target_pairs={{0,128},{32,160},{64,192},{96,224},{128,0},{160,32},{192,64},{224,... | collective-permute-start | bytes 49160 | tf_op jit(solution)/shard_map/ppermute | solution.py:469
  67.0 6.7 %collective-permute-start.20 = (f32[32,128]{1,0:T(8,128)S(1)}, f32[32,128]{1,0:T(8,128)S(1)}, u32[]{:S(2)}, u32[]{:S(2)}) collective-permute-start(f32[32,128]{1,0:T(8,128)S(1)} %pair_sum.1.mine), channel_id=1, source_target_pairs={{0,1},{1,0},{2,3},{3,2},{4,5},{5,4},{6,7},{7,6},{8,9},{9,8},{10,11... | collective-permute-start | bytes 49160 | tf_op jit(solution)/shard_map/ppermute | solution.py:469

commit v5 on v4

--- a/solution.py
+++ b/solution.py
@@ -206,7 +206,7 @@
 
 
 def owner_kernel(
-    c_ref, f0, f3, f2, f1, r0, r2, r3, b3, b2, b1, q_gain, k_gain, home_gains,
+    c_ref, f0, f3, f2, f1, r0, r2, r3, b2, b3, b1, q_gain, k_gain, home_gains,
     x0, x1, x2, x3, t1, t2, t3, far_k, far_v, gains_out, gains,
 ):
     c = c_ref[0]
@@ -535,7 +535,7 @@
         scratch_shapes=[pltpu.VMEM((2 * HEADS, HD), F32)],
         compiler_params=params,
         name="owned_heads",
-    )(here, early[0], early[3], early[2], early[1], *late, crossed[2], crossed[1], crossed[0], qg, kg, home_gains)
+    )(here, early[0], early[3], early[2], early[1], *late, crossed[1], crossed[2], crossed[0], qg, kg, home_gains)
     back_early, terms, far_k, far_v, own_gains = outs[:4], outs[4:7], outs[7], outs[8], outs[9]
     moved = {mask: swap(terms[steps.index(mask)], "ctx", mask) for mask in (28, 12, 16)}
     terms_in = [moved[mask] for mask in steps]

time: 74.6 us -> 74 us (level)
  starting transfers between devices: 40.8 us -> 38.2 us
  waiting for transfers between devices: 21.1 us -> 23.2 us
    ppermute x21, starting transfers between devices: 40.8 us -> 38.2 us  [swap(): return lax.ppermute(block, axis, [(i, i ^ mask) for i in range(count)])]
    ppermute x21, waiting for transfers between devices: 21.1 us -> 23.2 us  [swap(): return lax.ppermute(block, axis, [(i, i ^ mask) for i in range(count)])]
  transfers between devices with their start and end apart: 21 -> 21, of which waited for: 9 -> 10; matrix products, arithmetic and copies ran while one was open for 0% -> 0% of each run, Pallas kernels for 10% -> 10%
where the time goes in v5:
time: 74 us; the launch traced here: 73.8 us
  starting transfers between devices  38.2 us (52%)
  waiting for transfers between devices  23.2 us (31%)
  Pallas kernels  11.6 us (16%)
  between operations  0.76 us (1%)
    ppermute x21, starting transfers between devices, swap(): return lax.ppermute(block, axis, [(i, i ^ mask) for i in range(count)])  38.2 us
    ppermute x21, waiting for transfers between devices, swap(): return lax.ppermute(block, axis, [(i, i ^ mask) for i in range(count)])  23.2 us
    pallas_call x1, Pallas kernels, per_device(): pl.pallas_call(home_kernel, in_specs=[smem_spec()] + [hbm_spec()] * 4 + [...  5.18 us
    pallas_call x2, Pallas kernels, pack_call(): pl.pallas_call(functools.partial(pack_kernel, plan), in_specs=[smem_spec(...  2.21 us
    pallas_call x1, Pallas kernels, per_device(): pl.pallas_call(owner_kernel, in_specs=[smem_spec()] + [vmem_spec()] * 13,...  2.13 us
  transfers between devices with their start and end apart: 21, of which 10 were waited for; matrix products, arithmetic and copies ran while one was open for 0% of the time, Pallas kernels for 10%

profile of v5, /device:TPU:1, one launch (start us, length us, event | category | flops | bytes accessed | tf_op | source)
XLA Modules:
  0.0 73.8 jit_solution(9774967211806336385)
XLA Ops:
  0.6 1.0 %pack_early.1 = (bf16[128,128]{1,0:T(8,128)(2,1)S(1)}, bf16[640,128]{1,0:T(8,128)(2,1)S(1)}, bf16[128,128]{1,0:T(8,128)(2,1)S(1)}, bf16[128,128]{1,0:T(8,128)(2,1)S(1)}) custom-call(s32[1]{0:T(128)} %bitcast.c_ref, bf16[128,2048]{1,0:T(8,128)(2,1)} %bitcast.17, bf16[128,2048]{1,0:T(8,128)(2,1)} %bitcast.20, bf16[128,2048]{1,0:T(8,128)(2,1)} %bitcast.23, ...), custom_call_target="tpu_custom_call" | custom-call | tf_op jit(solution)/shard_map/pack_early/pallas_call | solution.py:481
  1.7 2.6 %collective-permute-start.2 = (bf16[640,128]{1,0:T(8,128)(2,1)S(1)}, bf16[640,128]{1,0:T(8,128)(2,1)S(1)}, u32[]{:S(2)}, u32[]{:S(2)}) collective-permute-start(bf16[640,128]{1,0:T(8,128)(2,1)S(1)} %get-tuple-element.41.f1), channel_id=1, source_target_pairs={{0,2},{1,3},{2,0},{3,1},{4,6},{5,7},{6,4},{7,5},{8,10},{9,11},{10,... | collective-permute-start | bytes 491528 | tf_op jit(solution)/shard_map/ppermute | solution.py:469
  4.2 2.8 %collective-permute-start = (bf16[128,128]{1,0:T(8,128)(2,1)S(1)}, bf16[128,128]{1,0:T(8,128)(2,1)S(1)}, u32[]{:S(2)}, u32[]{:S(2)}) collective-permute-start(bf16[128,128]{1,0:T(8,128)(2,1)S(1)} %get-tuple-element.39.f3), channel_id=1, source_target_pairs={{0,6},{1,7},{2,4},{3,5},{4,2},{5,3},{6,0},{7,1},{8,14},{9,15},{10,... | collective-permute-start | bytes 98312 | tf_op jit(solution)/shard_map/ppermute | solution.py:469
  7.2 1.2 %pack_late.1 = (bf16[512,128]{1,0:T(8,128)(2,1)S(1)}, bf16[512,128]{1,0:T(8,128)(2,1)S(1)}, bf16[512,128]{1,0:T(8,128)(2,1)S(1)}) custom-call(s32[1]{0:T(128)} %bitcast.c_ref, bf16[128,2048]{1,0:T(8,128)(2,1)} %bitcast.18, bf16[128,2048]{1,0:T(8,128)(2,1)} %bitcast.21, bf16[128,2048]{1,0:T(8,128)(2,1)} %bitcast.24, bf16[128,2048]{1,0:T(8,128)(2,1)} %bitcast.27, ...), custom_call_target="tpu_custom_call" | custom-call | tf_op jit(solution)/shard_map/pack_late/pallas_call | solution.py:481
  8.4 2.8 %collective-permute-done.f3 = bf16[128,128]{1,0:T(8,128)(2,1)S(1)} collective-permute-done((bf16[128,128]{1,0:T(8,128)(2,1)S(1)}, bf16[128,128]{1,0:T(8,128)(2,1)S(1)}, u32[]{:S(2)}, u32[]{:S(2)}) %collective-permute-start) | collective-permute-done | bytes 32800 | tf_op jit(solution)/shard_map/ppermute | solution.py:469
  11.4 2.8 %collective-permute-start.7 = (bf16[512,128]{1,0:T(8,128)(2,1)S(1)}, bf16[512,128]{1,0:T(8,128)(2,1)S(1)}, u32[]{:S(2)}, u32[]{:S(2)}) collective-permute-start(bf16[512,128]{1,0:T(8,128)(2,1)S(1)} %pack_far_rows.1), channel_id=1, source_target_pairs={{0,16},{1,17},{2,18},{3,19},{4,20},{5,21},{6,22},{7,23},{8,24},{9,... | collective-permute-start | bytes 393224 | tf_op jit(solution)/shard_map/ppermute | solution.py:469
  14.2 4.0 %collective-permute-start.6 = (bf16[512,128]{1,0:T(8,128)(2,1)S(1)}, bf16[512,128]{1,0:T(8,128)(2,1)S(1)}, u32[]{:S(2)}, u32[]{:S(2)}) collective-permute-start(bf16[512,128]{1,0:T(8,128)(2,1)S(1)} %pack_far_rows.1), channel_id=1, source_target_pairs={{0,28},{1,29},{2,30},{3,31},{4,24},{5,25},{6,26},{7,27},{8,20},{9,... | collective-permute-start | bytes 393224 | tf_op jit(solution)/shard_map/ppermute | solution.py:469
  18.3 1.1 %collective-permute-start.3 = (bf16[512,128]{1,0:T(8,128)(2,1)S(1)}, bf16[512,128]{1,0:T(8,128)(2,1)S(1)}, u32[]{:S(2)}, u32[]{:S(2)}) collective-permute-start(bf16[512,128]{1,0:T(8,128)(2,1)S(1)} %get-tuple-element.43.m2), channel_id=1, source_target_pairs={{0,4},{1,5},{2,6},{3,7},{4,0},{5,1},{6,2},{7,3},{8,12},{9,13},{10,... | collective-permute-start | bytes 393224 | tf_op jit(solution)/shard_map/ppermute | solution.py:469
  19.3 1.6 %collective-permute-start.4 = (bf16[512,128]{1,0:T(8,128)(2,1)S(1)}, bf16[512,128]{1,0:T(8,128)(2,1)S(1)}, u32[]{:S(2)}, u32[]{:S(2)}) collective-permute-start(bf16[512,128]{1,0:T(8,128)(2,1)S(1)} %get-tuple-element.44.m3), channel_id=1, source_target_pairs={{0,6},{1,7},{2,4},{3,5},{4,2},{5,3},{6,0},{7,1},{8,14},{9,15},{10,... | collective-permute-start | bytes 393224 | tf_op jit(solution)/shard_map/ppermute | solution.py:469
  21.0 5.2 %home_slab.1 = (bf16[128,2048]{1,0:T(8,128)(2,1)}, bf16[128,2048]{1,0:T(8,128)(2,1)}, bf16[128,2048]{1,0:T(8,128)(2,1)}, f32[12,64,128]{2,1,0:T(8,128)S(1)}, f32...) custom-call(s32[1]{0:T(128)} %bitcast.c_ref, bf16[128,2048]{1,0:T(8,128)(2,1)} %bitcast.19, bf16[128,2048]{1,0:T(8,128)(2,1)} %bitcast.22, ...), custom_call_target="tpu_custom_call" | custom-call | tf_op jit(solution)/shard_map/home_slab/pallas_call | solution.py:496
  26.2 2.8 %collective-permute-done.5.b2 = bf16[512,128]{1,0:T(8,128)(2,1)S(1)} collective-permute-done((bf16[512,128]{1,0:T(8,128)(2,1)S(1)}, bf16[512,128]{1,0:T(8,128)(2,1)S(1)}, u32[]{:S(2)}, u32[]{:S(2)}) %collective-permute-start.5) | collective-permute-done | bytes 131104 | tf_op jit(solution)/shard_map/ppermute | solution.py:469
  29.0 2.1 %owned_heads.1 = (bf16[384,128]{1,0:T(8,128)(2,1)S(1)}, bf16[384,128]{1,0:T(8,128)(2,1)S(1)}, bf16[384,128]{1,0:T(8,128)(2,1)S(1)}, bf16[384,128]{1,0:T(8,128)(2...) custom-call(s32[1]{0:T(128)} %bitcast.c_ref, ...), custom_call_target="tpu_custom_call" | custom-call | tf_op jit(solution)/shard_map/owned_heads/pallas_call | solution.py:527
  31.1 7.0 %collective-permute-start.8 = (bf16[576,128]{1,0:T(8,128)(2,1)S(1)}, bf16[576,128]{1,0:T(8,128)(2,1)S(1)}, u32[]{:S(2)}, u32[]{:S(2)}) collective-permute-start(bf16[576,128]{1,0:T(8,128)(2,1)S(1)} %get-tuple-element.49), channel_id=1, source_target_pairs={{0,28},{1,29},{2,30},{3,31},{4,24},{5,25},{6,26},{7,27},{8,20},{9,... | collective-permute-start | bytes 442376 | tf_op jit(solution)/shard_map/ppermute | solution.py:469
  38.1 0.4 collective-permute-start.10
  38.5 2.2 %collective-permute-start.11 = (bf16[384,128]{1,0:T(8,128)(2,1)S(1)}, bf16[384,128]{1,0:T(8,128)(2,1)S(1)}, u32[]{:S(2)}, u32[]{:S(2)}) collective-permute-start(bf16[384,128]{1,0:T(8,128)(2,1)S(1)} %get-tuple-element.55), channel_id=1, source_target_pairs={{0,4},{1,5},{2,6},{3,7},{4,0},{5,1},{6,2},{7,3},{8,12},{9,13},{10,... | collective-permute-start | bytes 294920 | tf_op jit(solution)/shard_map/ppermute | solution.py:469
  40.7 1.2 %collective-permute-start.12 = (bf16[384,128]{1,0:T(8,128)(2,1)S(1)}, bf16[384,128]{1,0:T(8,128)(2,1)S(1)}, u32[]{:S(2)}, u32[]{:S(2)}) collective-permute-start(bf16[384,128]{1,0:T(8,128)(2,1)S(1)} %get-tuple-element.56), channel_id=1, source_target_pairs={{0,6},{1,7},{2,4},{3,5},{4,2},{5,3},{6,0},{7,1},{8,14},{9,15},{10,... | collective-permute-start | bytes 294920 | tf_op jit(solution)/shard_map/ppermute | solution.py:469
  41.8 4.2 %collective-permute-done.8.u1 = bf16[576,128]{1,0:T(8,128)(2,1)S(1)} collective-permute-done((bf16[576,128]{1,0:T(8,128)(2,1)S(1)}, bf16[576,128]{1,0:T(8,128)(2,1)S(1)}, u32[]{:S(2)}, u32[]{:S(2)}) %collective-permute-start.8) | collective-permute-done | bytes 147488 | tf_op jit(solution)/shard_map/ppermute | solution.py:469
  46.0 4.8 %collective-permute-done.9.u2 = bf16[576,128]{1,0:T(8,128)(2,1)S(1)} collective-permute-done((bf16[576,128]{1,0:T(8,128)(2,1)S(1)}, bf16[576,128]{1,0:T(8,128)(2,1)S(1)}, u32[]{:S(2)}, u32[]{:S(2)}) %collective-permute-start.9) | collective-permute-done | bytes 147488 | tf_op jit(solution)/shard_map/ppermute | solution.py:469
  51.1 2.1 %collective-permute-start.13 = (bf16[192,128]{1,0:T(8,128)(2,1)S(1)}, bf16[192,128]{1,0:T(8,128)(2,1)S(1)}, u32[]{:S(2)}, u32[]{:S(2)}) collective-permute-start(bf16[192,128]{1,0:T(8,128)(2,1)S(1)} %after_early.1), channel_id=1, source_target_pairs={{0,4},{1,5},{2,6},{3,7},{4,0},{5,1},{6,2},{7,3},{8,12},{9,13},{10,... | collective-permute-start | bytes 147464 | tf_op jit(solution)/shard_map/ppermute | solution.py:469
  53.1 1.5 %collective-permute-start.14 = (bf16[192,128]{1,0:T(8,128)(2,1)S(1)}, bf16[192,128]{1,0:T(8,128)(2,1)S(1)}, u32[]{:S(2)}, u32[]{:S(2)}) collective-permute-start(bf16[192,128]{1,0:T(8,128)(2,1)S(1)} %get-tuple-element.57), channel_id=1, source_target_pairs={{0,6},{1,7},{2,4},{3,5},{4,2},{5,3},{6,0},{7,1},{8,14},{9,15},{10,... | collective-permute-start | bytes 147464 | tf_op jit(solution)/shard_map/ppermute | solution.py:469
  54.7 0.4 collective-permute-done.13.z2.y2
  55.1 3.3 %collective-permute-done.14.z3.y3 = bf16[192,128]{1,0:T(8,128)(2,1)S(1)} collective-permute-done((bf16[192,128]{1,0:T(8,128)(2,1)S(1)}, bf16[192,128]{1,0:T(8,128)(2,1)S(1)}, u32[]{:S(2)}, u32[]{:S(2)}) %collective-permute-start.14) | collective-permute-done | bytes 49184 | tf_op jit(solution)/shard_map/ppermute | solution.py:469
  58.4 3.0 %collective-permute-start.18 = (f32[32,128]{1,0:T(8,128)S(1)}, f32[32,128]{1,0:T(8,128)S(1)}, u32[]{:S(2)}, u32[]{:S(2)}) collective-permute-start(f32[32,128]{1,0:T(8,128)S(1)} %sum_gains.1), channel_id=1, source_target_pairs={{0,64},{32,96},{64,0},{96,32},{128,192},{160,224},{192,128},{224,1... | collective-permute-start | bytes 49160 | tf_op jit(solution)/shard_map/ppermute | solution.py:469
  61.4 0.8 %collective-permute-start.17 = (f32[32,128]{1,0:T(8,128)S(1)}, f32[32,128]{1,0:T(8,128)S(1)}, u32[]{:S(2)}, u32[]{:S(2)}) collective-permute-start(f32[32,128]{1,0:T(8,128)S(1)} %sum_gains.1), channel_id=1, source_target_pairs={{0,96},{32,64},{64,32},{96,0},{128,224},{160,192},{192,160},{224,1... | collective-permute-start | bytes 49160 | tf_op jit(solution)/shard_map/ppermute | solution.py:469
  62.2 0.4 collective-permute-done.18
  62.6 2.6 %collective-permute-done.17 = f32[32,128]{1,0:T(8,128)S(1)} collective-permute-done((f32[32,128]{1,0:T(8,128)S(1)}, f32[32,128]{1,0:T(8,128)S(1)}, u32[]{:S(2)}, u32[]{:S(2)}) %collective-permute-start.17) | collective-permute-done | bytes 16416 | tf_op jit(solution)/shard_map/ppermute | solution.py:469
  65.2 0.6 collective-permute-start.19
  65.8 1.2 %finish_rows.1 = (bf16[128,2048]{1,0:T(8,128)(2,1)}, bf16[128,2048]{1,0:T(8,128)(2,1)}, bf16[128,2048]{1,0:T(8,128)(2,1)}, f32[8,128]{1,0:T(8,128)S(1)}) custom-call(s32[1]{0:T(128)} %bitcast.c_ref, bf16[192,128]{1,0:T(8,128)(2,1)S(1)} %get-tuple-element.53.z0.y0, ...), custom_call_target="tpu_custom_call", output_to_operand_aliasing={{0}: (18, {}), {1}: (19, {}), {2}: (20, {})} | custom-call | tf_op jit(solution)/shard_map/finish_rows/pallas_call | solution.py:581
  67.1 1.1 %collective-permute-done.19.other = f32[32,128]{1,0:T(8,128)S(1)} collective-permute-done((f32[32,128]{1,0:T(8,128)S(1)}, f32[32,128]{1,0:T(8,128)S(1)}, u32[]{:S(2)}, u32[]{:S(2)}) %collective-permute-start.19) | collective-permute-done | bytes 16416 | tf_op jit(solution)/shard_map/ppermute | solution.py:469
  68.1 4.2 %collective-permute-start.20 = (f32[32,128]{1,0:T(8,128)S(1)}, f32[32,128]{1,0:T(8,128)S(1)}, u32[]{:S(2)}, u32[]{:S(2)}) collective-permute-start(f32[32,128]{1,0:T(8,128)S(1)} %pair_sum.1.mine), channel_id=1, source_target_pairs={{0,1},{1,0},{2,3},{3,2},{4,5},{5,4},{6,7},{7,6},{8,9},{9,8},{10,11... | collective-permute-start | bytes 49160 | tf_op jit(solution)/shard_map/ppermute | solution.py:469
  72.4 0.8 %collective-permute-done.20.other = f32[32,128]{1,0:T(8,128)S(1)} collective-permute-done((f32[32,128]{1,0:T(8,128)S(1)}, f32[32,128]{1,0:T(8,128)S(1)}, u32[]{:S(2)}, u32[]{:S(2)}) %collective-permute-start.20) | collective-permute-done | bytes 16416 | tf_op jit(solution)/shard_map/ppermute | solution.py:469
  73.2 0.6 last_sum.1
  (26 shorter events, 0.7 us)
Async XLA Ops:
  1.7 5.6 %collective-permute-start.2 = (bf16[640,128]{1,0:T(8,128)(2,1)S(1)}, bf16[640,128]{1,0:T(8,128)(2,1)S(1)}, u32[]{:S(2)}, u32[]{:S(2)}) collective-permute-start(bf16[640,128]{1,0:T(8,128)(2,1)S(1)} %get-tuple-element.41.f1), channel_id=1, source_target_pairs={{0,2},{1,3},{2,0},{3,1},{4,6},{5,7},{6,4},{7,5},{8,10},{9,11},{10,... | collective-permute-start | bytes 491528 | tf_op jit(solution)/shard_map/ppermute | solution.py:469
  4.2 6.9 %collective-permute-start = (bf16[128,128]{1,0:T(8,128)(2,1)S(1)}, bf16[128,128]{1,0:T(8,128)(2,1)S(1)}, u32[]{:S(2)}, u32[]{:S(2)}) collective-permute-start(bf16[128,128]{1,0:T(8,128)(2,1)S(1)} %get-tuple-element.39.f3), channel_id=1, source_target_pairs={{0,6},{1,7},{2,4},{3,5},{4,2},{5,3},{6,0},{7,1},{8,14},{9,15},{10,... | collective-permute-start | bytes 98312 | tf_op jit(solution)/shard_map/ppermute | solution.py:469
  7.1 4.1 %collective-permute-start.1 = (bf16[128,128]{1,0:T(8,128)(2,1)S(1)}, bf16[128,128]{1,0:T(8,128)(2,1)S(1)}, u32[]{:S(2)}, u32[]{:S(2)}) collective-permute-start(bf16[128,128]{1,0:T(8,128)(2,1)S(1)} %get-tuple-element.40.f2), channel_id=1, source_target_pairs={{0,4},{1,5},{2,6},{3,7},{4,0},{5,1},{6,2},{7,3},{8,12},{9,13},{10,... | collective-permute-start | bytes 98312 | tf_op jit(solution)/shard_map/ppermute | solution.py:469
  11.2 9.8 %copy-start = (f32[2048]{0:T(1024)S(1)}, f32[2048]{0:T(1024)}, u32[]{:S(2)}) copy-start(f32[2048]{0:T(1024)} %param.11) | copy-start | bytes 24580
  11.2 9.8 %copy-start.1 = (f32[2048]{0:T(1024)S(1)}, f32[2048]{0:T(1024)}, u32[]{:S(2)}) copy-start(f32[2048]{0:T(1024)} %param.10) | copy-start | bytes 24580
  11.4 14.8 %collective-permute-start.7 = (bf16[512,128]{1,0:T(8,128)(2,1)S(1)}, bf16[512,128]{1,0:T(8,128)(2,1)S(1)}, u32[]{:S(2)}, u32[]{:S(2)}) collective-permute-start(bf16[512,128]{1,0:T(8,128)(2,1)S(1)} %pack_far_rows.1), channel_id=1, source_target_pairs={{0,16},{1,17},{2,18},{3,19},{4,20},{5,21},{6,22},{7,23},{8,24},{9,... | collective-permute-start | bytes 393224 | tf_op jit(solution)/shard_map/ppermute | solution.py:469
  14.2 12.0 %collective-permute-start.6 = (bf16[512,128]{1,0:T(8,128)(2,1)S(1)}, bf16[512,128]{1,0:T(8,128)(2,1)S(1)}, u32[]{:S(2)}, u32[]{:S(2)}) collective-permute-start(bf16[512,128]{1,0:T(8,128)(2,1)S(1)} %pack_far_rows.1), channel_id=1, source_target_pairs={{0,28},{1,29},{2,30},{3,31},{4,24},{5,25},{6,26},{7,27},{8,20},{9,... | collective-permute-start | bytes 393224 | tf_op jit(solution)/shard_map/ppermute | solution.py:469
  18.2 10.7 %collective-permute-start.5 = (bf16[512,128]{1,0:T(8,128)(2,1)S(1)}, bf16[512,128]{1,0:T(8,128)(2,1)S(1)}, u32[]{:S(2)}, u32[]{:S(2)}) collective-permute-start(bf16[512,128]{1,0:T(8,128)(2,1)S(1)} %pack_far_rows.1), channel_id=1, source_target_pairs={{0,12},{1,13},{2,14},{3,15},{4,8},{5,9},{6,10},{7,11},{8,4},{9,5},... | collective-permute-start | bytes 393224 | tf_op jit(solution)/shard_map/ppermute | solution.py:469
  18.3 10.7 %collective-permute-start.3 = (bf16[512,128]{1,0:T(8,128)(2,1)S(1)}, bf16[512,128]{1,0:T(8,128)(2,1)S(1)}, u32[]{:S(2)}, u32[]{:S(2)}) collective-permute-start(bf16[512,128]{1,0:T(8,128)(2,1)S(1)} %get-tuple-element.43.m2), channel_id=1, source_target_pairs={{0,4},{1,5},{2,6},{3,7},{4,0},{5,1},{6,2},{7,3},{8,12},{9,13},{10,... | collective-permute-start | bytes 393224 | tf_op jit(solution)/shard_map/ppermute | solution.py:469
  19.3 9.6 %collective-permute-start.4 = (bf16[512,128]{1,0:T(8,128)(2,1)S(1)}, bf16[512,128]{1,0:T(8,128)(2,1)S(1)}, u32[]{:S(2)}, u32[]{:S(2)}) collective-permute-start(bf16[512,128]{1,0:T(8,128)(2,1)S(1)} %get-tuple-element.44.m3), channel_id=1, source_target_pairs={{0,6},{1,7},{2,4},{3,5},{4,2},{5,3},{6,0},{7,1},{8,14},{9,15},{10,... | collective-permute-start | bytes 393224 | tf_op jit(solution)/shard_map/ppermute | solution.py:469
  31.1 14.9 %collective-permute-start.8 = (bf16[576,128]{1,0:T(8,128)(2,1)S(1)}, bf16[576,128]{1,0:T(8,128)(2,1)S(1)}, u32[]{:S(2)}, u32[]{:S(2)}) collective-permute-start(bf16[576,128]{1,0:T(8,128)(2,1)S(1)} %get-tuple-element.49), channel_id=1, source_target_pairs={{0,28},{1,29},{2,30},{3,31},{4,24},{5,25},{6,26},{7,27},{8,20},{9,... | collective-permute-start | bytes 442376 | tf_op jit(solution)/shard_map/ppermute | solution.py:469
  38.1 12.7 %collective-permute-start.9 = (bf16[576,128]{1,0:T(8,128)(2,1)S(1)}, bf16[576,128]{1,0:T(8,128)(2,1)S(1)}, u32[]{:S(2)}, u32[]{:S(2)}) collective-permute-start(bf16[576,128]{1,0:T(8,128)(2,1)S(1)} %get-tuple-element.50), channel_id=1, source_target_pairs={{0,12},{1,13},{2,14},{3,15},{4,8},{5,9},{6,10},{7,11},{8,4},{9,5},... | collective-permute-start | bytes 442376 | tf_op jit(solution)/shard_map/ppermute | solution.py:469
  38.1 12.7 %collective-permute-start.10 = (bf16[576,128]{1,0:T(8,128)(2,1)S(1)}, bf16[576,128]{1,0:T(8,128)(2,1)S(1)}, u32[]{:S(2)}, u32[]{:S(2)}) collective-permute-start(bf16[576,128]{1,0:T(8,128)(2,1)S(1)} %get-tuple-element.51), channel_id=1, source_target_pairs={{0,16},{1,17},{2,18},{3,19},{4,20},{5,21},{6,22},{7,23},{8,24},{9,... | collective-permute-start | bytes 442376 | tf_op jit(solution)/shard_map/ppermute | solution.py:469
  38.5 12.5 %collective-permute-start.11 = (bf16[384,128]{1,0:T(8,128)(2,1)S(1)}, bf16[384,128]{1,0:T(8,128)(2,1)S(1)}, u32[]{:S(2)}, u32[]{:S(2)}) collective-permute-start(bf16[384,128]{1,0:T(8,128)(2,1)S(1)} %get-tuple-element.55), channel_id=1, source_target_pairs={{0,4},{1,5},{2,6},{3,7},{4,0},{5,1},{6,2},{7,3},{8,12},{9,13},{10,... | collective-permute-start | bytes 294920 | tf_op jit(solution)/shard_map/ppermute | solution.py:469
  40.7 10.4 %collective-permute-start.12 = (bf16[384,128]{1,0:T(8,128)(2,1)S(1)}, bf16[384,128]{1,0:T(8,128)(2,1)S(1)}, u32[]{:S(2)}, u32[]{:S(2)}) collective-permute-start(bf16[384,128]{1,0:T(8,128)(2,1)S(1)} %get-tuple-element.56), channel_id=1, source_target_pairs={{0,6},{1,7},{2,4},{3,5},{4,2},{5,3},{6,0},{7,1},{8,14},{9,15},{10,... | collective-permute-start | bytes 294920 | tf_op jit(solution)/shard_map/ppermute | solution.py:469
  50.9 7.5 %collective-permute-start.15 = (bf16[576,128]{1,0:T(8,128)(2,1)S(1)}, bf16[576,128]{1,0:T(8,128)(2,1)S(1)}, u32[]{:S(2)}, u32[]{:S(2)}) collective-permute-start(bf16[576,128]{1,0:T(8,128)(2,1)S(1)} %get-tuple-element.58), channel_id=1, source_target_pairs={{0,2},{1,3},{2,0},{3,1},{4,6},{5,7},{6,4},{7,5},{8,10},{9,11},{10,... | collective-permute-start | bytes 442376 | tf_op jit(solution)/shard_map/ppermute | solution.py:469
  51.1 4.0 %collective-permute-start.13 = (bf16[192,128]{1,0:T(8,128)(2,1)S(1)}, bf16[192,128]{1,0:T(8,128)(2,1)S(1)}, u32[]{:S(2)}, u32[]{:S(2)}) collective-permute-start(bf16[192,128]{1,0:T(8,128)(2,1)S(1)} %after_early.1), channel_id=1, source_target_pairs={{0,4},{1,5},{2,6},{3,7},{4,0},{5,1},{6,2},{7,3},{8,12},{9,13},{10,... | collective-permute-start | bytes 147464 | tf_op jit(solution)/shard_map/ppermute | solution.py:469
  53.1 5.3 %collective-permute-start.14 = (bf16[192,128]{1,0:T(8,128)(2,1)S(1)}, bf16[192,128]{1,0:T(8,128)(2,1)S(1)}, u32[]{:S(2)}, u32[]{:S(2)}) collective-permute-start(bf16[192,128]{1,0:T(8,128)(2,1)S(1)} %get-tuple-element.57), channel_id=1, source_target_pairs={{0,6},{1,7},{2,4},{3,5},{4,2},{5,3},{6,0},{7,1},{8,14},{9,15},{10,... | collective-permute-start | bytes 147464 | tf_op jit(solution)/shard_map/ppermute | solution.py:469
  58.4 4.2 %collective-permute-start.18 = (f32[32,128]{1,0:T(8,128)S(1)}, f32[32,128]{1,0:T(8,128)S(1)}, u32[]{:S(2)}, u32[]{:S(2)}) collective-permute-start(f32[32,128]{1,0:T(8,128)S(1)} %sum_gains.1), channel_id=1, source_target_pairs={{0,64},{32,96},{64,0},{96,32},{128,192},{160,224},{192,128},{224,1... | collective-permute-start | bytes 49160 | tf_op jit(solution)/shard_map/ppermute | solution.py:469
  61.4 3.8 %collective-permute-start.17 = (f32[32,128]{1,0:T(8,128)S(1)}, f32[32,128]{1,0:T(8,128)S(1)}, u32[]{:S(2)}, u32[]{:S(2)}) collective-permute-start(f32[32,128]{1,0:T(8,128)S(1)} %sum_gains.1), channel_id=1, source_target_pairs={{0,96},{32,64},{64,32},{96,0},{128,224},{160,192},{192,160},{224,1... | collective-permute-start | bytes 49160 | tf_op jit(solution)/shard_map/ppermute | solution.py:469
  62.2 3.0 %collective-permute-start.16 = (f32[32,128]{1,0:T(8,128)S(1)}, f32[32,128]{1,0:T(8,128)S(1)}, u32[]{:S(2)}, u32[]{:S(2)}) collective-permute-start(f32[32,128]{1,0:T(8,128)S(1)} %sum_gains.1), channel_id=1, source_target_pairs={{0,32},{32,0},{64,96},{96,64},{128,160},{160,128},{192,224},{224,1... | collective-permute-start | bytes 49160 | tf_op jit(solution)/shard_map/ppermute | solution.py:469
  65.2 2.9 %collective-permute-start.19 = (f32[32,128]{1,0:T(8,128)S(1)}, f32[32,128]{1,0:T(8,128)S(1)}, u32[]{:S(2)}, u32[]{:S(2)}) collective-permute-start(f32[32,128]{1,0:T(8,128)S(1)} %add_add_fusion.mine), channel_id=1, source_target_pairs={{0,128},{32,160},{64,192},{96,224},{128,0},{160,32},{192,64},{224,... | collective-permute-start | bytes 49160 | tf_op jit(solution)/shard_map/ppermute | solution.py:469
  68.1 5.1 %collective-permute-start.20 = (f32[32,128]{1,0:T(8,128)S(1)}, f32[32,128]{1,0:T(8,128)S(1)}, u32[]{:S(2)}, u32[]{:S(2)}) collective-permute-start(f32[32,128]{1,0:T(8,128)S(1)} %pair_sum.1.mine), channel_id=1, source_target_pairs={{0,1},{1,0},{2,3},{3,2},{4,5},{5,4},{6,7},{7,6},{8,9},{9,8},{10,11... | collective-permute-start | bytes 49160 | tf_op jit(solution)/shard_map/ppermute | solution.py:469
